TPU v7x, 32 devices: a whole 2x2x4 slice. The times are simulated.
32 devices in a mesh: group: 2 (over x), ep: 16 (over z, y, core).
Axes of the slice: x: 2, y: 2, z: 4, core: 2. Of those that a mesh axis runs over, the one named last changes fastest.
Arguments:
- hidden: bfloat16 [2048, 3584], P(('group', 'ep')), parts along dimension 0, may hold values from -6 to 6
- lengths: int32 [64], P(('group', 'ep')), parts along dimension 0, may hold values from 16 to 32
- norm_gain: float32 [3584], replicated, may hold values from 0.25 to 1.75
- w_gate: bfloat16 [16, 3584, 256], P('ep'), may hold values from -0.09375 to 0.09375
- w_up: bfloat16 [16, 3584, 256], P('ep'), may hold values from -0.09375 to 0.09375
- w_down: bfloat16 [16, 256, 3584], P('ep'), may hold values from -0.1875 to 0.1875
- expert_ids: int32 [2048, 2], P(('group', 'ep')), parts along dimension 0, may hold values from 0 to 3, all different within a row; in each aligned block of 64 rows (0 to 63, 64 to 127, ...) at most 48 rows name the same one
- gate_weights: float32 [2048, 2], P(('group', 'ep')), parts along dimension 0, may hold values from 0.3 to 1.5
Outputs:
- moe_out: bfloat16 [2048, 3584], P(('group', 'ep')), parts along dimension 0
There are 2 independent parts, one for each index of `group`. A program takes and returns all parts, laid end to end along the dimension named above; an argument that names none is the same for every part. Nothing has to cross between parts.
Inputs may be any that keep to these rules, and one draw needn't show every extreme that they name: `expert_ids`: within the 64 rows of one rank no expert is chosen more than 48 times; a token's choices differ.
All inputs are finite; a program needn't handle non-finite values.
Results may differ from a plain program's by a relative error of at most 0.0052.
Values may be sent and summed in bfloat16 or wider, within the bound.
No kernel may reach another device: no remote copies, remote signals or barrier semaphores. Data moves between devices by JAX's collectives and lax.ppermute only.
A program may use at most 128 MiB of HBM per device.

v0:
```python
import jax
import jax.numpy as jnp
from jax import lax
from jax.sharding import PartitionSpec as P

SPLIT = 4


def expert_slice(rows, w_gate, w_up, w_down):
    width = rows.shape[-1]
    flat = rows.reshape(-1, width)
    gate_p = jnp.dot(flat, w_gate[0], preferred_element_type=jnp.float32)
    up_p = jnp.dot(flat, w_up[0], preferred_element_type=jnp.float32)
    act = (jax.nn.silu(gate_p) * up_p).astype(jnp.bfloat16)
    part = jnp.dot(act, w_down[0], preferred_element_type=jnp.float32).astype(jnp.bfloat16)
    return part.reshape(rows.shape)


def body(hidden, lengths, norm_gain, w_gate, w_up, w_down, expert_ids, gate_weights):
    tokens_here, width = hidden.shape
    prompts = lengths.shape[0]
    slots_per = tokens_here // prompts
    topk = expert_ids.shape[1]
    experts = lax.axis_size("ep") // SPLIT
    capacity = SPLIT * ((3 * tokens_here * topk + 2 * experts * SPLIT - 1) // (2 * experts * SPLIT))
    position = jnp.arange(tokens_here, dtype=jnp.int32)
    prompt_line = jnp.arange(prompts, dtype=jnp.int32)
    inside = (position // slots_per)[:, None] == prompt_line[None, :]
    below = (position % slots_per)[:, None] < lengths[None, :]
    live_f = jnp.sum((inside & below).astype(jnp.float32), axis=1)
    hidden_f = hidden.astype(jnp.float32)
    meansq = jnp.mean(hidden_f * hidden_f, axis=-1, keepdims=True)
    normed = (hidden_f * lax.rsqrt(meansq + 1e-06) * norm_gain).astype(jnp.bfloat16)
    expert_line = jnp.arange(experts, dtype=jnp.int32)
    onehot = (expert_ids[:, :, None] == expert_line).astype(jnp.float32) * live_f[:, None, None]
    chosen = jnp.sum(onehot, axis=1)
    weight = jnp.sum(onehot * gate_weights[:, :, None], axis=1)
    before = jnp.cumsum(chosen, axis=0) - chosen
    slot_line = jnp.arange(capacity, dtype=jnp.float32)
    placed = ((before[:, :, None] == slot_line) & (chosen[:, :, None] > 0)).astype(jnp.float32)
    picker = placed.reshape(tokens_here, experts * capacity).T.astype(jnp.bfloat16)
    packed = jnp.dot(picker, normed, preferred_element_type=jnp.float32).astype(jnp.bfloat16)
    outgoing = jnp.broadcast_to(
        packed.reshape(experts, 1, capacity, width), (experts, SPLIT, capacity, width)
    )
    outgoing = outgoing.reshape(experts * SPLIT, capacity, width)
    part = expert_slice(
        lax.all_to_all(outgoing, "ep", split_axis=0, concat_axis=0, tiled=True),
        w_gate,
        w_up,
        w_down,
    )
    results = lax.all_to_all(part, "ep", split_axis=0, concat_axis=0, tiled=True)
    summed = results.reshape(experts, SPLIT, capacity, width).astype(jnp.float32)
    summed = jnp.sum(summed, axis=1).reshape(experts * capacity, width)
    mixing = (placed * weight[:, :, None]).reshape(tokens_here, experts * capacity)
    routed = jnp.dot(
        mixing, summed, precision=lax.Precision.HIGHEST, preferred_element_type=jnp.float32
    )
    moe_out = (hidden_f + routed).astype(jnp.bfloat16)
    return moe_out


def solution(mesh):
    return jax.shard_map(
        body,
        mesh=mesh,
        in_specs=(
            P(("group", "ep"), None),
            P(("group", "ep")),
            P(),
            P("ep", None, None),
            P("ep", None, None),
            P("ep", None, None),
            P(("group", "ep"), None),
            P(("group", "ep"), None),
        ),
        out_specs=P(("group", "ep"), None),
        check_vma=False,
    )
```

profile of v0, /device:TPU:0, one launch (start us, length us, event | category | flops | bytes accessed | tf_op | source)
XLA Modules:
  0.0 278.9 jit_solution(15718558302090054610)
XLA Ops:
  0.0 0.0 copy-start
  0.0 0.9 fusion.36
  0.9 0.7 fusion.35
  1.6 0.1 copy.13
  1.7 1.2 fusion.15
  2.9 0.1 eq.63
  3.0 0.1 reduce_window_sum.11
  3.1 0.1 copy.15
  3.2 0.1 convert_convert_fusion
  3.3 1.6 convolution_convert_fusion.1
  4.9 0.5 broadcast_in_dim.5
  5.5 0.0 copy-start.3
  5.5 128.7 %all_to_all.10 = bf16[16,48,3584]{2,1,0:T(8,128)(2,1)S(1)} all-to-all(bf16[16,48,3584]{2,1,0:T(8,128)(2,1)S(1)} %bitcast.40), channel_id=1, replica_groups=mesh['group'=2,'ep'=16] {'ep'}, dimensions={0} | all-to-all | bytes 11010048 | tf_op jit(solution)/shard_map/all_to_all | solution.py:48
  134.2 0.0 copy-start.1
  134.2 2.4 copy-done.1
  136.6 0.0 copy-done.3
  136.6 1.6 fusion.5
  138.2 0.0 copy-done
  138.2 11.4 %convolution_convert_fusion = bf16[768,3584]{1,0:T(8,128)(2,1)} fusion(bf16[1,256,3584]{2,1,0:T(8,128)(2,1)S(1)} %copy-done, bf16[768,3584]{1,0:T(8,128)(2,1)} %bitcast.42, bf16[1,3584,256]{2,1,0:T(8,128)(2,1)} %param.12, f32[768,256]{1,0:T(8,128)S(1)} %fusion.5), kind=kOutput, calls=%fused_computation.1 | convolution fusion | flops 2822504448 | bytes 15466496 | tf_op jit(solution)/shard_map/dot_general | solution.py:15
  149.5 125.8 %all_to_all.11 = bf16[16,48,3584]{2,1,0:T(8,128)(2,1)S(1)} all-to-all(bf16[16,48,3584]{2,1,0:T(8,128)(2,1)} %bitcast.43), channel_id=1, replica_groups=mesh['group'=2,'ep'=16] {'ep'}, dimensions={0} | all-to-all | bytes 11010048 | tf_op jit(solution)/shard_map/all_to_all | solution.py:53
  275.3 0.0 copy-start.2
  275.3 1.0 convert_reduce_fusion
  276.3 0.0 copy-done.2
  276.3 2.6 fusion.1
  (5 shorter events, 0.0 us)
Async XLA Ops:
  0.0 138.2 %copy-start = (bf16[1,256,3584]{2,1,0:T(8,128)(2,1)S(1)}, bf16[1,256,3584]{2,1,0:T(8,128)(2,1)}, u32[]{:S(2)}) copy-start(bf16[1,256,3584]{2,1,0:T(8,128)(2,1)} %param.13) | copy-start | bytes 5505028
  5.5 131.1 %copy-start.3 = (bf16[1,3584,256]{2,1,0:T(8,128)(2,1)S(1)}, bf16[1,3584,256]{2,1,0:T(8,128)(2,1)}, u32[]{:S(2)}) copy-start(bf16[1,3584,256]{2,1,0:T(8,128)(2,1)} %param.11) | copy-start | bytes 5505028
  134.2 2.4 copy-start.1
  275.3 1.0 copy-start.2
where the time goes:
time: 280 us; the launch traced here: 279 us
  blocking collectives  254 us (91%)
  matrix products  17.2 us (6%)
  other arithmetic  3.99 us (1%)
  local copies, waits for them, and re-layouts  3.22 us (1%)
    all_to_all x1, blocking collectives, body(): lax.all_to_all(outgoing, 'ep', split_axis=0, concat_axis=0, tiled=True)  129 us
    all_to_all x1, blocking collectives, body(): lax.all_to_all(part, 'ep', split_axis=0, concat_axis=0, tiled=True)  126 us
    dot_general x1, matrix products, expert_slice(): jnp.dot(act, w_down[0], preferred_element_type=jnp.float32)  11.4 us

commit v1 on v0

v1 whole, which is shorter than its diff:
```python
import jax
import jax.numpy as jnp
from jax import lax
from jax.sharding import PartitionSpec as P

SPLIT = 4


def body(hidden, lengths, norm_gain, w_gate, w_up, w_down, expert_ids, gate_weights):
    tokens_here, width = hidden.shape
    prompts = lengths.shape[0]
    slots_per = tokens_here // prompts
    topk = expert_ids.shape[1]
    ranks = lax.axis_size("ep")
    experts = ranks // SPLIT
    capacity = SPLIT * ((3 * tokens_here * topk + 2 * experts * SPLIT - 1) // (2 * experts * SPLIT))
    plane = lax.axis_index("ep") // SPLIT

    swap_core = [(i, i ^ 1) for i in range(ranks)]
    swap_side = [(i, i ^ 2) for i in range(ranks)]

    def shift(d):
        return [(i, (i + SPLIT * d) % ranks) for i in range(ranks)]

    gates = (w_gate[0], lax.ppermute(w_gate[0], "ep", swap_core))
    ups = (w_up[0], lax.ppermute(w_up[0], "ep", swap_core))
    downs = (w_down[0], lax.ppermute(w_down[0], "ep", swap_core))

    position = jnp.arange(tokens_here, dtype=jnp.int32)
    prompt_line = jnp.arange(prompts, dtype=jnp.int32)
    inside = (position // slots_per)[:, None] == prompt_line[None, :]
    below = (position % slots_per)[:, None] < lengths[None, :]
    live = jnp.any(inside & below, axis=1)
    hidden_f = hidden.astype(jnp.float32)
    meansq = jnp.mean(hidden_f * hidden_f, axis=-1, keepdims=True)
    normed = (hidden_f * lax.rsqrt(meansq + 1e-06) * norm_gain).astype(jnp.bfloat16)

    away = (expert_ids - plane + experts) % experts
    distance_line = jnp.arange(experts, dtype=jnp.int32)
    onehot = ((away[:, :, None] == distance_line) & live[:, None, None]).astype(jnp.float32)
    chosen = jnp.sum(onehot, axis=1)
    weight = jnp.sum(onehot * gate_weights[:, :, None], axis=1)
    before = jnp.cumsum(chosen, axis=0) - chosen
    slot_line = jnp.arange(capacity, dtype=jnp.float32)
    placed = ((before[:, :, None] == slot_line) & (chosen[:, :, None] > 0)).astype(jnp.bfloat16)
    picker = placed.reshape(tokens_here, experts * capacity).T
    packed = jnp.dot(picker, normed, preferred_element_type=jnp.float32).astype(jnp.bfloat16)
    packed = packed.reshape(experts, capacity, width)

    def expert(rows):
        total = None
        for gate, up, down in zip(gates, ups, downs):
            gate_p = jnp.dot(rows, gate, preferred_element_type=jnp.float32)
            up_p = jnp.dot(rows, up, preferred_element_type=jnp.float32)
            act = (jax.nn.silu(gate_p) * up_p).astype(jnp.bfloat16)
            part = jnp.dot(act, down, preferred_element_type=jnp.float32)
            total = part if total is None else total + part
        return total

    if experts == 4:
        groups = [[0], [2], [1, 3]]
    else:
        groups = [[d] for d in range(experts)]

    arrived = {0: packed[0]}
    for d in [d for g in groups for d in g if d]:
        arrived[d] = lax.ppermute(packed[d], "ep", shift(d))

    routed = jnp.zeros((tokens_here, width), jnp.float32)
    for g in groups:
        mine = jnp.concatenate([arrived[d] for d in g]) if len(g) > 1 else arrived[g[0]]
        theirs = lax.ppermute(mine, "ep", swap_side)
        part = expert(jnp.concatenate([mine, theirs]))
        half = mine.shape[0]
        other = lax.ppermute(part[half:].astype(jnp.bfloat16), "ep", swap_side)
        summed = (part[:half] + other.astype(jnp.float32)).astype(jnp.bfloat16)
        for k, d in enumerate(g):
            rows = summed[k * capacity : (k + 1) * capacity]
            if d:
                rows = lax.ppermute(rows, "ep", shift(experts - d))
            taken = jnp.dot(placed[:, d], rows, preferred_element_type=jnp.float32)
            routed = routed + weight[:, d : d + 1] * taken
    return (hidden_f + routed).astype(jnp.bfloat16)


def solution(mesh):
    return jax.shard_map(
        body,
        mesh=mesh,
        in_specs=(
            P(("group", "ep"), None),
            P(("group", "ep")),
            P(),
            P("ep", None, None),
            P("ep", None, None),
            P("ep", None, None),
            P(("group", "ep"), None),
            P(("group", "ep"), None),
        ),
        out_specs=P(("group", "ep"), None),
        check_vma=False,
    )
```

time: 280 us -> 151 us (0.54)
  blocking collectives: 254 us -> 0 us
  waiting for transfers between devices: 0 us -> 53.4 us
  matrix products: 17.2 us -> 47.5 us
  starting transfers between devices: 0 us -> 27.8 us
  local copies, waits for them, and re-layouts: 3.22 us -> 11.4 us
  other arithmetic: 3.99 us -> 7.97 us
    all_to_all x2 -> x0, blocking collectives: 254 us -> none  [the longest x1 129 us: body(): lax.all_to_all(outgoing, 'ep', split_axis=0, concat_axis=0, tiled=True)]
    ppermute x0 -> x15, waiting for transfers between devices: none -> 53.4 us  [the longest x3 18.1 us: body(): rows = lax.ppermute(rows, 'ep', shift(experts - d))]
    dot_general x3 -> x16, matrix products: 15.5 us -> 45.9 us  [the longest x6 28.2 us: expert(): part = jnp.dot(act, down, preferred_element_type=jnp.float32)]
    ppermute x0 -> x15, starting transfers between devices: none -> 27.8 us  [the longest x3 16.1 us: body(): arrived[d] = lax.ppermute(packed[d], 'ep', shift(d))]
    slice x0 -> x5, local copies, waits for them, and re-layouts: none -> 5.58 us  [the longest x3 5.44 us: body(): other = lax.ppermute(part[half:].astype(jnp.bfloat16), 'ep', swap_side)]
    concatenate x0 -> x2, local copies, waits for them, and re-layouts: none -> 2.91 us  [body(): part = expert(jnp.concatenate([mine, theirs]))]
  transfers between devices with their start and end apart: 0 -> 15, of which waited for: 0 -> 6; matrix products, arithmetic and copies ran while one was open for 0% -> 35% of each run, Pallas kernels for 0% -> 0%
where the time goes in v1:
time: 151 us; the launch traced here: 148 us
  waiting for transfers between devices  53.4 us (35%)
  matrix products  47.5 us (31%)
  starting transfers between devices  27.8 us (18%)
  local copies, waits for them, and re-layouts  11.4 us (8%)
  other arithmetic  7.97 us (5%)
    dot_general x6, matrix products, expert(): part = jnp.dot(act, down, preferred_element_type=jnp.float32)  28.2 us
    ppermute x3, waiting for transfers between devices, body(): rows = lax.ppermute(rows, 'ep', shift(experts - d))  18.1 us
    ppermute x3, starting transfers between devices, body(): arrived[d] = lax.ppermute(packed[d], 'ep', shift(d))  16.1 us
    ppermute x3, waiting for transfers between devices, body(): arrived[d] = lax.ppermute(packed[d], 'ep', shift(d))  15 us
    ppermute x3, waiting for transfers between devices, body(): theirs = lax.ppermute(mine, 'ep', swap_side)  13.9 us
    dot_general x5, matrix products, expert(): gate_p = jnp.dot(rows, gate, preferred_element_type=jnp.float32)  12.9 us
    ppermute x3, waiting for transfers between devices, body(): other = lax.ppermute(part[half:].astype(jnp.bfloat16), 'ep', swap_side)  6.38 us
    slice x3, local copies, waits for them, and re-layouts, body(): other = lax.ppermute(part[half:].astype(jnp.bfloat16), 'ep', swap_side)  5.44 us
  transfers between devices with their start and end apart: 15, of which 6 were waited for; matrix products, arithmetic and copies ran while one was open for 35% of the time, Pallas kernels for 0%

profile of v1, /device:TPU:0, one launch (start us, length us, event | category | flops | bytes accessed | tf_op | source)
XLA Modules:
  0.0 148.3 jit_solution(3803332060544287294)
XLA Ops:
  0.0 0.7 and_select_fusion.2
  0.7 0.7 and_reduce_fusion
  1.4 0.7 select_reduce_fusion
  2.5 1.2 fusion.6
  3.9 1.6 %convolution_convert_fusion = bf16[192,3584]{1,0:T(8,128)(2,1)S(1)} fusion(pred[64,192]{0,1:T(32,128)(4,1)S(1)} %fusion.19, bf16[64,3584]{1,0:T(8,128)(2,1)} %param.8, f32[3584]{0:T(1024)} %param.10, f32[64]{0:T(128)S(1)} %add_rsqrt_fusion), kind=kOutput, calls=%fused_computation.1 | convolution fusion | flops 89686016 | bytes 1861888 | tf_op jit(solution)/shard_map/dot_general | solution.py:47
  5.6 3.1 %collective-permute-start.9 = (bf16[48,3584]{1,0:T(8,128)(2,1)S(1)}, bf16[48,3584]{1,0:T(8,128)(2,1)S(1)}, u32[]{:S(2)}, u32[]{:S(2)}) collective-permute-start(bf16[48,3584]{1,0:T(8,128)(2,1)S(1)} %get-tuple-element.9), channel_id=1, source_target_pairs={{0,4},{1,5},{2,6},{3,7},{4,8},{5,9},{6,10},{7,11},{8,12},{9,13},{1... | collective-permute-start | bytes 1032200 | tf_op jit(solution)/shard_map/ppermute | solution.py:67
  8.6 2.1 %collective-permute-start.10 = (bf16[48,3584]{1,0:T(8,128)(2,1)S(1)}, bf16[48,3584]{1,0:T(8,128)(2,1)S(1)}, u32[]{:S(2)}, u32[]{:S(2)}) collective-permute-start(bf16[48,3584]{1,0:T(8,128)(2,1)S(1)} %get-tuple-element.8), channel_id=1, source_target_pairs={{0,12},{1,13},{2,14},{3,15},{4,0},{5,1},{6,2},{7,3},{8,4},{9,5},{1... | collective-permute-start | bytes 1032200 | tf_op jit(solution)/shard_map/ppermute | solution.py:67
  10.7 0.5 collective-permute-start.1
  11.3 0.6 slice_bitcast_fusion.9
  11.8 0.6 fusion.18
  12.5 7.1 %collective-permute-done.9 = bf16[48,3584]{1,0:T(8,128)(2,1)S(1)} collective-permute-done((bf16[48,3584]{1,0:T(8,128)(2,1)S(1)}, bf16[48,3584]{1,0:T(8,128)(2,1)S(1)}, u32[]{:S(2)}, u32[]{:S(2)}) %collective-permute-start.9) | collective-permute-done | bytes 344096 | tf_op jit(solution)/shard_map/ppermute | solution.py:67
  19.6 10.9 %collective-permute-start.5 = (bf16[48,3584]{1,0:T(8,128)(2,1)S(1)}, bf16[48,3584]{1,0:T(8,128)(2,1)}, u32[]{:S(2)}, u32[]{:S(2)}) collective-permute-start(bf16[48,3584]{1,0:T(8,128)(2,1)S(1)} %get-tuple-element.10), channel_id=1, source_target_pairs={{0,8},{1,9},{2,10},{3,11},{4,12},{5,13},{6,14},{7,15},{8,0},{9,1},... | collective-permute-start | bytes 1032200 | tf_op jit(solution)/shard_map/ppermute | solution.py:67
  30.6 1.6 %collective-permute-start = (bf16[48,3584]{1,0:T(8,128)(2,1)S(1)}, bf16[48,3584]{1,0:T(8,128)(2,1)S(1)}, u32[]{:S(2)}, u32[]{:S(2)}) collective-permute-start(bf16[48,3584]{1,0:T(8,128)(2,1)S(1)} %get-tuple-element.7), channel_id=1, source_target_pairs={{0,2},{1,3},{2,0},{3,1},{4,6},{5,7},{6,4},{7,5},{8,10},{9,11},{10,... | collective-permute-start | bytes 1032200 | tf_op jit(solution)/shard_map/ppermute | solution.py:72
  32.1 0.9 pad_maximum_fusion.1
  33.1 7.9 %collective-permute-done.5 = bf16[48,3584]{1,0:T(8,128)(2,1)} collective-permute-done((bf16[48,3584]{1,0:T(8,128)(2,1)S(1)}, bf16[48,3584]{1,0:T(8,128)(2,1)}, u32[]{:S(2)}, u32[]{:S(2)}) %collective-permute-start.5) | collective-permute-done | bytes 344096 | tf_op jit(solution)/shard_map/ppermute | solution.py:67
  41.0 1.5 %collective-permute-start.11 = (bf16[96,3584]{1,0:T(8,128)(2,1)}, bf16[96,3584]{1,0:T(8,128)(2,1)}, u32[]{:S(2)}, u32[]{:S(2)}) collective-permute-start(bf16[96,3584]{1,0:T(8,128)(2,1)} %pad_maximum_fusion.1), channel_id=1, source_target_pairs={{0,2},{1,3},{2,0},{3,1},{4,6},{5,7},{6,4},{7,5},{8,10},{9,11},{10,... | collective-permute-start | bytes 2064392 | tf_op jit(solution)/shard_map/ppermute | solution.py:72
  42.5 1.7 %constant_dynamic-update-slice_fusion.1 = bf16[96,3584]{1,0:T(8,128)(2,1)} fusion(bf16[48,3584]{1,0:T(8,128)(2,1)} %collective-permute-done.5), kind=kLoop, calls=%fused_computation.55 | loop fusion | bytes 688128
  44.2 0.5 collective-permute-start.6
  44.9 2.6 %fusion.53 = f32[96,256]{1,0:T(8,128)} fusion(bf16[1,3584,256]{2,1,0:T(8,128)(2,1)} %param.11, bf16[48,3584]{1,0:T(8,128)(2,1)S(1)} %collective-permute-done, bf16[48,3584]{1,0:T(8,128)(2,1)S(1)} %get-tuple-element.7), kind=kOutput, calls=%fused_computation.92 | convolution fusion | flops 177537024 | bytes 2621440 | tf_op jit(solution)/shard_map/dot_general | solution.py:53
  47.5 4.4 %fusion.20 = f32[96,3584]{1,0:T(8,128)} fusion(f32[96,256]{1,0:T(8,128)} %fusion.53, bf16[1,256,3584]{2,1,0:T(8,128)(2,1)} %param.13, bf16[1,3584,256]{2,1,0:T(8,128)(2,1)} %param.12, bf16[48,3584]{1,0:T(8,128)(2,1)} %copy-done.4, bf16[48,3584]{1,0:T(8,128)(2,1)S(1)} %get-tuple-element.7), kind=kOutput, calls=%fused_computation.44 | convolution fusion | flops 353845248 | bytes 5832704 | tf_op jit(solution)/shard_map/dot_general | solution.py:56
  52.0 13.9 %collective-permute-done.6 = bf16[48,3584]{1,0:T(8,128)(2,1)} collective-permute-done((bf16[48,3584]{1,0:T(8,128)(2,1)}, bf16[48,3584]{1,0:T(8,128)(2,1)}, u32[]{:S(2)}, u32[]{:S(2)}) %collective-permute-start.6) | collective-permute-done | bytes 344096 | tf_op jit(solution)/shard_map/ppermute | solution.py:72
  65.9 1.8 %constant_dynamic-update-slice_fusion = bf16[96,3584]{1,0:T(8,128)(2,1)} fusion(bf16[96,3584]{1,0:T(8,128)(2,1)} %constant_dynamic-update-slice_fusion.1, bf16[48,3584]{1,0:T(8,128)(2,1)} %collective-permute-done.6), kind=kLoop, calls=%fused_computation.54 | loop fusion | bytes 688128 | tf_op jit(solution)/shard_map/concatenate | solution.py:73
  67.7 2.8 %fusion.51 = f32[96,256]{1,0:T(8,128)} fusion(bf16[96,3584]{1,0:T(8,128)(2,1)} %constant_dynamic-update-slice_fusion, bf16[1,3584,256]{2,1,0:T(8,128)(2,1)} %param.11), kind=kOutput, calls=%fused_computation.90 | convolution fusion | flops 176160768 | bytes 2621440 | tf_op jit(solution)/shard_map/dot_general | solution.py:53
  70.5 4.6 %fusion.21 = f32[96,3584]{1,0:T(8,128)} fusion(f32[96,256]{1,0:T(8,128)} %fusion.51, bf16[1,256,3584]{2,1,0:T(8,128)(2,1)} %param.13, bf16[96,3584]{1,0:T(8,128)(2,1)} %constant_dynamic-update-slice_fusion, bf16[1,3584,256]{2,1,0:T(8,128)(2,1)} %param.12), kind=kOutput, calls=%fused_computation.45 | convolution fusion | flops 352468992 | bytes 5832704 | tf_op jit(solution)/shard_map/dot_general | solution.py:56
  75.1 1.1 constant_dynamic-update-slice_fusion.2
  76.2 2.7 %fusion.49 = f32[192,256]{1,0:T(8,128)} fusion(bf16[192,3584]{1,0:T(8,128)(2,1)S(1)} %constant_dynamic-update-slice_fusion.2, bf16[1,3584,256]{2,1,0:T(8,128)(2,1)} %param.11), kind=kOutput, calls=%fused_computation.88 | convolution fusion | flops 352321536 | bytes 3407872 | tf_op jit(solution)/shard_map/dot_general | solution.py:53
  78.9 5.3 %fusion.15 = f32[192,3584]{1,0:T(8,128)} fusion(f32[192,256]{1,0:T(8,128)} %fusion.49, bf16[1,256,3584]{2,1,0:T(8,128)(2,1)} %param.13, bf16[192,3584]{1,0:T(8,128)(2,1)S(1)} %constant_dynamic-update-slice_fusion.2, bf16[1,3584,256]{2,1,0:T(8,128)(2,1)} %param.12), kind=kOutput, calls=%fused_computation.33 | convolution fusion | flops 704937984 | bytes 7995392 | tf_op jit(solution)/shard_map/dot_general | solution.py:56
  84.3 2.7 %fusion.70 = f32[192,256]{1,0:T(8,128)} fusion(bf16[192,3584]{1,0:T(8,128)(2,1)S(1)} %constant_dynamic-update-slice_fusion.2, bf16[3584,256]{1,0:T(8,128)(2,1)} %collective-permute-done.1), kind=kOutput, calls=%fused_computation.107 | convolution fusion | flops 352321536 | bytes 3407872 | tf_op jit(solution)/shard_map/dot_general | solution.py:53
  87.0 5.6 %convolution_add_fusion = f32[192,3584]{1,0:T(8,128)} fusion(f32[192,3584]{1,0:T(8,128)} %fusion.15, bf16[256,3584]{1,0:T(8,128)(2,1)S(1)} %collective-permute-done.3, f32[192,256]{1,0:T(8,128)} %fusion.70, bf16[192,3584]{1,0:T(8,128)(2,1)S(1)} %constant_dynamic-update-slice_fusion.2, bf16[3584,256]{1,0:T(8,128)(2,1)} %collective-permute-done.2), kind=kOutput, calls=%fused_computation | convolution fusion | flops 705626112 | bytes 10747904 | tf_op jit(solution)/shard_map/dot_general | solution.py:56
  92.6 2.3 %slice.128 = bf16[96,3584]{1,0:T(8,128)(2,1)} slice(f32[192,3584]{1,0:T(8,128)} %convolution_add_fusion), slice={[96:192], [0:3584]} | slice | bytes 1376256 | tf_op jit(solution)/shard_map/slice | solution.py:75
  95.0 1.5 %collective-permute-start.12 = (bf16[96,3584]{1,0:T(8,128)(2,1)}, bf16[96,3584]{1,0:T(8,128)(2,1)}, u32[]{:S(2)}, u32[]{:S(2)}) collective-permute-start(bf16[96,3584]{1,0:T(8,128)(2,1)} %slice.128), channel_id=1, source_target_pairs={{0,2},{1,3},{2,0},{3,1},{4,6},{5,7},{6,4},{7,5},{8,10},{9,11},{10,... | collective-permute-start | bytes 2064392 | tf_op jit(solution)/shard_map/ppermute | solution.py:75
  96.5 2.1 %fusion.69 = f32[96,256]{1,0:T(8,128)S(1)} fusion(bf16[96,3584]{1,0:T(8,128)(2,1)} %constant_dynamic-update-slice_fusion, bf16[3584,256]{1,0:T(8,128)(2,1)} %collective-permute-done.1), kind=kOutput, calls=%fused_computation.106 | convolution fusion | flops 176160768 | bytes 2621440 | tf_op jit(solution)/shard_map/dot_general | solution.py:53
  98.7 4.2 %convolution_add_fusion.1 = f32[96,3584]{1,0:T(8,128)} fusion(f32[96,3584]{1,0:T(8,128)} %fusion.21, bf16[256,3584]{1,0:T(8,128)(2,1)S(1)} %collective-permute-done.3, f32[96,256]{1,0:T(8,128)S(1)} %fusion.69, bf16[96,3584]{1,0:T(8,128)(2,1)S(1)} %copy-done, bf16[3584,256]{1,0:T(8,128)(2,1)} %collective-permute-done.2), kind=kOutput, calls=%fused_computation.2 | convolution fusion | flops 352813056 | bytes 7208960 | tf_op jit(solution)/shard_map/dot_general | solution.py:56
  102.9 2.0 %slice.129 = bf16[48,3584]{1,0:T(8,128)(2,1)} slice(f32[96,3584]{1,0:T(8,128)} %convolution_add_fusion.1), slice={[48:96], [0:3584]} | slice | bytes 688128 | tf_op jit(solution)/shard_map/slice | solution.py:75
  104.9 0.5 collective-permute-start.7
  105.4 2.7 %fusion.61 = f32[96,256]{1,0:T(8,128)} fusion(bf16[3584,256]{1,0:T(8,128)(2,1)} %collective-permute-done.2, bf16[48,3584]{1,0:T(8,128)(2,1)} %copy-done.4, bf16[48,3584]{1,0:T(8,128)(2,1)S(1)} %get-tuple-element.7), kind=kOutput, calls=%fused_computation.100 | convolution fusion | flops 177537024 | bytes 2621440 | tf_op jit(solution)/shard_map/dot_general | solution.py:54
  108.1 3.9 %convolution_add_fusion.2 = f32[96,3584]{1,0:T(8,128)} fusion(f32[96,3584]{1,0:T(8,128)S(1)} %copy-done.1, bf16[256,3584]{1,0:T(8,128)(2,1)S(1)} %collective-permute-done.3, f32[96,256]{1,0:T(8,128)} %fusion.61, bf16[3584,256]{1,0:T(8,128)(2,1)} %collective-permute-done.1, bf16[48,3584]{1,0:T(8,128)(2,1)} %copy-done.4, bf16[48,3584]{1,0:T(8,128)(2,1)S(1)} %get-tuple-element.7), kind=kOutput, calls=%fused_computation.3 | convolution fusion | flops 354189312 | bytes 7208960 | tf_op jit(solution)/shard_map/dot_general | solution.py:56
  111.9 1.1 slice.130
  113.1 1.6 %collective-permute-start.4 = (bf16[48,3584]{1,0:T(8,128)(2,1)S(1)}, bf16[48,3584]{1,0:T(8,128)(2,1)S(1)}, u32[]{:S(2)}, u32[]{:S(2)}) collective-permute-start(bf16[48,3584]{1,0:T(8,128)(2,1)S(1)} %slice.130), channel_id=1, source_target_pairs={{0,2},{1,3},{2,0},{3,1},{4,6},{5,7},{6,4},{7,5},{8,10},{9,11},{10,... | collective-permute-start | bytes 1032200 | tf_op jit(solution)/shard_map/ppermute | solution.py:75
  114.7 6.4 %collective-permute-done.7 = bf16[48,3584]{1,0:T(8,128)(2,1)} collective-permute-done((bf16[48,3584]{1,0:T(8,128)(2,1)}, bf16[48,3584]{1,0:T(8,128)(2,1)}, u32[]{:S(2)}, u32[]{:S(2)}) %collective-permute-start.7) | collective-permute-done | bytes 344096 | tf_op jit(solution)/shard_map/ppermute | solution.py:75
  121.0 1.2 fusion.9
  122.4 1.6 %fusion.5 = bf16[96,3584]{1,0:T(8,128)(2,1)S(1)} fusion(f32[192,3584]{1,0:T(8,128)} %convolution_add_fusion, bf16[96,3584]{1,0:T(8,128)(2,1)} %collective-permute-done.12), kind=kLoop, calls=%fused_computation.15 | loop fusion | flops 1032192 | bytes 2752512 | tf_op jit(solution)/shard_map/convert_element_type | solution.py:76
  124.1 2.4 %collective-permute-start.14 = (bf16[48,3584]{1,0:T(8,128)(2,1)S(1)}, bf16[48,3584]{1,0:T(8,128)(2,1)S(1)}, u32[]{:S(2)}, u32[]{:S(2)}) collective-permute-start(bf16[48,3584]{1,0:T(8,128)(2,1)S(1)} %get-tuple-element.12), channel_id=1, source_target_pairs={{0,4},{1,5},{2,6},{3,7},{4,8},{5,9},{6,10},{7,11},{8,12},{9,13},{1... | collective-permute-start | bytes 1032200 | tf_op jit(solution)/shard_map/ppermute | solution.py:80
  126.5 1.5 %collective-permute-start.13 = (bf16[48,3584]{1,0:T(8,128)(2,1)S(1)}, bf16[48,3584]{1,0:T(8,128)(2,1)S(1)}, u32[]{:S(2)}, u32[]{:S(2)}) collective-permute-start(bf16[48,3584]{1,0:T(8,128)(2,1)S(1)} %get-tuple-element.11), channel_id=1, source_target_pairs={{0,12},{1,13},{2,14},{3,15},{4,0},{5,1},{6,2},{7,3},{8,4},{9,5},{1... | collective-permute-start | bytes 1032200 | tf_op jit(solution)/shard_map/ppermute | solution.py:80
  128.0 15.8 %collective-permute-done.8 = bf16[48,3584]{1,0:T(8,128)(2,1)S(1)} collective-permute-done((bf16[48,3584]{1,0:T(8,128)(2,1)S(1)}, bf16[48,3584]{1,0:T(8,128)(2,1)S(1)}, u32[]{:S(2)}, u32[]{:S(2)}) %collective-permute-start.8) | collective-permute-done | bytes 344096 | tf_op jit(solution)/shard_map/ppermute | solution.py:80
  144.2 0.3 fusion.2
  144.9 2.2 %collective-permute-done.13 = bf16[48,3584]{1,0:T(8,128)(2,1)S(1)} collective-permute-done((bf16[48,3584]{1,0:T(8,128)(2,1)S(1)}, bf16[48,3584]{1,0:T(8,128)(2,1)S(1)}, u32[]{:S(2)}, u32[]{:S(2)}) %collective-permute-start.13) | collective-permute-done | bytes 344096 | tf_op jit(solution)/shard_map/ppermute | solution.py:80
  147.1 1.1 fusion.4
  (48 shorter events, 1.7 us)
Async XLA Ops:
  5.6 14.0 %collective-permute-start.9 = (bf16[48,3584]{1,0:T(8,128)(2,1)S(1)}, bf16[48,3584]{1,0:T(8,128)(2,1)S(1)}, u32[]{:S(2)}, u32[]{:S(2)}) collective-permute-start(bf16[48,3584]{1,0:T(8,128)(2,1)S(1)} %get-tuple-element.9), channel_id=1, source_target_pairs={{0,4},{1,5},{2,6},{3,7},{4,8},{5,9},{6,10},{7,11},{8,12},{9,13},{1... | collective-permute-start | bytes 1032200 | tf_op jit(solution)/shard_map/ppermute | solution.py:67
  8.6 21.9 %collective-permute-start.10 = (bf16[48,3584]{1,0:T(8,128)(2,1)S(1)}, bf16[48,3584]{1,0:T(8,128)(2,1)S(1)}, u32[]{:S(2)}, u32[]{:S(2)}) collective-permute-start(bf16[48,3584]{1,0:T(8,128)(2,1)S(1)} %get-tuple-element.8), channel_id=1, source_target_pairs={{0,12},{1,13},{2,14},{3,15},{4,0},{5,1},{6,2},{7,3},{8,4},{9,5},{1... | collective-permute-start | bytes 1032200 | tf_op jit(solution)/shard_map/ppermute | solution.py:67
  10.7 76.3 %collective-permute-start.3 = (bf16[256,3584]{1,0:T(8,128)(2,1)}, bf16[256,3584]{1,0:T(8,128)(2,1)S(1)}, u32[]{:S(2)}, u32[]{:S(2)}) collective-permute-start(bf16[256,3584]{1,0:T(8,128)(2,1)} %bitcast.6), channel_id=1, source_target_pairs={{0,1},{1,0},{2,3},{3,2},{4,5},{5,4},{6,7},{7,6},{8,9},{9,8},{10,11... | collective-permute-start | bytes 5505032 | tf_op jit(solution)/shard_map/ppermute | solution.py:27
  10.7 73.6 %collective-permute-start.1 = (bf16[3584,256]{1,0:T(8,128)(2,1)}, bf16[3584,256]{1,0:T(8,128)(2,1)}, u32[]{:S(2)}, u32[]{:S(2)}) collective-permute-start(bf16[3584,256]{1,0:T(8,128)(2,1)} %bitcast.4), channel_id=1, source_target_pairs={{0,1},{1,0},{2,3},{3,2},{4,5},{5,4},{6,7},{7,6},{8,9},{9,8},{10,11... | collective-permute-start | bytes 5505032 | tf_op jit(solution)/shard_map/ppermute | solution.py:25
  11.2 75.8 %collective-permute-start.2 = (bf16[3584,256]{1,0:T(8,128)(2,1)}, bf16[3584,256]{1,0:T(8,128)(2,1)}, u32[]{:S(2)}, u32[]{:S(2)}) collective-permute-start(bf16[3584,256]{1,0:T(8,128)(2,1)} %bitcast.5), channel_id=1, source_target_pairs={{0,1},{1,0},{2,3},{3,2},{4,5},{5,4},{6,7},{7,6},{8,9},{9,8},{10,11... | collective-permute-start | bytes 5505032 | tf_op jit(solution)/shard_map/ppermute | solution.py:26
  19.6 21.4 %collective-permute-start.5 = (bf16[48,3584]{1,0:T(8,128)(2,1)S(1)}, bf16[48,3584]{1,0:T(8,128)(2,1)}, u32[]{:S(2)}, u32[]{:S(2)}) collective-permute-start(bf16[48,3584]{1,0:T(8,128)(2,1)S(1)} %get-tuple-element.10), channel_id=1, source_target_pairs={{0,8},{1,9},{2,10},{3,11},{4,12},{5,13},{6,14},{7,15},{8,0},{9,1},... | collective-permute-start | bytes 1032200 | tf_op jit(solution)/shard_map/ppermute | solution.py:67
  30.6 13.7 %collective-permute-start = (bf16[48,3584]{1,0:T(8,128)(2,1)S(1)}, bf16[48,3584]{1,0:T(8,128)(2,1)S(1)}, u32[]{:S(2)}, u32[]{:S(2)}) collective-permute-start(bf16[48,3584]{1,0:T(8,128)(2,1)S(1)} %get-tuple-element.7), channel_id=1, source_target_pairs={{0,2},{1,3},{2,0},{3,1},{4,6},{5,7},{6,4},{7,5},{8,10},{9,11},{10,... | collective-permute-start | bytes 1032200 | tf_op jit(solution)/shard_map/ppermute | solution.py:72
  41.0 34.1 %collective-permute-start.11 = (bf16[96,3584]{1,0:T(8,128)(2,1)}, bf16[96,3584]{1,0:T(8,128)(2,1)}, u32[]{:S(2)}, u32[]{:S(2)}) collective-permute-start(bf16[96,3584]{1,0:T(8,128)(2,1)} %pad_maximum_fusion.1), channel_id=1, source_target_pairs={{0,2},{1,3},{2,0},{3,1},{4,6},{5,7},{6,4},{7,5},{8,10},{9,11},{10,... | collective-permute-start | bytes 2064392 | tf_op jit(solution)/shard_map/ppermute | solution.py:72
  44.2 0.7 copy-start.4
  44.2 21.7 %collective-permute-start.6 = (bf16[48,3584]{1,0:T(8,128)(2,1)}, bf16[48,3584]{1,0:T(8,128)(2,1)}, u32[]{:S(2)}, u32[]{:S(2)}) collective-permute-start(bf16[48,3584]{1,0:T(8,128)(2,1)} %collective-permute-done.5), channel_id=1, source_target_pairs={{0,2},{1,3},{2,0},{3,1},{4,6},{5,7},{6,4},{7,5},{8,10},{9,11},{10,... | collective-permute-start | bytes 1032200 | tf_op jit(solution)/shard_map/ppermute | solution.py:72
  92.6 6.0 %copy-start = (bf16[96,3584]{1,0:T(8,128)(2,1)S(1)}, bf16[96,3584]{1,0:T(8,128)(2,1)}, u32[]{:S(2)}) copy-start(bf16[96,3584]{1,0:T(8,128)(2,1)} %constant_dynamic-update-slice_fusion) | copy-start | bytes 2064388
  95.0 27.4 %collective-permute-start.12 = (bf16[96,3584]{1,0:T(8,128)(2,1)}, bf16[96,3584]{1,0:T(8,128)(2,1)}, u32[]{:S(2)}, u32[]{:S(2)}) collective-permute-start(bf16[96,3584]{1,0:T(8,128)(2,1)} %slice.128), channel_id=1, source_target_pairs={{0,2},{1,3},{2,0},{3,1},{4,6},{5,7},{6,4},{7,5},{8,10},{9,11},{10,... | collective-permute-start | bytes 2064392 | tf_op jit(solution)/shard_map/ppermute | solution.py:75
  102.9 5.2 %copy-start.1 = (f32[96,3584]{1,0:T(8,128)S(1)}, f32[96,3584]{1,0:T(8,128)}, u32[]{:S(2)}) copy-start(f32[96,3584]{1,0:T(8,128)} %fusion.20) | copy-start | bytes 4128772
  104.9 16.2 %collective-permute-start.7 = (bf16[48,3584]{1,0:T(8,128)(2,1)}, bf16[48,3584]{1,0:T(8,128)(2,1)}, u32[]{:S(2)}, u32[]{:S(2)}) collective-permute-start(bf16[48,3584]{1,0:T(8,128)(2,1)} %slice.129), channel_id=1, source_target_pairs={{0,2},{1,3},{2,0},{3,1},{4,6},{5,7},{6,4},{7,5},{8,10},{9,11},{10,... | collective-permute-start | bytes 1032200 | tf_op jit(solution)/shard_map/ppermute | solution.py:75
  113.1 31.1 %collective-permute-start.4 = (bf16[48,3584]{1,0:T(8,128)(2,1)S(1)}, bf16[48,3584]{1,0:T(8,128)(2,1)S(1)}, u32[]{:S(2)}, u32[]{:S(2)}) collective-permute-start(bf16[48,3584]{1,0:T(8,128)(2,1)S(1)} %slice.130), channel_id=1, source_target_pairs={{0,2},{1,3},{2,0},{3,1},{4,6},{5,7},{6,4},{7,5},{8,10},{9,11},{10,... | collective-permute-start | bytes 1032200 | tf_op jit(solution)/shard_map/ppermute | solution.py:75
  122.3 21.5 %copy-start.5 = (pred[64,4,48]{0,2,1:T(8,128)(4,1)S(1)}, pred[64,4,48]{0,2,1:T(8,128)(4,1)}, u32[]{:S(2)}) copy-start(pred[64,4,48]{0,2,1:T(8,128)(4,1)} %fusion.18) | copy-start | bytes 36868
  122.3 21.5 %copy-start.8 = (f32[64]{0:T(128)S(1)}, f32[64]{0:T(128)}, u32[]{:S(2)}) copy-start(f32[64]{0:T(128)} %get-tuple-element.15) | copy-start | bytes 772
  122.3 21.5 %collective-permute-start.8 = (bf16[48,3584]{1,0:T(8,128)(2,1)S(1)}, bf16[48,3584]{1,0:T(8,128)(2,1)S(1)}, u32[]{:S(2)}, u32[]{:S(2)}) collective-permute-start(bf16[48,3584]{1,0:T(8,128)(2,1)S(1)} %fusion.9), channel_id=1, source_target_pairs={{0,8},{1,9},{2,10},{3,11},{4,12},{5,13},{6,14},{7,15},{8,0},{9,1},... | collective-permute-start | bytes 1032200 | tf_op jit(solution)/shard_map/ppermute | solution.py:80
  124.0 20.2 %copy-start.2 = (f32[96,3584]{1,0:T(8,128)S(1)}, f32[96,3584]{1,0:T(8,128)}, u32[]{:S(2)}) copy-start(f32[96,3584]{1,0:T(8,128)} %convolution_add_fusion.2) | copy-start | bytes 4128772
  124.0 20.2 %copy-start.9 = (f32[64]{0:T(128)S(1)}, f32[64]{0:T(128)}, u32[]{:S(2)}) copy-start(f32[64]{0:T(128)} %get-tuple-element.16) | copy-start | bytes 772
  124.1 20.5 %collective-permute-start.14 = (bf16[48,3584]{1,0:T(8,128)(2,1)S(1)}, bf16[48,3584]{1,0:T(8,128)(2,1)S(1)}, u32[]{:S(2)}, u32[]{:S(2)}) collective-permute-start(bf16[48,3584]{1,0:T(8,128)(2,1)S(1)} %get-tuple-element.12), channel_id=1, source_target_pairs={{0,4},{1,5},{2,6},{3,7},{4,8},{5,9},{6,10},{7,11},{8,12},{9,13},{1... | collective-permute-start | bytes 1032200 | tf_op jit(solution)/shard_map/ppermute | solution.py:80
  126.5 20.7 %collective-permute-start.13 = (bf16[48,3584]{1,0:T(8,128)(2,1)S(1)}, bf16[48,3584]{1,0:T(8,128)(2,1)S(1)}, u32[]{:S(2)}, u32[]{:S(2)}) collective-permute-start(bf16[48,3584]{1,0:T(8,128)(2,1)S(1)} %get-tuple-element.11), channel_id=1, source_target_pairs={{0,12},{1,13},{2,14},{3,15},{4,0},{5,1},{6,2},{7,3},{8,4},{9,5},{1... | collective-permute-start | bytes 1032200 | tf_op jit(solution)/shard_map/ppermute | solution.py:80
  143.8 0.7 copy-start.7
  144.2 2.9 %copy-start.3 = (bf16[64,3584]{1,0:T(8,128)(2,1)S(1)}, bf16[64,3584]{1,0:T(8,128)(2,1)}, u32[]{:S(2)}) copy-start(bf16[64,3584]{1,0:T(8,128)(2,1)} %param.8) | copy-start | bytes 1376260
  144.2 2.9 %copy-start.6 = (f32[64]{0:T(128)S(1)}, f32[64]{0:T(128)}, u32[]{:S(2)}) copy-start(f32[64]{0:T(128)} %get-tuple-element.13) | copy-start | bytes 772

commit v2 on v0

v2 whole, which is shorter than its diff:
```python
import functools

import jax
import jax.numpy as jnp
from jax import lax
from jax.experimental import pallas as pl
from jax.experimental.pallas import tpu as pltpu
from jax.sharding import PartitionSpec as P

SPLIT = 4
LANES = 128
VMEM = pl.BlockSpec(memory_space=pltpu.VMEM)
SMEM = pl.BlockSpec(memory_space=pltpu.SMEM)
ANY = pl.BlockSpec(memory_space=pl.ANY)


def dot(a, b):
    return jnp.dot(a, b, preferred_element_type=jnp.float32)


def columns_of(width):
    return next(c for c in (512, 256, 128, width) if width % c == 0)


def pack_kernel(experts, capacity, plane_ref, lengths_ref, hidden_ref, gain_ref, ids_ref, gates_ref, *outs):
    packed_refs, slot_ref, weight_ref = outs[:experts], outs[experts], outs[experts + 1]
    tokens, width = hidden_ref.shape
    prompts = lengths_ref.shape[0]
    slots_per = tokens // prompts
    row = lax.broadcasted_iota(jnp.int32, (tokens, 1), 0)
    live = row < 0
    for p in range(prompts):
        live = live | ((row >= p * slots_per) & (row < p * slots_per + lengths_ref[p]))
    lane = lax.broadcasted_iota(jnp.int32, (tokens, LANES), 1)
    chosen = jnp.zeros((tokens, LANES), jnp.float32)
    weight = jnp.zeros((tokens, LANES), jnp.float32)
    for k in range(ids_ref.shape[1]):
        away = ids_ref[:, k : k + 1] - plane_ref[0]
        away = jnp.where(away < 0, away + experts, away)
        hit = ((away == lane) & live).astype(jnp.float32)
        chosen += hit
        weight += hit * gates_ref[:, k : k + 1]
    below = lax.broadcasted_iota(jnp.int32, (tokens, tokens), 1) < lax.broadcasted_iota(
        jnp.int32, (tokens, tokens), 0
    )
    before = dot(below.astype(jnp.bfloat16), chosen.astype(jnp.bfloat16))
    slot = jnp.where(chosen > 0, before, -1.0)
    slot_ref[...] = slot
    weight_ref[...] = weight
    slot_t = slot.T

    hidden = hidden_ref[...].astype(jnp.float32)
    meansq = jnp.mean(hidden * hidden, axis=-1, keepdims=True)
    scale = lax.rsqrt(meansq + 1e-06)
    line = lax.broadcasted_iota(jnp.int32, (capacity, tokens), 0).astype(jnp.float32)
    picker = jnp.concatenate(
        [(line == slot_t[d : d + 1, :]).astype(jnp.float32) for d in range(experts)]
    ).astype(jnp.bfloat16)
    step = columns_of(width)
    for c in range(0, width, step):
        normed = hidden_ref[:, c : c + step].astype(jnp.float32) * scale * gain_ref[:, c : c + step]
        rows = dot(picker, normed.astype(jnp.bfloat16)).astype(jnp.bfloat16)
        for d in range(experts):
            packed_refs[d][:, c : c + step] = rows[d * capacity : (d + 1) * capacity]


def expert_kernel(mine_ref, theirs_ref, *refs):
    weights, (own_ref, sent_ref), held, sems = refs[:6], refs[6:8], refs[8:14], refs[14]
    copies = [pltpu.make_async_copy(weights[i], held[i], sems.at[i]) for i in range(6)]
    for copy in copies:
        copy.start()
    half, width = mine_ref.shape
    rows = jnp.concatenate([mine_ref[...], theirs_ref[...]])
    acts = []
    for k in range(2):
        copies[3 * k].wait()
        gate_p = dot(rows, held[3 * k][...])
        copies[3 * k + 1].wait()
        up_p = dot(rows, held[3 * k + 1][...])
        acts.append((jax.nn.silu(gate_p) * up_p).astype(jnp.bfloat16))
    copies[2].wait()
    copies[5].wait()
    step = columns_of(width)
    for c in range(0, width, step):
        part = dot(acts[0], held[2][:, c : c + step]) + dot(acts[1], held[5][:, c : c + step])
        own_ref[:, c : c + step] = part[:half]
        sent_ref[:, c : c + step] = part[half:].astype(jnp.bfloat16)


def mix_kernel(experts, capacity, hidden_ref, slot_ref, weight_ref, own_ref, other_ref, *refs):
    rows_refs, out_ref = refs[:-1], refs[-1]
    tokens, width = hidden_ref.shape
    line = lax.broadcasted_iota(jnp.int32, (tokens, capacity), 1).astype(jnp.float32)
    placed = [(line == slot_ref[:, d : d + 1]).astype(jnp.bfloat16) for d in range(experts)]
    step = columns_of(width)
    for c in range(0, width, step):
        cols = slice(c, c + step)
        total = hidden_ref[:, cols].astype(jnp.float32)
        for d in range(experts):
            if d:
                rows = rows_refs[d - 1][:, cols]
            else:
                rows = (own_ref[:, cols] + other_ref[:, cols].astype(jnp.float32)).astype(jnp.bfloat16)
            total += weight_ref[:, d : d + 1] * dot(placed[d], rows)
        out_ref[:, cols] = total.astype(jnp.bfloat16)


def body(hidden, lengths, norm_gain, w_gate, w_up, w_down, expert_ids, gate_weights):
    tokens_here, width = hidden.shape
    topk = expert_ids.shape[1]
    ranks = lax.axis_size("ep")
    experts = ranks // SPLIT
    capacity = SPLIT * ((3 * tokens_here * topk + 2 * experts * SPLIT - 1) // (2 * experts * SPLIT))
    capacity = -(-capacity // 16) * 16
    ff = w_gate.shape[-1]
    plane = (lax.axis_index("ep") // SPLIT).astype(jnp.int32).reshape(1)

    swap_core = [(i, i ^ 1) for i in range(ranks)]
    swap_side = [(i, i ^ 2) for i in range(ranks)]

    def shift(d):
        return [(i, (i + SPLIT * d) % ranks) for i in range(ranks)]

    def struct(rows, cols, dtype):
        return jax.ShapeDtypeStruct((rows, cols), dtype)

    block = struct(capacity, width, jnp.bfloat16)
    *packed, slot, weight = pl.pallas_call(
        functools.partial(pack_kernel, experts, capacity),
        out_shape=[block] * experts + [struct(tokens_here, LANES, jnp.float32)] * 2,
        in_specs=[SMEM, SMEM, VMEM, VMEM, VMEM, VMEM],
        out_specs=[VMEM] * (experts + 2),
        compiler_params=pltpu.CompilerParams(vmem_limit_bytes=16 << 20),
    )(plane, lengths, hidden, norm_gain.reshape(1, width), expert_ids, gate_weights)

    own_weights = (w_gate[0], w_up[0], w_down[0])
    weights = own_weights + tuple(lax.ppermute(w, "ep", swap_core) for w in own_weights)

    flops = 2 * 2 * capacity * width * ff * 6
    expert = pl.pallas_call(
        expert_kernel,
        out_shape=[struct(capacity, width, jnp.float32), block],
        in_specs=[VMEM, VMEM] + [ANY] * 6,
        out_specs=[VMEM, VMEM],
        scratch_shapes=[pltpu.VMEM(w.shape, w.dtype) for w in weights] + [pltpu.SemaphoreType.DMA((6,))],
        compiler_params=pltpu.CompilerParams(vmem_limit_bytes=28 << 20),
        cost_estimate=pl.CostEstimate(
            flops=flops, bytes_accessed=12 * width * ff, transcendentals=4 * capacity * ff
        ),
    )

    if experts == 4:
        order = [0, 2, 1, 3]
    else:
        order = list(range(experts))
    arrived = {d: lax.ppermute(packed[d], "ep", shift(d)) if d else packed[0] for d in order}
    back = {}
    for d in order:
        own, sent = expert(arrived[d], lax.ppermute(arrived[d], "ep", swap_side), *weights)
        other = lax.ppermute(sent, "ep", swap_side)
        if d:
            rows = (own + other.astype(jnp.float32)).astype(jnp.bfloat16)
            back[d] = lax.ppermute(rows, "ep", shift(experts - d))
        else:
            back[0] = (own, other)
    return pl.pallas_call(
        functools.partial(mix_kernel, experts, capacity),
        out_shape=struct(tokens_here, width, jnp.bfloat16),
        in_specs=[VMEM] * (experts + 4),
        out_specs=VMEM,
        compiler_params=pltpu.CompilerParams(vmem_limit_bytes=16 << 20),
    )(hidden, slot, weight, *back[0], *(back[d] for d in range(1, experts)))


def solution(mesh):
    return jax.shard_map(
        body,
        mesh=mesh,
        in_specs=(
            P(("group", "ep"), None),
            P(("group", "ep")),
            P(),
            P("ep", None, None),
            P("ep", None, None),
            P("ep", None, None),
            P(("group", "ep"), None),
            P(("group", "ep"), None),
        ),
        out_specs=P(("group", "ep"), None),
        check_vma=False,
    )
```

time: 280 us -> 113 us (0.40)
  blocking collectives: 254 us -> 0 us
  waiting for transfers between devices: 0 us -> 69.9 us
  Pallas kernels: 0 us -> 17.8 us
  matrix products: 17.2 us -> 0 us
  starting transfers between devices: 0 us -> 15.6 us
  local copies, waits for them, and re-layouts: 3.22 us -> 8.44 us
  other arithmetic: 3.99 us -> 0.18 us
    all_to_all x2 -> x0, blocking collectives: 254 us -> none  [the longest x1 129 us: body(): lax.all_to_all(outgoing, 'ep', split_axis=0, concat_axis=0, tiled=True)]
    ppermute x0 -> x17, waiting for transfers between devices: none -> 69.9 us  [the longest x3 29.6 us: body(): lax.ppermute(packed[d], 'ep', shift(d))]
    pallas_call x0 -> x6, Pallas kernels: none -> 17.8 us  [the longest x4 15.1 us: body(): expert(arrived[d], lax.ppermute(arrived[d], 'ep', swap_side), *weights)]
    dot_general x4 -> x0, matrix products: 17.2 us -> none  [the longest x1 11.4 us: expert_slice(): jnp.dot(act, w_down[0], preferred_element_type=jnp.float32)]
    ppermute x0 -> x17, starting transfers between devices: none -> 15.6 us  [the longest x4 5.33 us: body(): other = lax.ppermute(sent, 'ep', swap_side)]
    unnamed x8 -> x16, local copies, waits for them, and re-layouts: 2.44 us -> 7.71 us
    reduce_sum x4 -> x0, other arithmetic: 3.76 us -> none  [the longest x1 1.21 us: body(): meansq = jnp.mean(hidden_f * hidden_f, axis=-1, keepdims=True)]
  transfers between devices with their start and end apart: 0 -> 17, of which waited for: 0 -> 10; matrix products, arithmetic and copies ran while one was open for 0% -> 2% of each run, Pallas kernels for 0% -> 15%
where the time goes in v2:
time: 113 us; the launch traced here: 112 us
  waiting for transfers between devices  69.9 us (62%)
  Pallas kernels  17.8 us (16%)
  starting transfers between devices  15.6 us (14%)
  local copies, waits for them, and re-layouts  8.44 us (7%)
    ppermute x3, waiting for transfers between devices, body(): lax.ppermute(packed[d], 'ep', shift(d))  29.6 us
    ppermute x4, waiting for transfers between devices, body(): other = lax.ppermute(sent, 'ep', swap_side)  22.5 us
    pallas_call x4, Pallas kernels, body(): expert(arrived[d], lax.ppermute(arrived[d], 'ep', swap_side), *weights)  15.1 us
    ppermute x4, waiting for transfers between devices, body(): lax.ppermute(arrived[d], 'ep', swap_side)  9.45 us
    ppermute x3, waiting for transfers between devices, body(): back[d] = lax.ppermute(rows, 'ep', shift(experts - d))  8.4 us
    unnamed x16, local copies, waits for them, and re-layouts  7.71 us
    ppermute x4, starting transfers between devices, body(): other = lax.ppermute(sent, 'ep', swap_side)  5.33 us
    ppermute x3, starting transfers between devices, body(): lax.ppermute(packed[d], 'ep', shift(d))  5.07 us
  transfers between devices with their start and end apart: 17, of which 10 were waited for; matrix products, arithmetic and copies ran while one was open for 2% of the time, Pallas kernels for 15%

profile of v2, /device:TPU:0, one launch (start us, length us, event | category | flops | bytes accessed | tf_op | source)
XLA Modules:
  0.0 112.1 jit_solution(8153745467930428717)
XLA Ops:
  0.0 0.5 collective-permute-start.1
  0.5 0.1 collective-permute-start.2
  0.5 0.5 collective-permute-start.3
  1.0 0.8 copy.10.gates_ref
  1.7 0.8 copy.9.ids_ref
  2.5 0.7 reshape.7.gain_ref
  3.2 0.0 copy-start.4
  3.3 1.0 copy-done.4
  4.3 0.7 copy-done.6
  4.9 1.3 %shard_map.82 = (bf16[48,3584]{1,0:T(8,128)(2,1)S(1)}, bf16[48,3584]{1,0:T(8,128)(2,1)S(1)}, bf16[48,3584]{1,0:T(8,128)(2,1)S(1)}, bf16[48,3584]{1,0:T(8,128)(2,...) custom-call(s32[1]{0:T(128)} %bitcast.plane_ref, s32[2]{0:T(128)S(1)} %copy-done.6, bf16[64,3584]{1,0:T(8,128)(2,1)S(1)} %copy-done.4, ...), custom_call_target="tpu_custom_call" | custom-call | tf_op jit(solution)/shard_map/pallas_call | solution.py:128
  6.3 4.7 %collective-permute-start.13 = (bf16[48,3584]{1,0:T(8,128)(2,1)S(1)}, bf16[48,3584]{1,0:T(8,128)(2,1)S(1)}, u32[]{:S(2)}, u32[]{:S(2)}) collective-permute-start(bf16[48,3584]{1,0:T(8,128)(2,1)S(1)} %get-tuple-element.30), channel_id=1, source_target_pairs={{0,12},{1,13},{2,14},{3,15},{4,0},{5,1},{6,2},{7,3},{8,4},{9,5},{1... | collective-permute-start | bytes 1032200 | tf_op jit(solution)/shard_map/ppermute | solution.py:156
  10.9 0.0 collective-permute-start.9
  10.9 8.4 %collective-permute-done.13.mine_ref = bf16[48,3584]{1,0:T(8,128)(2,1)S(1)} collective-permute-done((bf16[48,3584]{1,0:T(8,128)(2,1)S(1)}, bf16[48,3584]{1,0:T(8,128)(2,1)S(1)}, u32[]{:S(2)}, u32[]{:S(2)}) %collective-permute-start.13) | collective-permute-done | bytes 344096 | tf_op jit(solution)/shard_map/ppermute | solution.py:156
  19.3 0.4 collective-permute-start.5
  19.7 21.2 %collective-permute-done.9.mine_ref = bf16[48,3584]{1,0:T(8,128)(2,1)S(1)} collective-permute-done((bf16[48,3584]{1,0:T(8,128)(2,1)S(1)}, bf16[48,3584]{1,0:T(8,128)(2,1)S(1)}, u32[]{:S(2)}, u32[]{:S(2)}) %collective-permute-start.9) | collective-permute-done | bytes 344096 | tf_op jit(solution)/shard_map/ppermute | solution.py:156
  40.9 1.5 %collective-permute-start.14 = (bf16[48,3584]{1,0:T(8,128)(2,1)S(1)}, bf16[48,3584]{1,0:T(8,128)(2,1)S(1)}, u32[]{:S(2)}, u32[]{:S(2)}) collective-permute-start(bf16[48,3584]{1,0:T(8,128)(2,1)S(1)} %collective-permute-done.13.mine_ref), channel_id=1, source_target_pairs={{0,2},{1,3},{2,0},{3,1},{4,6},{5,7},{6,4},{7,5},{8,10},{9,11},{10,... | collective-permute-start | bytes 1032200 | tf_op jit(solution)/shard_map/ppermute | solution.py:159
  42.4 0.0 collective-permute-done.5.mine_ref
  42.4 0.5 collective-permute-start.10
  42.9 8.9 %collective-permute-done.14.theirs_ref = bf16[48,3584]{1,0:T(8,128)(2,1)S(1)} collective-permute-done((bf16[48,3584]{1,0:T(8,128)(2,1)S(1)}, bf16[48,3584]{1,0:T(8,128)(2,1)S(1)}, u32[]{:S(2)}, u32[]{:S(2)}) %collective-permute-start.14) | collective-permute-done | bytes 344096 | tf_op jit(solution)/shard_map/ppermute | solution.py:159
  51.9 1.5 %collective-permute-start.6 = (bf16[48,3584]{1,0:T(8,128)(2,1)S(1)}, bf16[48,3584]{1,0:T(8,128)(2,1)S(1)}, u32[]{:S(2)}, u32[]{:S(2)}) collective-permute-start(bf16[48,3584]{1,0:T(8,128)(2,1)S(1)} %collective-permute-done.5.mine_ref), channel_id=1, source_target_pairs={{0,2},{1,3},{2,0},{3,1},{4,6},{5,7},{6,4},{7,5},{8,10},{9,11},{10,... | collective-permute-start | bytes 1032200 | tf_op jit(solution)/shard_map/ppermute | solution.py:159
  53.4 0.5 collective-permute-start
  53.9 1.5 %copy-done = bf16[1,3584,256]{2,1,0:T(8,128)(2,1)S(1)} copy-done((bf16[1,3584,256]{2,1,0:T(8,128)(2,1)S(1)}, bf16[1,3584,256]{2,1,0:T(8,128)(2,1)}, u32[]{:S(2)}) %copy-start) | copy-done | bytes 1835032
  55.4 1.5 %copy-done.2 = bf16[1,3584,256]{2,1,0:T(8,128)(2,1)S(1)} copy-done((bf16[1,3584,256]{2,1,0:T(8,128)(2,1)S(1)}, bf16[1,3584,256]{2,1,0:T(8,128)(2,1)}, u32[]{:S(2)}) %copy-start.2) | copy-done | bytes 1835032
  56.9 1.5 %copy-done.3 = bf16[1,256,3584]{2,1,0:T(8,128)(2,1)S(1)} copy-done((bf16[1,256,3584]{2,1,0:T(8,128)(2,1)S(1)}, bf16[1,256,3584]{2,1,0:T(8,128)(2,1)}, u32[]{:S(2)}) %copy-start.3) | copy-done | bytes 1835032
  58.4 3.8 %shard_map.86 = (f32[48,3584]{1,0:T(8,128)S(1)}, bf16[48,3584]{1,0:T(8,128)(2,1)S(1)}) custom-call(bf16[48,3584]{1,0:T(8,128)(2,1)S(1)} %collective-permute-done.13.mine_ref, bf16[48,3584]{1,0:T(8,128)(2,1)S(1)} %collective-permute-done.14.theirs_ref, bf16[3584,256]{1,0:T(8,128)(2,1)S(1)} %bitcast.5, bf16[3584,256]{1,0:T(8,128)(2,1)S(1)} %bitcast.10, ...), custom_call_target="tpu_custom_call" | custom-call | flops 1056964608 | bytes 11010048 | tf_op jit(solution)/shard_map/pallas_call | solution.py:159
  62.2 1.6 %collective-permute-start.15 = (bf16[48,3584]{1,0:T(8,128)(2,1)S(1)}, bf16[48,3584]{1,0:T(8,128)(2,1)S(1)}, u32[]{:S(2)}, u32[]{:S(2)}) collective-permute-start(bf16[48,3584]{1,0:T(8,128)(2,1)S(1)} %get-tuple-element.32), channel_id=1, source_target_pairs={{0,2},{1,3},{2,0},{3,1},{4,6},{5,7},{6,4},{7,5},{8,10},{9,11},{10,... | collective-permute-start | bytes 1032200 | tf_op jit(solution)/shard_map/ppermute | solution.py:160
  63.8 0.0 collective-permute-done.10.theirs_ref
  63.8 3.8 %shard_map.85 = (f32[48,3584]{1,0:T(8,128)S(1)}, bf16[48,3584]{1,0:T(8,128)(2,1)S(1)}) custom-call(bf16[48,3584]{1,0:T(8,128)(2,1)S(1)} %collective-permute-done.9.mine_ref, bf16[48,3584]{1,0:T(8,128)(2,1)S(1)} %collective-permute-done.10.theirs_ref, bf16[3584,256]{1,0:T(8,128)(2,1)S(1)} %bitcast.6, bf16[3584,256]{1,0:T(8,128)(2,1)S(1)} %bitcast.11, ...), custom_call_target="tpu_custom_call" | custom-call | flops 1056964608 | bytes 11010048 | tf_op jit(solution)/shard_map/pallas_call | solution.py:159
  67.5 0.0 copy-start.1
  67.6 0.6 collective-permute-start.11
  68.1 3.8 %shard_map.84 = (f32[48,3584]{1,0:T(8,128)S(1)}, bf16[48,3584]{1,0:T(8,128)(2,1)S(1)}) custom-call(bf16[48,3584]{1,0:T(8,128)(2,1)S(1)} %collective-permute-done.5.mine_ref, bf16[48,3584]{1,0:T(8,128)(2,1)S(1)} %collective-permute-done.6.theirs_ref, bf16[3584,256]{1,0:T(8,128)(2,1)S(1)} %bitcast.7, bf16[3584,256]{1,0:T(8,128)(2,1)S(1)} %bitcast.12, ...), custom_call_target="tpu_custom_call" | custom-call | flops 1056964608 | bytes 11010048 | tf_op jit(solution)/shard_map/pallas_call | solution.py:159
  71.9 1.6 %collective-permute-start.7 = (bf16[48,3584]{1,0:T(8,128)(2,1)S(1)}, bf16[48,3584]{1,0:T(8,128)(2,1)S(1)}, u32[]{:S(2)}, u32[]{:S(2)}) collective-permute-start(bf16[48,3584]{1,0:T(8,128)(2,1)S(1)} %get-tuple-element.26), channel_id=1, source_target_pairs={{0,2},{1,3},{2,0},{3,1},{4,6},{5,7},{6,4},{7,5},{8,10},{9,11},{10,... | collective-permute-start | bytes 1032200 | tf_op jit(solution)/shard_map/ppermute | solution.py:160
  73.5 0.5 collective-permute-done.theirs_ref
  74.0 3.8 %shard_map.83 = (f32[48,3584]{1,0:T(8,128)S(1)}, bf16[48,3584]{1,0:T(8,128)(2,1)S(1)}) custom-call(bf16[48,3584]{1,0:T(8,128)(2,1)S(1)} %get-tuple-element.21.mine_ref, bf16[48,3584]{1,0:T(8,128)(2,1)S(1)} %collective-permute-done.theirs_ref, bf16[3584,256]{1,0:T(8,128)(2,1)S(1)} %bitcast.8, bf16[3584,256]{1,0:T(8,128)(2,1)S(1)} %bitcast.13, ...), custom_call_target="tpu_custom_call" | custom-call | flops 1056964608 | bytes 11010048 | tf_op jit(solution)/shard_map/pallas_call | solution.py:159
  77.8 1.6 %collective-permute-start.4 = (bf16[48,3584]{1,0:T(8,128)(2,1)S(1)}, bf16[48,3584]{1,0:T(8,128)(2,1)S(1)}, u32[]{:S(2)}, u32[]{:S(2)}) collective-permute-start(bf16[48,3584]{1,0:T(8,128)(2,1)S(1)} %get-tuple-element.23), channel_id=1, source_target_pairs={{0,2},{1,3},{2,0},{3,1},{4,6},{5,7},{6,4},{7,5},{8,10},{9,11},{10,... | collective-permute-start | bytes 1032200 | tf_op jit(solution)/shard_map/ppermute | solution.py:160
  79.4 2.0 %collective-permute-done.15 = bf16[48,3584]{1,0:T(8,128)(2,1)S(1)} collective-permute-done((bf16[48,3584]{1,0:T(8,128)(2,1)S(1)}, bf16[48,3584]{1,0:T(8,128)(2,1)S(1)}, u32[]{:S(2)}, u32[]{:S(2)}) %collective-permute-start.15) | collective-permute-done | bytes 344096 | tf_op jit(solution)/shard_map/ppermute | solution.py:160
  81.4 0.1 add_convert_fusion
  81.4 0.1 collective-permute-start.16
  81.5 7.2 %collective-permute-done.11 = bf16[48,3584]{1,0:T(8,128)(2,1)S(1)} collective-permute-done((bf16[48,3584]{1,0:T(8,128)(2,1)S(1)}, bf16[48,3584]{1,0:T(8,128)(2,1)S(1)}, u32[]{:S(2)}, u32[]{:S(2)}) %collective-permute-start.11) | collective-permute-done | bytes 344096 | tf_op jit(solution)/shard_map/ppermute | solution.py:160
  88.7 0.1 add_convert_fusion.1
  88.8 0.1 collective-permute-start.12
  88.9 7.2 %collective-permute-done.7 = bf16[48,3584]{1,0:T(8,128)(2,1)S(1)} collective-permute-done((bf16[48,3584]{1,0:T(8,128)(2,1)S(1)}, bf16[48,3584]{1,0:T(8,128)(2,1)S(1)}, u32[]{:S(2)}, u32[]{:S(2)}) %collective-permute-start.7) | collective-permute-done | bytes 344096 | tf_op jit(solution)/shard_map/ppermute | solution.py:160
  96.1 0.1 add_convert_fusion.2
  96.2 0.1 collective-permute-start.8
  96.2 6.0 %collective-permute-done.4.other_ref = bf16[48,3584]{1,0:T(8,128)(2,1)S(1)} collective-permute-done((bf16[48,3584]{1,0:T(8,128)(2,1)S(1)}, bf16[48,3584]{1,0:T(8,128)(2,1)S(1)}, u32[]{:S(2)}, u32[]{:S(2)}) %collective-permute-start.4) | collective-permute-done | bytes 344096 | tf_op jit(solution)/shard_map/ppermute | solution.py:160
  102.2 3.5 %collective-permute-done.12.refs_1_ = bf16[48,3584]{1,0:T(8,128)(2,1)S(1)} collective-permute-done((bf16[48,3584]{1,0:T(8,128)(2,1)S(1)}, bf16[48,3584]{1,0:T(8,128)(2,1)S(1)}, u32[]{:S(2)}, u32[]{:S(2)}) %collective-permute-start.12) | collective-permute-done | bytes 344096 | tf_op jit(solution)/shard_map/ppermute | solution.py:163
  105.7 4.9 %collective-permute-done.8.refs_0_ = bf16[48,3584]{1,0:T(8,128)(2,1)S(1)} collective-permute-done((bf16[48,3584]{1,0:T(8,128)(2,1)S(1)}, bf16[48,3584]{1,0:T(8,128)(2,1)S(1)}, u32[]{:S(2)}, u32[]{:S(2)}) %collective-permute-start.8) | collective-permute-done | bytes 344096 | tf_op jit(solution)/shard_map/ppermute | solution.py:163
  110.6 1.5 %shard_map.87 = bf16[64,3584]{1,0:T(8,128)(2,1)} custom-call(bf16[64,3584]{1,0:T(8,128)(2,1)S(1)} %copy-done.5, f32[64,128]{1,0:T(8,128)S(1)} %get-tuple-element.19.slot_ref, f32[64,128]{1,0:T(8,128)S(1)} %get-tuple-element.20.weight_ref, f32[48,3584]{1,0:T(8,128)S(1)} %get-tuple-element.22.own_ref, bf16[48,3584]{1,0:T(8,128)(2,1)S(1)} %collective-permute-done.4.other_ref, ...), custom_call_target="tpu_custom_call" | custom-call | tf_op jit(solution)/shard_map/pallas_call | solution.py:166
  (12 shorter events, 0.0 us)
Async XLA Ops:
  0.0 53.4 %collective-permute-start.1 = (bf16[3584,256]{1,0:T(8,128)(2,1)}, bf16[3584,256]{1,0:T(8,128)(2,1)S(1)}, u32[]{:S(2)}, u32[]{:S(2)}) collective-permute-start(bf16[3584,256]{1,0:T(8,128)(2,1)} %bitcast.4), channel_id=1, source_target_pairs={{0,1},{1,0},{2,3},{3,2},{4,5},{5,4},{6,7},{7,6},{8,9},{9,8},{10,11... | collective-permute-start | bytes 5505032 | tf_op jit(solution)/shard_map/ppermute | solution.py:137
  0.5 53.5 %collective-permute-start.2 = (bf16[3584,256]{1,0:T(8,128)(2,1)}, bf16[3584,256]{1,0:T(8,128)(2,1)}, u32[]{:S(2)}, u32[]{:S(2)}) collective-permute-start(bf16[3584,256]{1,0:T(8,128)(2,1)} %bitcast.9), channel_id=1, source_target_pairs={{0,1},{1,0},{2,3},{3,2},{4,5},{5,4},{6,7},{7,6},{8,9},{9,8},{10,11... | collective-permute-start | bytes 5505032 | tf_op jit(solution)/shard_map/ppermute | solution.py:137
  0.5 53.4 %collective-permute-start.3 = (bf16[256,3584]{1,0:T(8,128)(2,1)}, bf16[256,3584]{1,0:T(8,128)(2,1)}, u32[]{:S(2)}, u32[]{:S(2)}) collective-permute-start(bf16[256,3584]{1,0:T(8,128)(2,1)} %bitcast.14), channel_id=1, source_target_pairs={{0,1},{1,0},{2,3},{3,2},{4,5},{5,4},{6,7},{7,6},{8,9},{9,8},{10,11... | collective-permute-start | bytes 5505032 | tf_op jit(solution)/shard_map/ppermute | solution.py:137
  3.2 1.0 copy-start.4
  4.3 0.7 copy-start.6
  6.3 13.1 %collective-permute-start.13 = (bf16[48,3584]{1,0:T(8,128)(2,1)S(1)}, bf16[48,3584]{1,0:T(8,128)(2,1)S(1)}, u32[]{:S(2)}, u32[]{:S(2)}) collective-permute-start(bf16[48,3584]{1,0:T(8,128)(2,1)S(1)} %get-tuple-element.30), channel_id=1, source_target_pairs={{0,12},{1,13},{2,14},{3,15},{4,0},{5,1},{6,2},{7,3},{8,4},{9,5},{1... | collective-permute-start | bytes 1032200 | tf_op jit(solution)/shard_map/ppermute | solution.py:156
  10.9 30.0 %collective-permute-start.9 = (bf16[48,3584]{1,0:T(8,128)(2,1)S(1)}, bf16[48,3584]{1,0:T(8,128)(2,1)S(1)}, u32[]{:S(2)}, u32[]{:S(2)}) collective-permute-start(bf16[48,3584]{1,0:T(8,128)(2,1)S(1)} %get-tuple-element.27), channel_id=1, source_target_pairs={{0,8},{1,9},{2,10},{3,11},{4,12},{5,13},{6,14},{7,15},{8,0},{9,1},... | collective-permute-start | bytes 1032200 | tf_op jit(solution)/shard_map/ppermute | solution.py:156
  19.3 23.1 %collective-permute-start.5 = (bf16[48,3584]{1,0:T(8,128)(2,1)S(1)}, bf16[48,3584]{1,0:T(8,128)(2,1)S(1)}, u32[]{:S(2)}, u32[]{:S(2)}) collective-permute-start(bf16[48,3584]{1,0:T(8,128)(2,1)S(1)} %get-tuple-element.24), channel_id=1, source_target_pairs={{0,4},{1,5},{2,6},{3,7},{4,8},{5,9},{6,10},{7,11},{8,12},{9,13},{1... | collective-permute-start | bytes 1032200 | tf_op jit(solution)/shard_map/ppermute | solution.py:156
  40.9 11.0 %collective-permute-start.14 = (bf16[48,3584]{1,0:T(8,128)(2,1)S(1)}, bf16[48,3584]{1,0:T(8,128)(2,1)S(1)}, u32[]{:S(2)}, u32[]{:S(2)}) collective-permute-start(bf16[48,3584]{1,0:T(8,128)(2,1)S(1)} %collective-permute-done.13.mine_ref), channel_id=1, source_target_pairs={{0,2},{1,3},{2,0},{3,1},{4,6},{5,7},{6,4},{7,5},{8,10},{9,11},{10,... | collective-permute-start | bytes 1032200 | tf_op jit(solution)/shard_map/ppermute | solution.py:159
  42.4 21.3 %collective-permute-start.10 = (bf16[48,3584]{1,0:T(8,128)(2,1)S(1)}, bf16[48,3584]{1,0:T(8,128)(2,1)S(1)}, u32[]{:S(2)}, u32[]{:S(2)}) collective-permute-start(bf16[48,3584]{1,0:T(8,128)(2,1)S(1)} %collective-permute-done.9.mine_ref), channel_id=1, source_target_pairs={{0,2},{1,3},{2,0},{3,1},{4,6},{5,7},{6,4},{7,5},{8,10},{9,11},{10,... | collective-permute-start | bytes 1032200 | tf_op jit(solution)/shard_map/ppermute | solution.py:159
  51.9 16.3 %collective-permute-start.6 = (bf16[48,3584]{1,0:T(8,128)(2,1)S(1)}, bf16[48,3584]{1,0:T(8,128)(2,1)S(1)}, u32[]{:S(2)}, u32[]{:S(2)}) collective-permute-start(bf16[48,3584]{1,0:T(8,128)(2,1)S(1)} %collective-permute-done.5.mine_ref), channel_id=1, source_target_pairs={{0,2},{1,3},{2,0},{3,1},{4,6},{5,7},{6,4},{7,5},{8,10},{9,11},{10,... | collective-permute-start | bytes 1032200 | tf_op jit(solution)/shard_map/ppermute | solution.py:159
  53.4 20.6 %collective-permute-start = (bf16[48,3584]{1,0:T(8,128)(2,1)S(1)}, bf16[48,3584]{1,0:T(8,128)(2,1)S(1)}, u32[]{:S(2)}, u32[]{:S(2)}) collective-permute-start(bf16[48,3584]{1,0:T(8,128)(2,1)S(1)} %get-tuple-element.21.mine_ref), channel_id=1, source_target_pairs={{0,2},{1,3},{2,0},{3,1},{4,6},{5,7},{6,4},{7,5},{8,10},{9,11},{10,... | collective-permute-start | bytes 1032200 | tf_op jit(solution)/shard_map/ppermute | solution.py:159
  53.9 1.5 %copy-start = (bf16[1,3584,256]{2,1,0:T(8,128)(2,1)S(1)}, bf16[1,3584,256]{2,1,0:T(8,128)(2,1)}, u32[]{:S(2)}) copy-start(bf16[1,3584,256]{2,1,0:T(8,128)(2,1)} %param.11) | copy-start | bytes 5505028
  55.4 1.5 %copy-start.2 = (bf16[1,3584,256]{2,1,0:T(8,128)(2,1)S(1)}, bf16[1,3584,256]{2,1,0:T(8,128)(2,1)}, u32[]{:S(2)}) copy-start(bf16[1,3584,256]{2,1,0:T(8,128)(2,1)} %param.12) | copy-start | bytes 5505028
  56.9 1.5 %copy-start.3 = (bf16[1,256,3584]{2,1,0:T(8,128)(2,1)S(1)}, bf16[1,256,3584]{2,1,0:T(8,128)(2,1)}, u32[]{:S(2)}) copy-start(bf16[1,256,3584]{2,1,0:T(8,128)(2,1)} %param.13) | copy-start | bytes 5505028
  62.2 19.2 %collective-permute-start.15 = (bf16[48,3584]{1,0:T(8,128)(2,1)S(1)}, bf16[48,3584]{1,0:T(8,128)(2,1)S(1)}, u32[]{:S(2)}, u32[]{:S(2)}) collective-permute-start(bf16[48,3584]{1,0:T(8,128)(2,1)S(1)} %get-tuple-element.32), channel_id=1, source_target_pairs={{0,2},{1,3},{2,0},{3,1},{4,6},{5,7},{6,4},{7,5},{8,10},{9,11},{10,... | collective-permute-start | bytes 1032200 | tf_op jit(solution)/shard_map/ppermute | solution.py:160
  67.5 6.5 %copy-start.1 = (bf16[1,3584,256]{2,1,0:T(8,128)(2,1)S(1)}, bf16[1,3584,256]{2,1,0:T(8,128)(2,1)}, u32[]{:S(2)}) copy-start(bf16[1,3584,256]{2,1,0:T(8,128)(2,1)} %param.11) | copy-start | bytes 5505028
  67.6 21.2 %collective-permute-start.11 = (bf16[48,3584]{1,0:T(8,128)(2,1)S(1)}, bf16[48,3584]{1,0:T(8,128)(2,1)S(1)}, u32[]{:S(2)}, u32[]{:S(2)}) collective-permute-start(bf16[48,3584]{1,0:T(8,128)(2,1)S(1)} %get-tuple-element.29), channel_id=1, source_target_pairs={{0,2},{1,3},{2,0},{3,1},{4,6},{5,7},{6,4},{7,5},{8,10},{9,11},{10,... | collective-permute-start | bytes 1032200 | tf_op jit(solution)/shard_map/ppermute | solution.py:160
  71.9 24.2 %collective-permute-start.7 = (bf16[48,3584]{1,0:T(8,128)(2,1)S(1)}, bf16[48,3584]{1,0:T(8,128)(2,1)S(1)}, u32[]{:S(2)}, u32[]{:S(2)}) collective-permute-start(bf16[48,3584]{1,0:T(8,128)(2,1)S(1)} %get-tuple-element.26), channel_id=1, source_target_pairs={{0,2},{1,3},{2,0},{3,1},{4,6},{5,7},{6,4},{7,5},{8,10},{9,11},{10,... | collective-permute-start | bytes 1032200 | tf_op jit(solution)/shard_map/ppermute | solution.py:160
  77.8 24.4 %collective-permute-start.4 = (bf16[48,3584]{1,0:T(8,128)(2,1)S(1)}, bf16[48,3584]{1,0:T(8,128)(2,1)S(1)}, u32[]{:S(2)}, u32[]{:S(2)}) collective-permute-start(bf16[48,3584]{1,0:T(8,128)(2,1)S(1)} %get-tuple-element.23), channel_id=1, source_target_pairs={{0,2},{1,3},{2,0},{3,1},{4,6},{5,7},{6,4},{7,5},{8,10},{9,11},{10,... | collective-permute-start | bytes 1032200 | tf_op jit(solution)/shard_map/ppermute | solution.py:160
  81.4 29.2 %copy-start.5 = (bf16[64,3584]{1,0:T(8,128)(2,1)S(1)}, bf16[64,3584]{1,0:T(8,128)(2,1)}, u32[]{:S(2)}) copy-start(bf16[64,3584]{1,0:T(8,128)(2,1)} %hidden_ref.3) | copy-start | bytes 1376260
  81.4 20.8 %collective-permute-start.16 = (bf16[48,3584]{1,0:T(8,128)(2,1)S(1)}, bf16[48,3584]{1,0:T(8,128)(2,1)S(1)}, u32[]{:S(2)}, u32[]{:S(2)}) collective-permute-start(bf16[48,3584]{1,0:T(8,128)(2,1)S(1)} %add_convert_fusion), channel_id=1, source_target_pairs={{0,4},{1,5},{2,6},{3,7},{4,8},{5,9},{6,10},{7,11},{8,12},{9,13},{1... | collective-permute-start | bytes 1032200 | tf_op jit(solution)/shard_map/ppermute | solution.py:163
  88.8 16.9 %collective-permute-start.12 = (bf16[48,3584]{1,0:T(8,128)(2,1)S(1)}, bf16[48,3584]{1,0:T(8,128)(2,1)S(1)}, u32[]{:S(2)}, u32[]{:S(2)}) collective-permute-start(bf16[48,3584]{1,0:T(8,128)(2,1)S(1)} %add_convert_fusion.1), channel_id=1, source_target_pairs={{0,8},{1,9},{2,10},{3,11},{4,12},{5,13},{6,14},{7,15},{8,0},{9,1},... | collective-permute-start | bytes 1032200 | tf_op jit(solution)/shard_map/ppermute | solution.py:163
  96.2 14.4 %collective-permute-start.8 = (bf16[48,3584]{1,0:T(8,128)(2,1)S(1)}, bf16[48,3584]{1,0:T(8,128)(2,1)S(1)}, u32[]{:S(2)}, u32[]{:S(2)}) collective-permute-start(bf16[48,3584]{1,0:T(8,128)(2,1)S(1)} %add_convert_fusion.2), channel_id=1, source_target_pairs={{0,12},{1,13},{2,14},{3,15},{4,0},{5,1},{6,2},{7,3},{8,4},{9,5},{1... | collective-permute-start | bytes 1032200 | tf_op jit(solution)/shard_map/ppermute | solution.py:163

commit v3 on v2

v3 whole, which is shorter than its diff:
```python
import functools

import jax
import jax.numpy as jnp
from jax import lax
from jax.experimental import pallas as pl
from jax.experimental.pallas import tpu as pltpu
from jax.sharding import PartitionSpec as P

SPLIT = 4
VMEM_BYTES = 60 << 20
VMEM = pl.BlockSpec(memory_space=pltpu.VMEM)
SMEM = pl.BlockSpec(memory_space=pltpu.SMEM)
HBM = pl.BlockSpec(memory_space=pltpu.HBM)


def dot(a, b):
    return jnp.dot(a, b, preferred_element_type=jnp.float32)


def columns_of(width):
    return next(c for c in (512, 256, 128, width) if width % c == 0)


def pack_kernel(experts, capacity, plane_ref, lengths_ref, hidden_ref, gain_ref, ids_ref, gates_ref, *outs):
    packed_refs, slot_ref, weight_ref = outs[:experts], outs[experts], outs[experts + 1]
    tokens, width = hidden_ref.shape
    prompts = lengths_ref.shape[0]
    slots_per = tokens // prompts
    column = lax.broadcasted_iota(jnp.int32, (1, tokens), 1)
    live = column < 0
    for p in range(prompts):
        live = live | ((column >= p * slots_per) & (column < p * slots_per + lengths_ref[p]))
    lines = slot_ref.shape[1]
    line = lax.broadcasted_iota(jnp.int32, (lines, tokens), 0)
    chosen = jnp.zeros((lines, tokens), jnp.float32)
    weight = jnp.zeros((lines, tokens), jnp.float32)
    for k in range(ids_ref.shape[0]):
        away = ids_ref[k : k + 1, :] - plane_ref[0]
        away = jnp.where(away < 0, away + experts, away)
        hit = ((away == line) & live).astype(jnp.float32)
        chosen += hit
        weight += hit * gates_ref[k : k + 1, :]
    earlier = lax.broadcasted_iota(jnp.int32, (tokens, tokens), 0) < lax.broadcasted_iota(
        jnp.int32, (tokens, tokens), 1
    )
    before = dot(chosen.astype(jnp.bfloat16), earlier.astype(jnp.bfloat16))
    slot = jnp.where(chosen > 0, before, -1.0)
    slot_ref[...] = slot.T
    weight_ref[...] = weight.T

    hidden = hidden_ref[...].astype(jnp.float32)
    meansq = jnp.mean(hidden * hidden, axis=-1, keepdims=True)
    scale = lax.rsqrt(meansq + 1e-06)
    place = lax.broadcasted_iota(jnp.int32, (capacity, tokens), 0).astype(jnp.float32)
    picker = jnp.concatenate(
        [(place == slot[d : d + 1, :]).astype(jnp.float32) for d in range(experts)]
    ).astype(jnp.bfloat16)
    step = columns_of(width)
    for c in range(0, width, step):
        normed = hidden_ref[:, c : c + step].astype(jnp.float32) * scale * gain_ref[c : c + step][None, :]
        rows = dot(picker, normed.astype(jnp.bfloat16)).astype(jnp.bfloat16)
        for d in range(experts):
            packed_refs[d][:, c : c + step] = rows[d * capacity : (d + 1) * capacity]


def activate(rows, gate_ref, up_ref):
    return (jax.nn.silu(dot(rows, gate_ref[...])) * dot(rows, up_ref[...])).astype(jnp.bfloat16)


def first_kernel(rows_ref, gate_ref, up_ref, down_ref, out_ref):
    act = activate(rows_ref[...], gate_ref, up_ref)
    step = columns_of(out_ref.shape[1])
    for c in range(0, out_ref.shape[1], step):
        out_ref[:, c : c + step] = dot(act, down_ref[:, c : c + step])


def expert_kernel(begun, mine_ref, theirs_ref, *refs):
    weights, (own_ref, sent_ref) = refs[:6], refs[-2:]
    half, width = mine_ref.shape
    rows = jnp.concatenate([mine_ref[...], theirs_ref[...]])
    near = activate(theirs_ref[...] if begun else rows, *weights[:2])
    far = activate(rows, *weights[3:5])
    step = columns_of(width)
    for c in range(0, width, step):
        cols = slice(c, c + step)
        part, other = dot(near, weights[2][:, cols]), dot(far, weights[5][:, cols])
        here = refs[6][:, cols] if begun else part[:half]
        own_ref[:, cols] = here + other[:half]
        sent_ref[:, cols] = (part[-half:] + other[half:]).astype(jnp.bfloat16)


def mix_kernel(experts, capacity, hidden_ref, slot_ref, weight_ref, own_ref, other_ref, *refs):
    rows_refs, out_ref = refs[:-1], refs[-1]
    tokens, width = hidden_ref.shape
    line = lax.broadcasted_iota(jnp.int32, (tokens, capacity), 1).astype(jnp.float32)
    placed = [(line == slot_ref[:, d : d + 1]).astype(jnp.bfloat16) for d in range(experts)]
    step = columns_of(width)
    for c in range(0, width, step):
        cols = slice(c, c + step)
        total = hidden_ref[:, cols].astype(jnp.float32)
        for d in range(experts):
            if d:
                rows = rows_refs[d - 1][:, cols]
            else:
                rows = (own_ref[:, cols] + other_ref[:, cols].astype(jnp.float32)).astype(jnp.bfloat16)
            total += weight_ref[:, d : d + 1] * dot(placed[d], rows)
        out_ref[:, cols] = total.astype(jnp.bfloat16)


def body(hidden, lengths, norm_gain, w_gate, w_up, w_down, expert_ids, gate_weights):
    tokens_here, width = hidden.shape
    topk = expert_ids.shape[1]
    ranks = lax.axis_size("ep")
    experts = ranks // SPLIT
    capacity = SPLIT * ((3 * tokens_here * topk + 2 * experts * SPLIT - 1) // (2 * experts * SPLIT))
    capacity = -(-capacity // 16) * 16
    ff = w_gate.shape[-1]
    plane = (lax.axis_index("ep") // SPLIT).astype(jnp.int32).reshape(1)

    swap_core = [(i, i ^ 1) for i in range(ranks)]
    swap_side = [(i, i ^ 2) for i in range(ranks)]

    def shift(d):
        return [(i, (i + SPLIT * d) % ranks) for i in range(ranks)]

    def struct(rows, cols, dtype):
        return jax.ShapeDtypeStruct((rows, cols), dtype)

    lines = max(8, -(-experts // 8) * 8)
    block = struct(capacity, width, jnp.bfloat16)
    *packed, slot, weight = pl.pallas_call(
        functools.partial(pack_kernel, experts, capacity),
        out_shape=[block] * experts + [struct(tokens_here, lines, jnp.float32)] * 2,
        in_specs=[SMEM, SMEM, VMEM, VMEM, VMEM, VMEM],
        out_specs=[VMEM] * (experts + 2),
        compiler_params=pltpu.CompilerParams(vmem_limit_bytes=VMEM_BYTES),
    )(plane, lengths, hidden, norm_gain, expert_ids.T, gate_weights.T)

    def after(value, *others):
        return lax.optimization_barrier((value, *others))[0]

    params = dict(
        compiler_params=pltpu.CompilerParams(vmem_limit_bytes=32 << 20),
        cost_estimate=pl.CostEstimate(flops=1, bytes_accessed=1, transcendentals=0),
    )

    def expert(*operands):
        return pl.pallas_call(
            functools.partial(expert_kernel, len(operands) > 8),
            out_shape=[struct(capacity, width, jnp.float32), block],
            in_specs=[VMEM] * len(operands),
            out_specs=[VMEM, VMEM],
            **params,
        )(*operands)

    def first(*operands):
        return pl.pallas_call(
            first_kernel,
            out_shape=struct(capacity, width, jnp.float32),
            in_specs=[VMEM] * 4,
            out_specs=VMEM,
            **params,
        )(*operands)

    def across(rows):
        return lax.ppermute(rows, "ep", swap_side)

    order = [2, 1, 3] if experts == 4 else list(range(1, experts))
    count = len(order)
    theirs = across(packed[0])
    arrived = [lax.ppermute(packed[order[0]], "ep", shift(order[0]))]
    own_weights = (w_gate[0], w_up[0], w_down[0])
    weights = own_weights + tuple(lax.ppermute(after(w, packed[0]), "ep", swap_core) for w in own_weights)

    def send_along(i, *tied):
        arrived.append(lax.ppermute(after(packed[order[i]], *tied), "ep", shift(order[i])))

    own_here, sent_here = expert(packed[0], theirs, *weights, first(packed[0], *own_weights))
    other_here = across(sent_here)
    crossed = [across(after(arrived[0], sent_here))]
    if count > 1:
        send_along(1, arrived[0], sent_here)
    own, sent, other, rows, back = [], [], [], [], {}

    def send_back(i, *tied):
        rows.append((own[i] + after(other[i], *tied).astype(jnp.float32)).astype(jnp.bfloat16))
        back[order[i]] = lax.ppermute(rows[i], "ep", shift(experts - order[i]))

    for i in range(count):
        tied = [] if i else [other_here]
        if i > 1:
            tied.append(rows[i - 2])
        if i + 1 < count:
            crossed.append(across(after(arrived[i + 1], sent[i - 1] if i else other_here)))
            tied.append(arrived[i + 1])
        if i + 2 < count:
            send_along(i + 2, arrived[i + 1])
        mine_sum, their_part = expert(arrived[i], after(crossed[i], *tied), *weights)
        own.append(mine_sum)
        sent.append(their_part)
        if i:
            send_back(i - 1, sent[i])
        other.append(across(after(sent[i], rows[i - 1]) if i else sent[i]))
    send_back(count - 1, *(back[d] for d in order[:-2]))
    back[0] = (own_here, other_here)
    return pl.pallas_call(
        functools.partial(mix_kernel, experts, capacity),
        out_shape=struct(tokens_here, width, jnp.bfloat16),
        in_specs=[VMEM] * (experts + 4),
        out_specs=VMEM,
        compiler_params=pltpu.CompilerParams(vmem_limit_bytes=16 << 20),
    )(hidden, slot, weight, *back[0], *(back[d] for d in range(1, experts)))


def solution(mesh):
    return jax.shard_map(
        body,
        mesh=mesh,
        in_specs=(
            P(("group", "ep"), None),
            P(("group", "ep")),
            P(),
            P("ep", None, None),
            P("ep", None, None),
            P("ep", None, None),
            P(("group", "ep"), None),
            P(("group", "ep"), None),
        ),
        out_specs=P(("group", "ep"), None),
        check_vma=False,
    )
```

time: 113 us -> 87 us (0.77)
  waiting for transfers between devices: 69.9 us -> 50.2 us
  Pallas kernels: 17.8 us -> 13.2 us
  local copies, waits for them, and re-layouts: 8.44 us -> 5.52 us
  starting transfers between devices: 15.6 us -> 17.5 us
    ppermute x17, waiting for transfers between devices: 69.9 us -> 50.2 us  [the longest x8 26.1 us: across(): return lax.ppermute(rows, 'ep', swap_side)]
    pallas_call x4 -> x5, Pallas kernels: 15.1 us -> 8.95 us  [the longest x4 7.81 us: expert(): pl.pallas_call(functools.partial(expert_kernel, len(operands) > 8), out_s...]
    unnamed x16 -> x24, local copies, waits for them, and re-layouts: 7.71 us -> 5.52 us
    ppermute x17, starting transfers between devices: 15.6 us -> 17.5 us  [the longest x8 9.36 us: across(): return lax.ppermute(rows, 'ep', swap_side)]
    pallas_call x1, Pallas kernels: 1.33 us -> 2.78 us  [body(): pl.pallas_call(functools.partial(pack_kernel, experts, capacity), out_sha...]
  transfers between devices with their start and end apart: 17 -> 17, of which waited for: 10 -> 10; matrix products, arithmetic and copies ran while one was open for 2% -> 0% of each run, Pallas kernels for 15% -> 10%
where the time goes in v3:
time: 87 us; the launch traced here: 86.7 us
  waiting for transfers between devices  50.2 us (58%)
  starting transfers between devices  17.5 us (20%)
  Pallas kernels  13.2 us (15%)
  local copies, waits for them, and re-layouts  5.52 us (6%)
    ppermute x8, waiting for transfers between devices, across(): return lax.ppermute(rows, 'ep', swap_side)  26.1 us
    ppermute x8, starting transfers between devices, across(): return lax.ppermute(rows, 'ep', swap_side)  9.36 us
    ppermute x2, waiting for transfers between devices, send_along(): lax.ppermute(after(packed[order[i]], *tied), 'ep', shift(order[i]))  9.14 us
    ppermute x3, waiting for transfers between devices, send_back(): back[order[i]] = lax.ppermute(rows[i], 'ep', shift(experts - order[i]))  9.04 us
    pallas_call x4, Pallas kernels, expert(): pl.pallas_call(functools.partial(expert_kernel, len(operands) > 8), out_s...  7.81 us
    ppermute x1, waiting for transfers between devices, body(): arrived = [lax.ppermute(packed[order[0]], 'ep', shift(order[0]))]  5.9 us
    unnamed x24, local copies, waits for them, and re-layouts  5.52 us
    pallas_call x1, Pallas kernels, body(): pl.pallas_call(functools.partial(pack_kernel, experts, capacity), out_sha...  2.78 us
  transfers between devices with their start and end apart: 17, of which 10 were waited for; matrix products, arithmetic and copies ran while one was open for 0% of the time, Pallas kernels for 10%

profile of v3, /device:TPU:0, one launch (start us, length us, event | category | flops | bytes accessed | tf_op | source)
XLA Modules:
  0.0 86.7 jit_solution(1876421129941834942)
XLA Ops:
  0.0 2.8 %shard_map.82 = (bf16[48,3584]{1,0:T(8,128)(2,1)}, bf16[48,3584]{1,0:T(8,128)(2,1)}, bf16[48,3584]{1,0:T(8,128)(2,1)}, bf16[48,3584]{1,0:T(8,128)(2,1)}, f32[64,8]{1,0:T(8,128)}, /*index=5*/f32[64,8]{1,0:T(8,128)}) custom-call(s32[1]{0:T(128)} %bitcast.plane_ref, s32[2]{0:T(128)} %lengths_ref.1, bf16[64,3584]{1,0:T(8,128)(2,1)} %hidden_ref.3, ...), custom_call_target="tpu_custom_call" | custom-call | tf_op jit(solution)/shard_map/pallas_call | solution.py:132
  2.8 0.5 collective-permute-start.1
  3.2 0.1 collective-permute-start.2
  3.3 0.4 collective-permute-start.3
  3.8 2.6 %collective-permute-start = (bf16[48,3584]{1,0:T(8,128)(2,1)}, bf16[48,3584]{1,0:T(8,128)(2,1)S(1)}, u32[]{:S(2)}, u32[]{:S(2)}) collective-permute-start(bf16[48,3584]{1,0:T(8,128)(2,1)} %get-tuple-element.37.rows_ref.mine_ref), channel_id=1, source_target_pairs={{0,2},{1,3},{2,0},{3,1},{4,6},{5,7},{6,4},{7,5},{8,10},{9,11},{10,... | collective-permute-start | bytes 1032200 | tf_op jit(solution)/shard_map/ppermute | solution.py:167
  6.3 2.6 %collective-permute-start.5 = (bf16[48,3584]{1,0:T(8,128)(2,1)}, bf16[48,3584]{1,0:T(8,128)(2,1)S(1)}, u32[]{:S(2)}, u32[]{:S(2)}) collective-permute-start(bf16[48,3584]{1,0:T(8,128)(2,1)} %get-tuple-element.44), channel_id=1, source_target_pairs={{0,8},{1,9},{2,10},{3,11},{4,12},{5,13},{6,14},{7,15},{8,0},{9,1},... | collective-permute-start | bytes 1032200 | tf_op jit(solution)/shard_map/ppermute | solution.py:172
  8.9 1.5 %copy-done = bf16[1,3584,256]{2,1,0:T(8,128)(2,1)S(1)} copy-done((bf16[1,3584,256]{2,1,0:T(8,128)(2,1)S(1)}, bf16[1,3584,256]{2,1,0:T(8,128)(2,1)}, u32[]{:S(2)}) %copy-start) | copy-done | bytes 1835032
  10.4 1.5 %copy-done.2 = bf16[1,3584,256]{2,1,0:T(8,128)(2,1)S(1)} copy-done((bf16[1,3584,256]{2,1,0:T(8,128)(2,1)S(1)}, bf16[1,3584,256]{2,1,0:T(8,128)(2,1)}, u32[]{:S(2)}) %copy-start.2) | copy-done | bytes 1835032
  11.9 1.5 %copy-done.4 = bf16[1,256,3584]{2,1,0:T(8,128)(2,1)S(1)} copy-done((bf16[1,256,3584]{2,1,0:T(8,128)(2,1)S(1)}, bf16[1,256,3584]{2,1,0:T(8,128)(2,1)}, u32[]{:S(2)}) %copy-start.4) | copy-done | bytes 1835032
  13.4 1.0 %copy-done.7 = bf16[48,3584]{1,0:T(8,128)(2,1)S(1)} copy-done((bf16[48,3584]{1,0:T(8,128)(2,1)S(1)}, bf16[48,3584]{1,0:T(8,128)(2,1)}, u32[]{:S(2)}) %copy-start.7) | copy-done | bytes 344088
  14.4 1.1 %shard_map.83.refs_6_ = f32[48,3584]{1,0:T(8,128)S(1)} custom-call(bf16[48,3584]{1,0:T(8,128)(2,1)S(1)} %copy-done.7, bf16[3584,256]{1,0:T(8,128)(2,1)S(1)} %bitcast.7, bf16[3584,256]{1,0:T(8,128)(2,1)S(1)} %bitcast.13, bf16[256,3584]{1,0:T(8,128)(2,1)S(1)} %bitcast.19), custom_call_target="tpu_custom_call" | custom-call | flops 1 | bytes 1 | tf_op jit(solution)/shard_map/pallas_call | solution.py:158
  15.5 0.0 copy-start.1
  15.6 0.0 copy-start.3
  15.6 0.0 copy-start.5
  15.6 0.0 collective-permute-done.theirs_ref
  15.6 0.0 collective-permute-done.2.refs_4_
  15.6 0.0 collective-permute-done.3.refs_5_
  15.6 2.0 %shard_map.84 = (f32[48,3584]{1,0:T(8,128)S(1)}, bf16[48,3584]{1,0:T(8,128)(2,1)S(1)}) custom-call(bf16[48,3584]{1,0:T(8,128)(2,1)S(1)} %copy-done.7, bf16[48,3584]{1,0:T(8,128)(2,1)S(1)} %collective-permute-done.theirs_ref, bf16[3584,256]{1,0:T(8,128)(2,1)S(1)} %bitcast.8, bf16[3584,256]{1,0:T(8,128)(2,1)S(1)} %bitcast.14, bf16[256,3584]{1,0:T(8,128)(2,1)S(1)} %bitcast.20, ...), custom_call_target="tpu_custom_call" | custom-call | flops 1 | bytes 1 | tf_op jit(solution)/shard_map/pallas_call | solution.py:149
  17.6 1.4 %collective-permute-start.4 = (bf16[48,3584]{1,0:T(8,128)(2,1)S(1)}, bf16[48,3584]{1,0:T(8,128)(2,1)S(1)}, u32[]{:S(2)}, u32[]{:S(2)}) collective-permute-start(bf16[48,3584]{1,0:T(8,128)(2,1)S(1)} %get-tuple-element.42), channel_id=1, source_target_pairs={{0,2},{1,3},{2,0},{3,1},{4,6},{5,7},{6,4},{7,5},{8,10},{9,11},{10,... | collective-permute-start | bytes 1032200 | tf_op jit(solution)/shard_map/ppermute | solution.py:167
  19.0 5.9 %collective-permute-done.5.mine_ref = bf16[48,3584]{1,0:T(8,128)(2,1)S(1)} collective-permute-done((bf16[48,3584]{1,0:T(8,128)(2,1)}, bf16[48,3584]{1,0:T(8,128)(2,1)S(1)}, u32[]{:S(2)}, u32[]{:S(2)}) %collective-permute-start.5) | collective-permute-done | bytes 344096 | tf_op jit(solution)/shard_map/ppermute | solution.py:172
  24.9 0.8 collective-permute-start.6
  25.7 0.5 collective-permute-start.9
  26.2 1.3 %collective-permute-done.4.other_ref = bf16[48,3584]{1,0:T(8,128)(2,1)S(1)} collective-permute-done((bf16[48,3584]{1,0:T(8,128)(2,1)S(1)}, bf16[48,3584]{1,0:T(8,128)(2,1)S(1)}, u32[]{:S(2)}, u32[]{:S(2)}) %collective-permute-start.4) | collective-permute-done | bytes 344096 | tf_op jit(solution)/shard_map/ppermute | solution.py:167
  27.6 9.1 %collective-permute-done.6.mine_ref = bf16[48,3584]{1,0:T(8,128)(2,1)S(1)} collective-permute-done((bf16[48,3584]{1,0:T(8,128)(2,1)S(1)}, bf16[48,3584]{1,0:T(8,128)(2,1)S(1)}, u32[]{:S(2)}, u32[]{:S(2)}) %collective-permute-start.6) | collective-permute-done | bytes 344096 | tf_op jit(solution)/shard_map/ppermute | solution.py:177
  36.7 0.5 collective-permute-start.7
  37.2 1.7 %collective-permute-start.8 = (bf16[48,3584]{1,0:T(8,128)(2,1)S(1)}, bf16[48,3584]{1,0:T(8,128)(2,1)S(1)}, u32[]{:S(2)}, u32[]{:S(2)}) collective-permute-start(bf16[48,3584]{1,0:T(8,128)(2,1)S(1)} %copy-done.10), channel_id=1, source_target_pairs={{0,12},{1,13},{2,14},{3,15},{4,0},{5,1},{6,2},{7,3},{8,4},{9,5},{1... | collective-permute-start | bytes 1032200 | tf_op jit(solution)/shard_map/ppermute | solution.py:177
  39.0 1.9 %shard_map.86 = (f32[48,3584]{1,0:T(8,128)S(1)}, bf16[48,3584]{1,0:T(8,128)(2,1)S(1)}) custom-call(bf16[48,3584]{1,0:T(8,128)(2,1)S(1)} %collective-permute-done.5.mine_ref, bf16[48,3584]{1,0:T(8,128)(2,1)S(1)} %collective-permute-done.9.theirs_ref, bf16[3584,256]{1,0:T(8,128)(2,1)S(1)} %bitcast.9, bf16[3584,256]{1,0:T(8,128)(2,1)S(1)} %bitcast.15, ...), custom_call_target="tpu_custom_call" | custom-call | flops 1 | bytes 1 | tf_op jit(solution)/shard_map/pallas_call | solution.py:149
  40.9 1.6 %collective-permute-start.10 = (bf16[48,3584]{1,0:T(8,128)(2,1)S(1)}, bf16[48,3584]{1,0:T(8,128)(2,1)S(1)}, u32[]{:S(2)}, u32[]{:S(2)}) collective-permute-start(bf16[48,3584]{1,0:T(8,128)(2,1)S(1)} %get-tuple-element.55), channel_id=1, source_target_pairs={{0,2},{1,3},{2,0},{3,1},{4,6},{5,7},{6,4},{7,5},{8,10},{9,11},{10,... | collective-permute-start | bytes 1032200 | tf_op jit(solution)/shard_map/ppermute | solution.py:167
  42.5 5.2 %collective-permute-done.7.theirs_ref = bf16[48,3584]{1,0:T(8,128)(2,1)S(1)} collective-permute-done((bf16[48,3584]{1,0:T(8,128)(2,1)S(1)}, bf16[48,3584]{1,0:T(8,128)(2,1)S(1)}, u32[]{:S(2)}, u32[]{:S(2)}) %collective-permute-start.7) | collective-permute-done | bytes 344096 | tf_op jit(solution)/shard_map/ppermute | solution.py:167
  47.7 1.9 %shard_map.85 = (f32[48,3584]{1,0:T(8,128)S(1)}, bf16[48,3584]{1,0:T(8,128)(2,1)S(1)}) custom-call(bf16[48,3584]{1,0:T(8,128)(2,1)S(1)} %collective-permute-done.6.mine_ref, bf16[48,3584]{1,0:T(8,128)(2,1)S(1)} %collective-permute-done.7.theirs_ref, bf16[3584,256]{1,0:T(8,128)(2,1)S(1)} %bitcast.10, bf16[3584,256]{1,0:T(8,128)(2,1)S(1)} %bitcast.16, ...), custom_call_target="tpu_custom_call" | custom-call | flops 1 | bytes 1 | tf_op jit(solution)/shard_map/pallas_call | solution.py:149
  49.6 3.5 %collective-permute-done.10 = bf16[48,3584]{1,0:T(8,128)(2,1)S(1)} collective-permute-done((bf16[48,3584]{1,0:T(8,128)(2,1)S(1)}, bf16[48,3584]{1,0:T(8,128)(2,1)S(1)}, u32[]{:S(2)}, u32[]{:S(2)}) %collective-permute-start.10) | collective-permute-done | bytes 344096 | tf_op jit(solution)/shard_map/ppermute | solution.py:167
  53.2 0.6 collective-permute-start.12
  53.7 0.1 add_convert_fusion.2
  53.8 1.5 %collective-permute-start.11 = (bf16[48,3584]{1,0:T(8,128)(2,1)S(1)}, bf16[48,3584]{1,0:T(8,128)(2,1)S(1)}, u32[]{:S(2)}, u32[]{:S(2)}) collective-permute-start(bf16[48,3584]{1,0:T(8,128)(2,1)S(1)} %get-tuple-element.57), channel_id=1, source_target_pairs={{0,2},{1,3},{2,0},{3,1},{4,6},{5,7},{6,4},{7,5},{8,10},{9,11},{10,... | collective-permute-start | bytes 1032200 | tf_op jit(solution)/shard_map/ppermute | solution.py:167
  55.3 0.3 collective-permute-start.14
  55.6 8.5 %collective-permute-done.12.theirs_ref = bf16[48,3584]{1,0:T(8,128)(2,1)S(1)} collective-permute-done((bf16[48,3584]{1,0:T(8,128)(2,1)S(1)}, bf16[48,3584]{1,0:T(8,128)(2,1)S(1)}, u32[]{:S(2)}, u32[]{:S(2)}) %collective-permute-start.12) | collective-permute-done | bytes 344096 | tf_op jit(solution)/shard_map/ppermute | solution.py:167
  64.2 1.9 %shard_map.87 = (f32[48,3584]{1,0:T(8,128)S(1)}, bf16[48,3584]{1,0:T(8,128)(2,1)S(1)}) custom-call(bf16[48,3584]{1,0:T(8,128)(2,1)S(1)} %collective-permute-done.8.mine_ref, bf16[48,3584]{1,0:T(8,128)(2,1)S(1)} %collective-permute-done.12.theirs_ref, bf16[3584,256]{1,0:T(8,128)(2,1)S(1)} %bitcast.11, bf16[3584,256]{1,0:T(8,128)(2,1)S(1)} %bitcast.17, ...), custom_call_target="tpu_custom_call" | custom-call | flops 1 | bytes 1 | tf_op jit(solution)/shard_map/pallas_call | solution.py:149
  66.1 0.0 copy-start.6
  66.1 2.6 %collective-permute-done.11 = bf16[48,3584]{1,0:T(8,128)(2,1)S(1)} collective-permute-done((bf16[48,3584]{1,0:T(8,128)(2,1)S(1)}, bf16[48,3584]{1,0:T(8,128)(2,1)S(1)}, u32[]{:S(2)}, u32[]{:S(2)}) %collective-permute-start.11) | collective-permute-done | bytes 344096 | tf_op jit(solution)/shard_map/ppermute | solution.py:167
  68.7 0.1 add_convert_fusion.1
  68.8 0.7 collective-permute-start.15
  69.5 1.7 %collective-permute-start.13 = (bf16[48,3584]{1,0:T(8,128)(2,1)S(1)}, bf16[48,3584]{1,0:T(8,128)(2,1)S(1)}, u32[]{:S(2)}, u32[]{:S(2)}) collective-permute-start(bf16[48,3584]{1,0:T(8,128)(2,1)S(1)} %add_convert_fusion.1), channel_id=1, source_target_pairs={{0,12},{1,13},{2,14},{3,15},{4,0},{5,1},{6,2},{7,3},{8,4},{9,5},{1... | collective-permute-start | bytes 1032200 | tf_op jit(solution)/shard_map/ppermute | solution.py:188
  71.2 4.9 %collective-permute-done.15 = bf16[48,3584]{1,0:T(8,128)(2,1)S(1)} collective-permute-done((bf16[48,3584]{1,0:T(8,128)(2,1)S(1)}, bf16[48,3584]{1,0:T(8,128)(2,1)S(1)}, u32[]{:S(2)}, u32[]{:S(2)}) %collective-permute-start.15) | collective-permute-done | bytes 344096 | tf_op jit(solution)/shard_map/ppermute | solution.py:167
  76.1 0.1 add_convert_fusion
  76.2 0.1 collective-permute-start.16
  76.2 5.3 %collective-permute-done.13.refs_0_ = bf16[48,3584]{1,0:T(8,128)(2,1)S(1)} collective-permute-done((bf16[48,3584]{1,0:T(8,128)(2,1)S(1)}, bf16[48,3584]{1,0:T(8,128)(2,1)S(1)}, u32[]{:S(2)}, u32[]{:S(2)}) %collective-permute-start.13) | collective-permute-done | bytes 344096 | tf_op jit(solution)/shard_map/ppermute | solution.py:188
  81.5 3.8 %collective-permute-done.16.refs_2_ = bf16[48,3584]{1,0:T(8,128)(2,1)S(1)} collective-permute-done((bf16[48,3584]{1,0:T(8,128)(2,1)S(1)}, bf16[48,3584]{1,0:T(8,128)(2,1)S(1)}, u32[]{:S(2)}, u32[]{:S(2)}) %collective-permute-start.16) | collective-permute-done | bytes 344096 | tf_op jit(solution)/shard_map/ppermute | solution.py:188
  85.3 1.5 %shard_map.88 = bf16[64,3584]{1,0:T(8,128)(2,1)} custom-call(bf16[64,3584]{1,0:T(8,128)(2,1)S(1)} %copy-done.6, f32[64,8]{1,0:T(8,128)S(1)} %copy-done.8, f32[64,8]{1,0:T(8,128)S(1)} %copy-done.9, f32[48,3584]{1,0:T(8,128)S(1)} %get-tuple-element.41.own_ref, bf16[48,3584]{1,0:T(8,128)(2,1)S(1)} %collective-permute-done.4.other_ref, ...), custom_call_target="tpu_custom_call" | custom-call | tf_op jit(solution)/shard_map/pallas_call | solution.py:207
  (20 shorter events, 0.0 us)
Async XLA Ops:
  2.8 12.8 %collective-permute-start.1 = (bf16[3584,256]{1,0:T(8,128)(2,1)}, bf16[3584,256]{1,0:T(8,128)(2,1)S(1)}, u32[]{:S(2)}, u32[]{:S(2)}) collective-permute-start(bf16[3584,256]{1,0:T(8,128)(2,1)} %bitcast.6), channel_id=1, source_target_pairs={{0,1},{1,0},{2,3},{3,2},{4,5},{5,4},{6,7},{7,6},{8,9},{9,8},{10,11... | collective-permute-start | bytes 5505032 | tf_op jit(solution)/shard_map/ppermute | solution.py:174
  3.2 12.4 %collective-permute-start.2 = (bf16[3584,256]{1,0:T(8,128)(2,1)}, bf16[3584,256]{1,0:T(8,128)(2,1)S(1)}, u32[]{:S(2)}, u32[]{:S(2)}) collective-permute-start(bf16[3584,256]{1,0:T(8,128)(2,1)} %bitcast.12), channel_id=1, source_target_pairs={{0,1},{1,0},{2,3},{3,2},{4,5},{5,4},{6,7},{7,6},{8,9},{9,8},{10,11... | collective-permute-start | bytes 5505032 | tf_op jit(solution)/shard_map/ppermute | solution.py:174
  3.3 12.3 %collective-permute-start.3 = (bf16[256,3584]{1,0:T(8,128)(2,1)}, bf16[256,3584]{1,0:T(8,128)(2,1)S(1)}, u32[]{:S(2)}, u32[]{:S(2)}) collective-permute-start(bf16[256,3584]{1,0:T(8,128)(2,1)} %bitcast.18), channel_id=1, source_target_pairs={{0,1},{1,0},{2,3},{3,2},{4,5},{5,4},{6,7},{7,6},{8,9},{9,8},{10,11... | collective-permute-start | bytes 5505032 | tf_op jit(solution)/shard_map/ppermute | solution.py:174
  3.8 11.8 %collective-permute-start = (bf16[48,3584]{1,0:T(8,128)(2,1)}, bf16[48,3584]{1,0:T(8,128)(2,1)S(1)}, u32[]{:S(2)}, u32[]{:S(2)}) collective-permute-start(bf16[48,3584]{1,0:T(8,128)(2,1)} %get-tuple-element.37.rows_ref.mine_ref), channel_id=1, source_target_pairs={{0,2},{1,3},{2,0},{3,1},{4,6},{5,7},{6,4},{7,5},{8,10},{9,11},{10,... | collective-permute-start | bytes 1032200 | tf_op jit(solution)/shard_map/ppermute | solution.py:167
  6.3 18.6 %collective-permute-start.5 = (bf16[48,3584]{1,0:T(8,128)(2,1)}, bf16[48,3584]{1,0:T(8,128)(2,1)S(1)}, u32[]{:S(2)}, u32[]{:S(2)}) collective-permute-start(bf16[48,3584]{1,0:T(8,128)(2,1)} %get-tuple-element.44), channel_id=1, source_target_pairs={{0,8},{1,9},{2,10},{3,11},{4,12},{5,13},{6,14},{7,15},{8,0},{9,1},... | collective-permute-start | bytes 1032200 | tf_op jit(solution)/shard_map/ppermute | solution.py:172
  8.9 1.5 %copy-start = (bf16[1,3584,256]{2,1,0:T(8,128)(2,1)S(1)}, bf16[1,3584,256]{2,1,0:T(8,128)(2,1)}, u32[]{:S(2)}) copy-start(bf16[1,3584,256]{2,1,0:T(8,128)(2,1)} %param.11) | copy-start | bytes 5505028
  10.4 1.5 %copy-start.2 = (bf16[1,3584,256]{2,1,0:T(8,128)(2,1)S(1)}, bf16[1,3584,256]{2,1,0:T(8,128)(2,1)}, u32[]{:S(2)}) copy-start(bf16[1,3584,256]{2,1,0:T(8,128)(2,1)} %param.12) | copy-start | bytes 5505028
  11.9 1.5 %copy-start.4 = (bf16[1,256,3584]{2,1,0:T(8,128)(2,1)S(1)}, bf16[1,256,3584]{2,1,0:T(8,128)(2,1)}, u32[]{:S(2)}) copy-start(bf16[1,256,3584]{2,1,0:T(8,128)(2,1)} %param.13) | copy-start | bytes 5505028
  13.4 1.0 %copy-start.7 = (bf16[48,3584]{1,0:T(8,128)(2,1)S(1)}, bf16[48,3584]{1,0:T(8,128)(2,1)}, u32[]{:S(2)}) copy-start(bf16[48,3584]{1,0:T(8,128)(2,1)} %get-tuple-element.37.rows_ref.mine_ref) | copy-start | bytes 1032196
  15.5 9.4 %copy-start.11 = (bf16[48,3584]{1,0:T(8,128)(2,1)S(1)}, bf16[48,3584]{1,0:T(8,128)(2,1)}, u32[]{:S(2)}) copy-start(bf16[48,3584]{1,0:T(8,128)(2,1)} %get-tuple-element.45) | copy-start | bytes 1032196
  15.5 21.7 %copy-start.10 = (bf16[48,3584]{1,0:T(8,128)(2,1)S(1)}, bf16[48,3584]{1,0:T(8,128)(2,1)}, u32[]{:S(2)}) copy-start(bf16[48,3584]{1,0:T(8,128)(2,1)} %get-tuple-element.48) | copy-start | bytes 1032196
  15.5 23.4 %copy-start.1 = (bf16[1,3584,256]{2,1,0:T(8,128)(2,1)S(1)}, bf16[1,3584,256]{2,1,0:T(8,128)(2,1)}, u32[]{:S(2)}) copy-start(bf16[1,3584,256]{2,1,0:T(8,128)(2,1)} %param.11) | copy-start | bytes 5505028
  15.6 23.4 %copy-start.3 = (bf16[1,3584,256]{2,1,0:T(8,128)(2,1)S(1)}, bf16[1,3584,256]{2,1,0:T(8,128)(2,1)}, u32[]{:S(2)}) copy-start(bf16[1,3584,256]{2,1,0:T(8,128)(2,1)} %param.12) | copy-start | bytes 5505028
  15.6 23.4 %copy-start.5 = (bf16[1,256,3584]{2,1,0:T(8,128)(2,1)S(1)}, bf16[1,256,3584]{2,1,0:T(8,128)(2,1)}, u32[]{:S(2)}) copy-start(bf16[1,256,3584]{2,1,0:T(8,128)(2,1)} %param.13) | copy-start | bytes 5505028
  17.6 9.9 %collective-permute-start.4 = (bf16[48,3584]{1,0:T(8,128)(2,1)S(1)}, bf16[48,3584]{1,0:T(8,128)(2,1)S(1)}, u32[]{:S(2)}, u32[]{:S(2)}) collective-permute-start(bf16[48,3584]{1,0:T(8,128)(2,1)S(1)} %get-tuple-element.42), channel_id=1, source_target_pairs={{0,2},{1,3},{2,0},{3,1},{4,6},{5,7},{6,4},{7,5},{8,10},{9,11},{10,... | collective-permute-start | bytes 1032200 | tf_op jit(solution)/shard_map/ppermute | solution.py:167
  24.9 11.8 %collective-permute-start.6 = (bf16[48,3584]{1,0:T(8,128)(2,1)S(1)}, bf16[48,3584]{1,0:T(8,128)(2,1)S(1)}, u32[]{:S(2)}, u32[]{:S(2)}) collective-permute-start(bf16[48,3584]{1,0:T(8,128)(2,1)S(1)} %copy-done.11), channel_id=1, source_target_pairs={{0,4},{1,5},{2,6},{3,7},{4,8},{5,9},{6,10},{7,11},{8,12},{9,13},{1... | collective-permute-start | bytes 1032200 | tf_op jit(solution)/shard_map/ppermute | solution.py:177
  25.7 13.2 %collective-permute-start.9 = (bf16[48,3584]{1,0:T(8,128)(2,1)S(1)}, bf16[48,3584]{1,0:T(8,128)(2,1)S(1)}, u32[]{:S(2)}, u32[]{:S(2)}) collective-permute-start(bf16[48,3584]{1,0:T(8,128)(2,1)S(1)} %collective-permute-done.5.mine_ref), channel_id=1, source_target_pairs={{0,2},{1,3},{2,0},{3,1},{4,6},{5,7},{6,4},{7,5},{8,10},{9,11},{10,... | collective-permute-start | bytes 1032200 | tf_op jit(solution)/shard_map/ppermute | solution.py:167
  36.7 11.0 %collective-permute-start.7 = (bf16[48,3584]{1,0:T(8,128)(2,1)S(1)}, bf16[48,3584]{1,0:T(8,128)(2,1)S(1)}, u32[]{:S(2)}, u32[]{:S(2)}) collective-permute-start(bf16[48,3584]{1,0:T(8,128)(2,1)S(1)} %collective-permute-done.6.mine_ref), channel_id=1, source_target_pairs={{0,2},{1,3},{2,0},{3,1},{4,6},{5,7},{6,4},{7,5},{8,10},{9,11},{10,... | collective-permute-start | bytes 1032200 | tf_op jit(solution)/shard_map/ppermute | solution.py:167
  37.2 10.5 %collective-permute-start.8 = (bf16[48,3584]{1,0:T(8,128)(2,1)S(1)}, bf16[48,3584]{1,0:T(8,128)(2,1)S(1)}, u32[]{:S(2)}, u32[]{:S(2)}) collective-permute-start(bf16[48,3584]{1,0:T(8,128)(2,1)S(1)} %copy-done.10), channel_id=1, source_target_pairs={{0,12},{1,13},{2,14},{3,15},{4,0},{5,1},{6,2},{7,3},{8,4},{9,5},{1... | collective-permute-start | bytes 1032200 | tf_op jit(solution)/shard_map/ppermute | solution.py:177
  40.9 12.3 %collective-permute-start.10 = (bf16[48,3584]{1,0:T(8,128)(2,1)S(1)}, bf16[48,3584]{1,0:T(8,128)(2,1)S(1)}, u32[]{:S(2)}, u32[]{:S(2)}) collective-permute-start(bf16[48,3584]{1,0:T(8,128)(2,1)S(1)} %get-tuple-element.55), channel_id=1, source_target_pairs={{0,2},{1,3},{2,0},{3,1},{4,6},{5,7},{6,4},{7,5},{8,10},{9,11},{10,... | collective-permute-start | bytes 1032200 | tf_op jit(solution)/shard_map/ppermute | solution.py:167
  53.2 11.0 %collective-permute-start.12 = (bf16[48,3584]{1,0:T(8,128)(2,1)S(1)}, bf16[48,3584]{1,0:T(8,128)(2,1)S(1)}, u32[]{:S(2)}, u32[]{:S(2)}) collective-permute-start(bf16[48,3584]{1,0:T(8,128)(2,1)S(1)} %collective-permute-done.8.mine_ref), channel_id=1, source_target_pairs={{0,2},{1,3},{2,0},{3,1},{4,6},{5,7},{6,4},{7,5},{8,10},{9,11},{10,... | collective-permute-start | bytes 1032200 | tf_op jit(solution)/shard_map/ppermute | solution.py:167
  53.8 14.9 %collective-permute-start.11 = (bf16[48,3584]{1,0:T(8,128)(2,1)S(1)}, bf16[48,3584]{1,0:T(8,128)(2,1)S(1)}, u32[]{:S(2)}, u32[]{:S(2)}) collective-permute-start(bf16[48,3584]{1,0:T(8,128)(2,1)S(1)} %get-tuple-element.57), channel_id=1, source_target_pairs={{0,2},{1,3},{2,0},{3,1},{4,6},{5,7},{6,4},{7,5},{8,10},{9,11},{10,... | collective-permute-start | bytes 1032200 | tf_op jit(solution)/shard_map/ppermute | solution.py:167
  55.3 15.9 %collective-permute-start.14 = (bf16[48,3584]{1,0:T(8,128)(2,1)S(1)}, bf16[48,3584]{1,0:T(8,128)(2,1)S(1)}, u32[]{:S(2)}, u32[]{:S(2)}) collective-permute-start(bf16[48,3584]{1,0:T(8,128)(2,1)S(1)} %add_convert_fusion.2), channel_id=1, source_target_pairs={{0,8},{1,9},{2,10},{3,11},{4,12},{5,13},{6,14},{7,15},{8,0},{9,1},... | collective-permute-start | bytes 1032200 | tf_op jit(solution)/shard_map/ppermute | solution.py:188
  66.1 19.2 %copy-start.6 = (bf16[64,3584]{1,0:T(8,128)(2,1)S(1)}, bf16[64,3584]{1,0:T(8,128)(2,1)}, u32[]{:S(2)}) copy-start(bf16[64,3584]{1,0:T(8,128)(2,1)} %hidden_ref.3) | copy-start | bytes 1376260
  66.1 19.2 %copy-start.8 = (f32[64,8]{1,0:T(8,128)S(1)}, f32[64,8]{1,0:T(8,128)}, u32[]{:S(2)}) copy-start(f32[64,8]{1,0:T(8,128)} %get-tuple-element.35.slot_ref) | copy-start | bytes 6148
  66.1 19.1 %copy-start.9 = (f32[64,8]{1,0:T(8,128)S(1)}, f32[64,8]{1,0:T(8,128)}, u32[]{:S(2)}) copy-start(f32[64,8]{1,0:T(8,128)} %get-tuple-element.36.weight_ref) | copy-start | bytes 6148
  68.8 7.3 %collective-permute-start.15 = (bf16[48,3584]{1,0:T(8,128)(2,1)S(1)}, bf16[48,3584]{1,0:T(8,128)(2,1)S(1)}, u32[]{:S(2)}, u32[]{:S(2)}) collective-permute-start(bf16[48,3584]{1,0:T(8,128)(2,1)S(1)} %get-tuple-element.63), channel_id=1, source_target_pairs={{0,2},{1,3},{2,0},{3,1},{4,6},{5,7},{6,4},{7,5},{8,10},{9,11},{10,... | collective-permute-start | bytes 1032200 | tf_op jit(solution)/shard_map/ppermute | solution.py:167
  69.5 12.0 %collective-permute-start.13 = (bf16[48,3584]{1,0:T(8,128)(2,1)S(1)}, bf16[48,3584]{1,0:T(8,128)(2,1)S(1)}, u32[]{:S(2)}, u32[]{:S(2)}) collective-permute-start(bf16[48,3584]{1,0:T(8,128)(2,1)S(1)} %add_convert_fusion.1), channel_id=1, source_target_pairs={{0,12},{1,13},{2,14},{3,15},{4,0},{5,1},{6,2},{7,3},{8,4},{9,5},{1... | collective-permute-start | bytes 1032200 | tf_op jit(solution)/shard_map/ppermute | solution.py:188
  76.2 9.1 %collective-permute-start.16 = (bf16[48,3584]{1,0:T(8,128)(2,1)S(1)}, bf16[48,3584]{1,0:T(8,128)(2,1)S(1)}, u32[]{:S(2)}, u32[]{:S(2)}) collective-permute-start(bf16[48,3584]{1,0:T(8,128)(2,1)S(1)} %add_convert_fusion), channel_id=1, source_target_pairs={{0,4},{1,5},{2,6},{3,7},{4,8},{5,9},{6,10},{7,11},{8,12},{9,13},{1... | collective-permute-start | bytes 1032200 | tf_op jit(solution)/shard_map/ppermute | solution.py:188

commit v4 on v3

--- a/solution.py
+++ b/solution.py
@@ -178,9 +178,9 @@
 
     own_here, sent_here = expert(packed[0], theirs, *weights, first(packed[0], *own_weights))
     other_here = across(sent_here)
-    crossed = [across(after(arrived[0], sent_here))]
+    crossed = [across(after(arrived[0], other_here))]
     if count > 1:
-        send_along(1, arrived[0], sent_here)
+        send_along(1, arrived[0], other_here)
     own, sent, other, rows, back = [], [], [], [], {}
 
     def send_back(i, *tied):
@@ -201,7 +201,7 @@
         sent.append(their_part)
         if i:
             send_back(i - 1, sent[i])
-        other.append(across(after(sent[i], rows[i - 1]) if i else sent[i]))
+        other.append(across(after(sent[i], rows[i - 1]) if i > 1 else sent[i]))
     send_back(count - 1, *(back[d] for d in order[:-2]))
     back[0] = (own_here, other_here)
     return pl.pallas_call(

time: 87 us -> 86.9 us (level)
  waiting for transfers between devices: 50.2 us -> 49.1 us
  starting transfers between devices: 17.5 us -> 18.5 us
    ppermute x2, waiting for transfers between devices: 9.14 us -> 8.11 us  [send_along(): lax.ppermute(after(packed[order[i]], *tied), 'ep', shift(order[i]))]
where the time goes in v4:
time: 86.9 us; the launch traced here: 86.7 us
  waiting for transfers between devices  49.1 us (57%)
  starting transfers between devices  18.5 us (21%)
  Pallas kernels  13.2 us (15%)
  local copies, waits for them, and re-layouts  5.52 us (6%)
    ppermute x8, waiting for transfers between devices, across(): return lax.ppermute(rows, 'ep', swap_side)  26 us
    ppermute x8, starting transfers between devices, across(): return lax.ppermute(rows, 'ep', swap_side)  9.64 us
    ppermute x3, waiting for transfers between devices, send_back(): back[order[i]] = lax.ppermute(rows[i], 'ep', shift(experts - order[i]))  9.13 us
    ppermute x2, waiting for transfers between devices, send_along(): lax.ppermute(after(packed[order[i]], *tied), 'ep', shift(order[i]))  8.11 us
    pallas_call x4, Pallas kernels, expert(): pl.pallas_call(functools.partial(expert_kernel, len(operands) > 8), out_s...  7.81 us
    ppermute x1, waiting for transfers between devices, body(): arrived = [lax.ppermute(packed[order[0]], 'ep', shift(order[0]))]  5.9 us
    unnamed x24, local copies, waits for them, and re-layouts  5.52 us
    ppermute x2, starting transfers between devices, send_along(): lax.ppermute(after(packed[order[i]], *tied), 'ep', shift(order[i]))  3.32 us
  transfers between devices with their start and end apart: 17, of which 10 were waited for; matrix products, arithmetic and copies ran while one was open for 0% of the time, Pallas kernels for 10%

profile of v4, /device:TPU:0, one launch (start us, length us, event | category | flops | bytes accessed | tf_op | source)
XLA Modules:
  0.0 86.7 jit_solution(10405257397458747535)
XLA Ops:
  0.0 2.8 %shard_map.82 = (bf16[48,3584]{1,0:T(8,128)(2,1)}, bf16[48,3584]{1,0:T(8,128)(2,1)}, bf16[48,3584]{1,0:T(8,128)(2,1)}, bf16[48,3584]{1,0:T(8,128)(2,1)}, f32[64,8]{1,0:T(8,128)}, /*index=5*/f32[64,8]{1,0:T(8,128)}) custom-call(s32[1]{0:T(128)} %bitcast.plane_ref, s32[2]{0:T(128)} %lengths_ref.1, bf16[64,3584]{1,0:T(8,128)(2,1)} %hidden_ref.3, ...), custom_call_target="tpu_custom_call" | custom-call | tf_op jit(solution)/shard_map/pallas_call | solution.py:132
  2.8 0.5 collective-permute-start.1
  3.2 0.1 collective-permute-start.2
  3.3 0.4 collective-permute-start.3
  3.8 2.6 %collective-permute-start = (bf16[48,3584]{1,0:T(8,128)(2,1)}, bf16[48,3584]{1,0:T(8,128)(2,1)S(1)}, u32[]{:S(2)}, u32[]{:S(2)}) collective-permute-start(bf16[48,3584]{1,0:T(8,128)(2,1)} %get-tuple-element.36.rows_ref.mine_ref), channel_id=1, source_target_pairs={{0,2},{1,3},{2,0},{3,1},{4,6},{5,7},{6,4},{7,5},{8,10},{9,11},{10,... | collective-permute-start | bytes 1032200 | tf_op jit(solution)/shard_map/ppermute | solution.py:167
  6.3 2.6 %collective-permute-start.5 = (bf16[48,3584]{1,0:T(8,128)(2,1)}, bf16[48,3584]{1,0:T(8,128)(2,1)S(1)}, u32[]{:S(2)}, u32[]{:S(2)}) collective-permute-start(bf16[48,3584]{1,0:T(8,128)(2,1)} %get-tuple-element.43), channel_id=1, source_target_pairs={{0,8},{1,9},{2,10},{3,11},{4,12},{5,13},{6,14},{7,15},{8,0},{9,1},... | collective-permute-start | bytes 1032200 | tf_op jit(solution)/shard_map/ppermute | solution.py:172
  8.9 1.5 %copy-done = bf16[1,3584,256]{2,1,0:T(8,128)(2,1)S(1)} copy-done((bf16[1,3584,256]{2,1,0:T(8,128)(2,1)S(1)}, bf16[1,3584,256]{2,1,0:T(8,128)(2,1)}, u32[]{:S(2)}) %copy-start) | copy-done | bytes 1835032
  10.4 1.5 %copy-done.2 = bf16[1,3584,256]{2,1,0:T(8,128)(2,1)S(1)} copy-done((bf16[1,3584,256]{2,1,0:T(8,128)(2,1)S(1)}, bf16[1,3584,256]{2,1,0:T(8,128)(2,1)}, u32[]{:S(2)}) %copy-start.2) | copy-done | bytes 1835032
  11.9 1.5 %copy-done.4 = bf16[1,256,3584]{2,1,0:T(8,128)(2,1)S(1)} copy-done((bf16[1,256,3584]{2,1,0:T(8,128)(2,1)S(1)}, bf16[1,256,3584]{2,1,0:T(8,128)(2,1)}, u32[]{:S(2)}) %copy-start.4) | copy-done | bytes 1835032
  13.4 1.0 %copy-done.7 = bf16[48,3584]{1,0:T(8,128)(2,1)S(1)} copy-done((bf16[48,3584]{1,0:T(8,128)(2,1)S(1)}, bf16[48,3584]{1,0:T(8,128)(2,1)}, u32[]{:S(2)}) %copy-start.7) | copy-done | bytes 344088
  14.4 1.1 %shard_map.83.refs_6_ = f32[48,3584]{1,0:T(8,128)S(1)} custom-call(bf16[48,3584]{1,0:T(8,128)(2,1)S(1)} %copy-done.7, bf16[3584,256]{1,0:T(8,128)(2,1)S(1)} %bitcast.7, bf16[3584,256]{1,0:T(8,128)(2,1)S(1)} %bitcast.13, bf16[256,3584]{1,0:T(8,128)(2,1)S(1)} %bitcast.19), custom_call_target="tpu_custom_call" | custom-call | flops 1 | bytes 1 | tf_op jit(solution)/shard_map/pallas_call | solution.py:158
  15.5 0.0 copy-start.1
  15.6 0.0 copy-start.3
  15.6 0.0 copy-start.5
  15.6 0.0 collective-permute-done.theirs_ref
  15.6 0.0 collective-permute-done.1.refs_3_
  15.6 2.0 %shard_map.84 = (f32[48,3584]{1,0:T(8,128)S(1)}, bf16[48,3584]{1,0:T(8,128)(2,1)S(1)}) custom-call(bf16[48,3584]{1,0:T(8,128)(2,1)S(1)} %copy-done.7, bf16[48,3584]{1,0:T(8,128)(2,1)S(1)} %collective-permute-done.theirs_ref, bf16[3584,256]{1,0:T(8,128)(2,1)S(1)} %bitcast.8, bf16[3584,256]{1,0:T(8,128)(2,1)S(1)} %bitcast.14, bf16[256,3584]{1,0:T(8,128)(2,1)S(1)} %bitcast.20, ...), custom_call_target="tpu_custom_call" | custom-call | flops 1 | bytes 1 | tf_op jit(solution)/shard_map/pallas_call | solution.py:149
  17.6 1.4 %collective-permute-start.4 = (bf16[48,3584]{1,0:T(8,128)(2,1)S(1)}, bf16[48,3584]{1,0:T(8,128)(2,1)S(1)}, u32[]{:S(2)}, u32[]{:S(2)}) collective-permute-start(bf16[48,3584]{1,0:T(8,128)(2,1)S(1)} %get-tuple-element.41), channel_id=1, source_target_pairs={{0,2},{1,3},{2,0},{3,1},{4,6},{5,7},{6,4},{7,5},{8,10},{9,11},{10,... | collective-permute-start | bytes 1032200 | tf_op jit(solution)/shard_map/ppermute | solution.py:167
  19.0 5.9 %collective-permute-done.5.mine_ref = bf16[48,3584]{1,0:T(8,128)(2,1)S(1)} collective-permute-done((bf16[48,3584]{1,0:T(8,128)(2,1)}, bf16[48,3584]{1,0:T(8,128)(2,1)S(1)}, u32[]{:S(2)}, u32[]{:S(2)}) %collective-permute-start.5) | collective-permute-done | bytes 344096 | tf_op jit(solution)/shard_map/ppermute | solution.py:172
  24.9 2.6 %collective-permute-done.4.other_ref = bf16[48,3584]{1,0:T(8,128)(2,1)S(1)} collective-permute-done((bf16[48,3584]{1,0:T(8,128)(2,1)S(1)}, bf16[48,3584]{1,0:T(8,128)(2,1)S(1)}, u32[]{:S(2)}, u32[]{:S(2)}) %collective-permute-start.4) | collective-permute-done | bytes 344096 | tf_op jit(solution)/shard_map/ppermute | solution.py:167
  27.6 1.6 %collective-permute-start.6 = (bf16[48,3584]{1,0:T(8,128)(2,1)S(1)}, bf16[48,3584]{1,0:T(8,128)(2,1)S(1)}, u32[]{:S(2)}, u32[]{:S(2)}) collective-permute-start(bf16[48,3584]{1,0:T(8,128)(2,1)S(1)} %copy-done.11), channel_id=1, source_target_pairs={{0,4},{1,5},{2,6},{3,7},{4,8},{5,9},{6,10},{7,11},{8,12},{9,13},{1... | collective-permute-start | bytes 1032200 | tf_op jit(solution)/shard_map/ppermute | solution.py:177
  29.1 1.1 %collective-permute-start.10 = (bf16[48,3584]{1,0:T(8,128)(2,1)S(1)}, bf16[48,3584]{1,0:T(8,128)(2,1)S(1)}, u32[]{:S(2)}, u32[]{:S(2)}) collective-permute-start(bf16[48,3584]{1,0:T(8,128)(2,1)S(1)} %collective-permute-done.5.mine_ref), channel_id=1, source_target_pairs={{0,2},{1,3},{2,0},{3,1},{4,6},{5,7},{6,4},{7,5},{8,10},{9,11},{10,... | collective-permute-start | bytes 1032200 | tf_op jit(solution)/shard_map/ppermute | solution.py:167
  30.2 8.1 %collective-permute-done.6.mine_ref = bf16[48,3584]{1,0:T(8,128)(2,1)S(1)} collective-permute-done((bf16[48,3584]{1,0:T(8,128)(2,1)S(1)}, bf16[48,3584]{1,0:T(8,128)(2,1)S(1)}, u32[]{:S(2)}, u32[]{:S(2)}) %collective-permute-start.6) | collective-permute-done | bytes 344096 | tf_op jit(solution)/shard_map/ppermute | solution.py:177
  38.3 0.9 %collective-permute-start.7 = (bf16[48,3584]{1,0:T(8,128)(2,1)S(1)}, bf16[48,3584]{1,0:T(8,128)(2,1)S(1)}, u32[]{:S(2)}, u32[]{:S(2)}) collective-permute-start(bf16[48,3584]{1,0:T(8,128)(2,1)S(1)} %collective-permute-done.6.mine_ref), channel_id=1, source_target_pairs={{0,2},{1,3},{2,0},{3,1},{4,6},{5,7},{6,4},{7,5},{8,10},{9,11},{10,... | collective-permute-start | bytes 1032200 | tf_op jit(solution)/shard_map/ppermute | solution.py:167
  39.3 1.7 %collective-permute-start.8 = (bf16[48,3584]{1,0:T(8,128)(2,1)S(1)}, bf16[48,3584]{1,0:T(8,128)(2,1)S(1)}, u32[]{:S(2)}, u32[]{:S(2)}) collective-permute-start(bf16[48,3584]{1,0:T(8,128)(2,1)S(1)} %copy-done.10), channel_id=1, source_target_pairs={{0,12},{1,13},{2,14},{3,15},{4,0},{5,1},{6,2},{7,3},{8,4},{9,5},{1... | collective-permute-start | bytes 1032200 | tf_op jit(solution)/shard_map/ppermute | solution.py:177
  41.0 1.9 %shard_map.86 = (f32[48,3584]{1,0:T(8,128)S(1)}, bf16[48,3584]{1,0:T(8,128)(2,1)S(1)}) custom-call(bf16[48,3584]{1,0:T(8,128)(2,1)S(1)} %collective-permute-done.5.mine_ref, bf16[48,3584]{1,0:T(8,128)(2,1)S(1)} %collective-permute-done.10.theirs_ref, bf16[3584,256]{1,0:T(8,128)(2,1)S(1)} %bitcast.9, bf16[3584,256]{1,0:T(8,128)(2,1)S(1)} %bitcast.15, ...), custom_call_target="tpu_custom_call" | custom-call | flops 1 | bytes 1 | tf_op jit(solution)/shard_map/pallas_call | solution.py:149
  43.0 0.6 collective-permute-start.12
  43.5 5.8 %collective-permute-done.7.theirs_ref = bf16[48,3584]{1,0:T(8,128)(2,1)S(1)} collective-permute-done((bf16[48,3584]{1,0:T(8,128)(2,1)S(1)}, bf16[48,3584]{1,0:T(8,128)(2,1)S(1)}, u32[]{:S(2)}, u32[]{:S(2)}) %collective-permute-start.7) | collective-permute-done | bytes 344096 | tf_op jit(solution)/shard_map/ppermute | solution.py:167
  49.3 0.0 collective-permute-done.8.mine_ref
  49.3 0.9 %collective-permute-start.11 = (bf16[48,3584]{1,0:T(8,128)(2,1)S(1)}, bf16[48,3584]{1,0:T(8,128)(2,1)S(1)}, u32[]{:S(2)}, u32[]{:S(2)}) collective-permute-start(bf16[48,3584]{1,0:T(8,128)(2,1)S(1)} %collective-permute-done.8.mine_ref), channel_id=1, source_target_pairs={{0,2},{1,3},{2,0},{3,1},{4,6},{5,7},{6,4},{7,5},{8,10},{9,11},{10,... | collective-permute-start | bytes 1032200 | tf_op jit(solution)/shard_map/ppermute | solution.py:167
  50.3 1.9 %shard_map.85 = (f32[48,3584]{1,0:T(8,128)S(1)}, bf16[48,3584]{1,0:T(8,128)(2,1)S(1)}) custom-call(bf16[48,3584]{1,0:T(8,128)(2,1)S(1)} %collective-permute-done.6.mine_ref, bf16[48,3584]{1,0:T(8,128)(2,1)S(1)} %collective-permute-done.7.theirs_ref, bf16[3584,256]{1,0:T(8,128)(2,1)S(1)} %bitcast.10, bf16[3584,256]{1,0:T(8,128)(2,1)S(1)} %bitcast.16, ...), custom_call_target="tpu_custom_call" | custom-call | flops 1 | bytes 1 | tf_op jit(solution)/shard_map/pallas_call | solution.py:149
  52.2 1.2 %collective-permute-start.9 = (bf16[48,3584]{1,0:T(8,128)(2,1)S(1)}, bf16[48,3584]{1,0:T(8,128)(2,1)S(1)}, u32[]{:S(2)}, u32[]{:S(2)}) collective-permute-start(bf16[48,3584]{1,0:T(8,128)(2,1)S(1)} %get-tuple-element.50), channel_id=1, source_target_pairs={{0,2},{1,3},{2,0},{3,1},{4,6},{5,7},{6,4},{7,5},{8,10},{9,11},{10,... | collective-permute-start | bytes 1032200 | tf_op jit(solution)/shard_map/ppermute | solution.py:167
  53.4 3.3 %collective-permute-done.12 = bf16[48,3584]{1,0:T(8,128)(2,1)S(1)} collective-permute-done((bf16[48,3584]{1,0:T(8,128)(2,1)S(1)}, bf16[48,3584]{1,0:T(8,128)(2,1)S(1)}, u32[]{:S(2)}, u32[]{:S(2)}) %collective-permute-start.12) | collective-permute-done | bytes 344096 | tf_op jit(solution)/shard_map/ppermute | solution.py:167
  56.7 0.1 add_convert_fusion.2
  56.8 0.2 collective-permute-start.14
  57.0 7.1 %collective-permute-done.11.theirs_ref = bf16[48,3584]{1,0:T(8,128)(2,1)S(1)} collective-permute-done((bf16[48,3584]{1,0:T(8,128)(2,1)S(1)}, bf16[48,3584]{1,0:T(8,128)(2,1)S(1)}, u32[]{:S(2)}, u32[]{:S(2)}) %collective-permute-start.11) | collective-permute-done | bytes 344096 | tf_op jit(solution)/shard_map/ppermute | solution.py:167
  64.1 1.9 %shard_map.87 = (f32[48,3584]{1,0:T(8,128)S(1)}, bf16[48,3584]{1,0:T(8,128)(2,1)S(1)}) custom-call(bf16[48,3584]{1,0:T(8,128)(2,1)S(1)} %collective-permute-done.8.mine_ref, bf16[48,3584]{1,0:T(8,128)(2,1)S(1)} %collective-permute-done.11.theirs_ref, bf16[3584,256]{1,0:T(8,128)(2,1)S(1)} %bitcast.11, bf16[3584,256]{1,0:T(8,128)(2,1)S(1)} %bitcast.17, ...), custom_call_target="tpu_custom_call" | custom-call | flops 1 | bytes 1 | tf_op jit(solution)/shard_map/pallas_call | solution.py:149
  66.0 0.0 copy-start.6
  66.1 2.5 %collective-permute-done.9 = bf16[48,3584]{1,0:T(8,128)(2,1)S(1)} collective-permute-done((bf16[48,3584]{1,0:T(8,128)(2,1)S(1)}, bf16[48,3584]{1,0:T(8,128)(2,1)S(1)}, u32[]{:S(2)}, u32[]{:S(2)}) %collective-permute-start.9) | collective-permute-done | bytes 344096 | tf_op jit(solution)/shard_map/ppermute | solution.py:167
  68.6 0.1 add_convert_fusion.1
  68.6 1.0 %collective-permute-start.15 = (bf16[48,3584]{1,0:T(8,128)(2,1)S(1)}, bf16[48,3584]{1,0:T(8,128)(2,1)S(1)}, u32[]{:S(2)}, u32[]{:S(2)}) collective-permute-start(bf16[48,3584]{1,0:T(8,128)(2,1)S(1)} %get-tuple-element.61), channel_id=1, source_target_pairs={{0,2},{1,3},{2,0},{3,1},{4,6},{5,7},{6,4},{7,5},{8,10},{9,11},{10,... | collective-permute-start | bytes 1032200 | tf_op jit(solution)/shard_map/ppermute | solution.py:167
  69.6 1.7 %collective-permute-start.13 = (bf16[48,3584]{1,0:T(8,128)(2,1)S(1)}, bf16[48,3584]{1,0:T(8,128)(2,1)S(1)}, u32[]{:S(2)}, u32[]{:S(2)}) collective-permute-start(bf16[48,3584]{1,0:T(8,128)(2,1)S(1)} %add_convert_fusion.1), channel_id=1, source_target_pairs={{0,12},{1,13},{2,14},{3,15},{4,0},{5,1},{6,2},{7,3},{8,4},{9,5},{1... | collective-permute-start | bytes 1032200 | tf_op jit(solution)/shard_map/ppermute | solution.py:188
  71.3 4.6 %collective-permute-done.15 = bf16[48,3584]{1,0:T(8,128)(2,1)S(1)} collective-permute-done((bf16[48,3584]{1,0:T(8,128)(2,1)S(1)}, bf16[48,3584]{1,0:T(8,128)(2,1)S(1)}, u32[]{:S(2)}, u32[]{:S(2)}) %collective-permute-start.15) | collective-permute-done | bytes 344096 | tf_op jit(solution)/shard_map/ppermute | solution.py:167
  75.9 0.1 add_convert_fusion
  76.0 0.1 collective-permute-start.16
  76.1 3.5 %collective-permute-done.13.refs_0_ = bf16[48,3584]{1,0:T(8,128)(2,1)S(1)} collective-permute-done((bf16[48,3584]{1,0:T(8,128)(2,1)S(1)}, bf16[48,3584]{1,0:T(8,128)(2,1)S(1)}, u32[]{:S(2)}, u32[]{:S(2)}) %collective-permute-start.13) | collective-permute-done | bytes 344096 | tf_op jit(solution)/shard_map/ppermute | solution.py:188
  79.5 5.6 %collective-permute-done.16.refs_2_ = bf16[48,3584]{1,0:T(8,128)(2,1)S(1)} collective-permute-done((bf16[48,3584]{1,0:T(8,128)(2,1)S(1)}, bf16[48,3584]{1,0:T(8,128)(2,1)S(1)}, u32[]{:S(2)}, u32[]{:S(2)}) %collective-permute-start.16) | collective-permute-done | bytes 344096 | tf_op jit(solution)/shard_map/ppermute | solution.py:188
  85.2 1.5 %shard_map.88 = bf16[64,3584]{1,0:T(8,128)(2,1)} custom-call(bf16[64,3584]{1,0:T(8,128)(2,1)S(1)} %copy-done.6, f32[64,8]{1,0:T(8,128)S(1)} %copy-done.8, f32[64,8]{1,0:T(8,128)S(1)} %copy-done.9, f32[48,3584]{1,0:T(8,128)S(1)} %get-tuple-element.40.own_ref, bf16[48,3584]{1,0:T(8,128)(2,1)S(1)} %collective-permute-done.4.other_ref, ...), custom_call_target="tpu_custom_call" | custom-call | tf_op jit(solution)/shard_map/pallas_call | solution.py:207
  (20 shorter events, 0.0 us)
Async XLA Ops:
  2.8 12.8 %collective-permute-start.1 = (bf16[3584,256]{1,0:T(8,128)(2,1)}, bf16[3584,256]{1,0:T(8,128)(2,1)S(1)}, u32[]{:S(2)}, u32[]{:S(2)}) collective-permute-start(bf16[3584,256]{1,0:T(8,128)(2,1)} %bitcast.6), channel_id=1, source_target_pairs={{0,1},{1,0},{2,3},{3,2},{4,5},{5,4},{6,7},{7,6},{8,9},{9,8},{10,11... | collective-permute-start | bytes 5505032 | tf_op jit(solution)/shard_map/ppermute | solution.py:174
  3.2 12.4 %collective-permute-start.2 = (bf16[3584,256]{1,0:T(8,128)(2,1)}, bf16[3584,256]{1,0:T(8,128)(2,1)S(1)}, u32[]{:S(2)}, u32[]{:S(2)}) collective-permute-start(bf16[3584,256]{1,0:T(8,128)(2,1)} %bitcast.12), channel_id=1, source_target_pairs={{0,1},{1,0},{2,3},{3,2},{4,5},{5,4},{6,7},{7,6},{8,9},{9,8},{10,11... | collective-permute-start | bytes 5505032 | tf_op jit(solution)/shard_map/ppermute | solution.py:174
  3.3 12.3 %collective-permute-start.3 = (bf16[256,3584]{1,0:T(8,128)(2,1)}, bf16[256,3584]{1,0:T(8,128)(2,1)S(1)}, u32[]{:S(2)}, u32[]{:S(2)}) collective-permute-start(bf16[256,3584]{1,0:T(8,128)(2,1)} %bitcast.18), channel_id=1, source_target_pairs={{0,1},{1,0},{2,3},{3,2},{4,5},{5,4},{6,7},{7,6},{8,9},{9,8},{10,11... | collective-permute-start | bytes 5505032 | tf_op jit(solution)/shard_map/ppermute | solution.py:174
  3.8 11.8 %collective-permute-start = (bf16[48,3584]{1,0:T(8,128)(2,1)}, bf16[48,3584]{1,0:T(8,128)(2,1)S(1)}, u32[]{:S(2)}, u32[]{:S(2)}) collective-permute-start(bf16[48,3584]{1,0:T(8,128)(2,1)} %get-tuple-element.36.rows_ref.mine_ref), channel_id=1, source_target_pairs={{0,2},{1,3},{2,0},{3,1},{4,6},{5,7},{6,4},{7,5},{8,10},{9,11},{10,... | collective-permute-start | bytes 1032200 | tf_op jit(solution)/shard_map/ppermute | solution.py:167
  6.3 18.6 %collective-permute-start.5 = (bf16[48,3584]{1,0:T(8,128)(2,1)}, bf16[48,3584]{1,0:T(8,128)(2,1)S(1)}, u32[]{:S(2)}, u32[]{:S(2)}) collective-permute-start(bf16[48,3584]{1,0:T(8,128)(2,1)} %get-tuple-element.43), channel_id=1, source_target_pairs={{0,8},{1,9},{2,10},{3,11},{4,12},{5,13},{6,14},{7,15},{8,0},{9,1},... | collective-permute-start | bytes 1032200 | tf_op jit(solution)/shard_map/ppermute | solution.py:172
  8.9 1.5 %copy-start = (bf16[1,3584,256]{2,1,0:T(8,128)(2,1)S(1)}, bf16[1,3584,256]{2,1,0:T(8,128)(2,1)}, u32[]{:S(2)}) copy-start(bf16[1,3584,256]{2,1,0:T(8,128)(2,1)} %param.11) | copy-start | bytes 5505028
  10.4 1.5 %copy-start.2 = (bf16[1,3584,256]{2,1,0:T(8,128)(2,1)S(1)}, bf16[1,3584,256]{2,1,0:T(8,128)(2,1)}, u32[]{:S(2)}) copy-start(bf16[1,3584,256]{2,1,0:T(8,128)(2,1)} %param.12) | copy-start | bytes 5505028
  11.9 1.5 %copy-start.4 = (bf16[1,256,3584]{2,1,0:T(8,128)(2,1)S(1)}, bf16[1,256,3584]{2,1,0:T(8,128)(2,1)}, u32[]{:S(2)}) copy-start(bf16[1,256,3584]{2,1,0:T(8,128)(2,1)} %param.13) | copy-start | bytes 5505028
  13.4 1.0 %copy-start.7 = (bf16[48,3584]{1,0:T(8,128)(2,1)S(1)}, bf16[48,3584]{1,0:T(8,128)(2,1)}, u32[]{:S(2)}) copy-start(bf16[48,3584]{1,0:T(8,128)(2,1)} %get-tuple-element.36.rows_ref.mine_ref) | copy-start | bytes 1032196
  15.5 12.0 %copy-start.11 = (bf16[48,3584]{1,0:T(8,128)(2,1)S(1)}, bf16[48,3584]{1,0:T(8,128)(2,1)}, u32[]{:S(2)}) copy-start(bf16[48,3584]{1,0:T(8,128)(2,1)} %get-tuple-element.44) | copy-start | bytes 1032196
  15.5 23.7 %copy-start.10 = (bf16[48,3584]{1,0:T(8,128)(2,1)S(1)}, bf16[48,3584]{1,0:T(8,128)(2,1)}, u32[]{:S(2)}) copy-start(bf16[48,3584]{1,0:T(8,128)(2,1)} %get-tuple-element.47) | copy-start | bytes 1032196
  15.5 25.5 %copy-start.1 = (bf16[1,3584,256]{2,1,0:T(8,128)(2,1)S(1)}, bf16[1,3584,256]{2,1,0:T(8,128)(2,1)}, u32[]{:S(2)}) copy-start(bf16[1,3584,256]{2,1,0:T(8,128)(2,1)} %param.11) | copy-start | bytes 5505028
  15.6 25.5 %copy-start.3 = (bf16[1,3584,256]{2,1,0:T(8,128)(2,1)S(1)}, bf16[1,3584,256]{2,1,0:T(8,128)(2,1)}, u32[]{:S(2)}) copy-start(bf16[1,3584,256]{2,1,0:T(8,128)(2,1)} %param.12) | copy-start | bytes 5505028
  15.6 25.4 %copy-start.5 = (bf16[1,256,3584]{2,1,0:T(8,128)(2,1)S(1)}, bf16[1,256,3584]{2,1,0:T(8,128)(2,1)}, u32[]{:S(2)}) copy-start(bf16[1,256,3584]{2,1,0:T(8,128)(2,1)} %param.13) | copy-start | bytes 5505028
  17.6 9.9 %collective-permute-start.4 = (bf16[48,3584]{1,0:T(8,128)(2,1)S(1)}, bf16[48,3584]{1,0:T(8,128)(2,1)S(1)}, u32[]{:S(2)}, u32[]{:S(2)}) collective-permute-start(bf16[48,3584]{1,0:T(8,128)(2,1)S(1)} %get-tuple-element.41), channel_id=1, source_target_pairs={{0,2},{1,3},{2,0},{3,1},{4,6},{5,7},{6,4},{7,5},{8,10},{9,11},{10,... | collective-permute-start | bytes 1032200 | tf_op jit(solution)/shard_map/ppermute | solution.py:167
  27.6 10.8 %collective-permute-start.6 = (bf16[48,3584]{1,0:T(8,128)(2,1)S(1)}, bf16[48,3584]{1,0:T(8,128)(2,1)S(1)}, u32[]{:S(2)}, u32[]{:S(2)}) collective-permute-start(bf16[48,3584]{1,0:T(8,128)(2,1)S(1)} %copy-done.11), channel_id=1, source_target_pairs={{0,4},{1,5},{2,6},{3,7},{4,8},{5,9},{6,10},{7,11},{8,12},{9,13},{1... | collective-permute-start | bytes 1032200 | tf_op jit(solution)/shard_map/ppermute | solution.py:177
  29.1 11.9 %collective-permute-start.10 = (bf16[48,3584]{1,0:T(8,128)(2,1)S(1)}, bf16[48,3584]{1,0:T(8,128)(2,1)S(1)}, u32[]{:S(2)}, u32[]{:S(2)}) collective-permute-start(bf16[48,3584]{1,0:T(8,128)(2,1)S(1)} %collective-permute-done.5.mine_ref), channel_id=1, source_target_pairs={{0,2},{1,3},{2,0},{3,1},{4,6},{5,7},{6,4},{7,5},{8,10},{9,11},{10,... | collective-permute-start | bytes 1032200 | tf_op jit(solution)/shard_map/ppermute | solution.py:167
  38.3 11.0 %collective-permute-start.7 = (bf16[48,3584]{1,0:T(8,128)(2,1)S(1)}, bf16[48,3584]{1,0:T(8,128)(2,1)S(1)}, u32[]{:S(2)}, u32[]{:S(2)}) collective-permute-start(bf16[48,3584]{1,0:T(8,128)(2,1)S(1)} %collective-permute-done.6.mine_ref), channel_id=1, source_target_pairs={{0,2},{1,3},{2,0},{3,1},{4,6},{5,7},{6,4},{7,5},{8,10},{9,11},{10,... | collective-permute-start | bytes 1032200 | tf_op jit(solution)/shard_map/ppermute | solution.py:167
  39.3 10.1 %collective-permute-start.8 = (bf16[48,3584]{1,0:T(8,128)(2,1)S(1)}, bf16[48,3584]{1,0:T(8,128)(2,1)S(1)}, u32[]{:S(2)}, u32[]{:S(2)}) collective-permute-start(bf16[48,3584]{1,0:T(8,128)(2,1)S(1)} %copy-done.10), channel_id=1, source_target_pairs={{0,12},{1,13},{2,14},{3,15},{4,0},{5,1},{6,2},{7,3},{8,4},{9,5},{1... | collective-permute-start | bytes 1032200 | tf_op jit(solution)/shard_map/ppermute | solution.py:177
  43.0 13.8 %collective-permute-start.12 = (bf16[48,3584]{1,0:T(8,128)(2,1)S(1)}, bf16[48,3584]{1,0:T(8,128)(2,1)S(1)}, u32[]{:S(2)}, u32[]{:S(2)}) collective-permute-start(bf16[48,3584]{1,0:T(8,128)(2,1)S(1)} %get-tuple-element.53), channel_id=1, source_target_pairs={{0,2},{1,3},{2,0},{3,1},{4,6},{5,7},{6,4},{7,5},{8,10},{9,11},{10,... | collective-permute-start | bytes 1032200 | tf_op jit(solution)/shard_map/ppermute | solution.py:167
  49.3 14.7 %collective-permute-start.11 = (bf16[48,3584]{1,0:T(8,128)(2,1)S(1)}, bf16[48,3584]{1,0:T(8,128)(2,1)S(1)}, u32[]{:S(2)}, u32[]{:S(2)}) collective-permute-start(bf16[48,3584]{1,0:T(8,128)(2,1)S(1)} %collective-permute-done.8.mine_ref), channel_id=1, source_target_pairs={{0,2},{1,3},{2,0},{3,1},{4,6},{5,7},{6,4},{7,5},{8,10},{9,11},{10,... | collective-permute-start | bytes 1032200 | tf_op jit(solution)/shard_map/ppermute | solution.py:167
  52.2 16.4 %collective-permute-start.9 = (bf16[48,3584]{1,0:T(8,128)(2,1)S(1)}, bf16[48,3584]{1,0:T(8,128)(2,1)S(1)}, u32[]{:S(2)}, u32[]{:S(2)}) collective-permute-start(bf16[48,3584]{1,0:T(8,128)(2,1)S(1)} %get-tuple-element.50), channel_id=1, source_target_pairs={{0,2},{1,3},{2,0},{3,1},{4,6},{5,7},{6,4},{7,5},{8,10},{9,11},{10,... | collective-permute-start | bytes 1032200 | tf_op jit(solution)/shard_map/ppermute | solution.py:167
  56.8 14.6 %collective-permute-start.14 = (bf16[48,3584]{1,0:T(8,128)(2,1)S(1)}, bf16[48,3584]{1,0:T(8,128)(2,1)S(1)}, u32[]{:S(2)}, u32[]{:S(2)}) collective-permute-start(bf16[48,3584]{1,0:T(8,128)(2,1)S(1)} %add_convert_fusion.2), channel_id=1, source_target_pairs={{0,8},{1,9},{2,10},{3,11},{4,12},{5,13},{6,14},{7,15},{8,0},{9,1},... | collective-permute-start | bytes 1032200 | tf_op jit(solution)/shard_map/ppermute | solution.py:188
  66.0 19.2 %copy-start.6 = (bf16[64,3584]{1,0:T(8,128)(2,1)S(1)}, bf16[64,3584]{1,0:T(8,128)(2,1)}, u32[]{:S(2)}) copy-start(bf16[64,3584]{1,0:T(8,128)(2,1)} %hidden_ref.3) | copy-start | bytes 1376260
  66.0 19.2 %copy-start.8 = (f32[64,8]{1,0:T(8,128)S(1)}, f32[64,8]{1,0:T(8,128)}, u32[]{:S(2)}) copy-start(f32[64,8]{1,0:T(8,128)} %get-tuple-element.34.slot_ref) | copy-start | bytes 6148
  66.0 19.2 %copy-start.9 = (f32[64,8]{1,0:T(8,128)S(1)}, f32[64,8]{1,0:T(8,128)}, u32[]{:S(2)}) copy-start(f32[64,8]{1,0:T(8,128)} %get-tuple-element.35.weight_ref) | copy-start | bytes 6148
  68.6 7.3 %collective-permute-start.15 = (bf16[48,3584]{1,0:T(8,128)(2,1)S(1)}, bf16[48,3584]{1,0:T(8,128)(2,1)S(1)}, u32[]{:S(2)}, u32[]{:S(2)}) collective-permute-start(bf16[48,3584]{1,0:T(8,128)(2,1)S(1)} %get-tuple-element.61), channel_id=1, source_target_pairs={{0,2},{1,3},{2,0},{3,1},{4,6},{5,7},{6,4},{7,5},{8,10},{9,11},{10,... | collective-permute-start | bytes 1032200 | tf_op jit(solution)/shard_map/ppermute | solution.py:167
  69.6 9.9 %collective-permute-start.13 = (bf16[48,3584]{1,0:T(8,128)(2,1)S(1)}, bf16[48,3584]{1,0:T(8,128)(2,1)S(1)}, u32[]{:S(2)}, u32[]{:S(2)}) collective-permute-start(bf16[48,3584]{1,0:T(8,128)(2,1)S(1)} %add_convert_fusion.1), channel_id=1, source_target_pairs={{0,12},{1,13},{2,14},{3,15},{4,0},{5,1},{6,2},{7,3},{8,4},{9,5},{1... | collective-permute-start | bytes 1032200 | tf_op jit(solution)/shard_map/ppermute | solution.py:188
  76.0 9.2 %collective-permute-start.16 = (bf16[48,3584]{1,0:T(8,128)(2,1)S(1)}, bf16[48,3584]{1,0:T(8,128)(2,1)S(1)}, u32[]{:S(2)}, u32[]{:S(2)}) collective-permute-start(bf16[48,3584]{1,0:T(8,128)(2,1)S(1)} %add_convert_fusion), channel_id=1, source_target_pairs={{0,4},{1,5},{2,6},{3,7},{4,8},{5,9},{6,10},{7,11},{8,12},{9,13},{1... | collective-permute-start | bytes 1032200 | tf_op jit(solution)/shard_map/ppermute | solution.py:188

commit v5 on v4

--- a/solution.py
+++ b/solution.py
@@ -19,7 +19,7 @@
 
 
 def columns_of(width):
-    return next(c for c in (512, 256, 128, width) if width % c == 0)
+    return next(c for c in (1792, 512, 256, 128, width) if width % c == 0)
 
 
 def pack_kernel(experts, capacity, plane_ref, lengths_ref, hidden_ref, gain_ref, ids_ref, gates_ref, *outs):

time: 86.9 us -> 87 us (level)
  no operation moved by 1% of the time
where the time goes in v5:
time: 87 us; the launch traced here: 86.7 us
  waiting for transfers between devices  49.3 us (57%)
  starting transfers between devices  18.5 us (21%)
  Pallas kernels  13.1 us (15%)
  local copies, waits for them, and re-layouts  5.52 us (6%)
    ppermute x8, waiting for transfers between devices, across(): return lax.ppermute(rows, 'ep', swap_side)  26.2 us
    ppermute x8, starting transfers between devices, across(): return lax.ppermute(rows, 'ep', swap_side)  9.65 us
    ppermute x3, waiting for transfers between devices, send_back(): back[order[i]] = lax.ppermute(rows[i], 'ep', shift(experts - order[i]))  9.12 us
    ppermute x2, waiting for transfers between devices, send_along(): lax.ppermute(after(packed[order[i]], *tied), 'ep', shift(order[i]))  8.1 us
    pallas_call x4, Pallas kernels, expert(): pl.pallas_call(functools.partial(expert_kernel, len(operands) > 8), out_s...  7.65 us
    ppermute x1, waiting for transfers between devices, body(): arrived = [lax.ppermute(packed[order[0]], 'ep', shift(order[0]))]  5.88 us
    unnamed x24, local copies, waits for them, and re-layouts  5.52 us
    ppermute x2, starting transfers between devices, send_along(): lax.ppermute(after(packed[order[i]], *tied), 'ep', shift(order[i]))  3.32 us
  transfers between devices with their start and end apart: 17, of which 10 were waited for; matrix products, arithmetic and copies ran while one was open for 0% of the time, Pallas kernels for 10%

profile of v5, /device:TPU:0, one launch (start us, length us, event | category | flops | bytes accessed | tf_op | source)
XLA Modules:
  0.0 86.7 jit_solution(16531434955697516982)
XLA Ops:
  0.0 2.8 %shard_map.82 = (bf16[48,3584]{1,0:T(8,128)(2,1)}, bf16[48,3584]{1,0:T(8,128)(2,1)}, bf16[48,3584]{1,0:T(8,128)(2,1)}, bf16[48,3584]{1,0:T(8,128)(2,1)}, f32[64,8]{1,0:T(8,128)}, /*index=5*/f32[64,8]{1,0:T(8,128)}) custom-call(s32[1]{0:T(128)} %bitcast.plane_ref, s32[2]{0:T(128)} %lengths_ref.1, bf16[64,3584]{1,0:T(8,128)(2,1)} %hidden_ref.3, ...), custom_call_target="tpu_custom_call" | custom-call | tf_op jit(solution)/shard_map/pallas_call | solution.py:132
  2.8 0.5 collective-permute-start.1
  3.2 0.1 collective-permute-start.2
  3.3 0.4 collective-permute-start.3
  3.8 2.6 %collective-permute-start = (bf16[48,3584]{1,0:T(8,128)(2,1)}, bf16[48,3584]{1,0:T(8,128)(2,1)S(1)}, u32[]{:S(2)}, u32[]{:S(2)}) collective-permute-start(bf16[48,3584]{1,0:T(8,128)(2,1)} %get-tuple-element.36.rows_ref.mine_ref), channel_id=1, source_target_pairs={{0,2},{1,3},{2,0},{3,1},{4,6},{5,7},{6,4},{7,5},{8,10},{9,11},{10,... | collective-permute-start | bytes 1032200 | tf_op jit(solution)/shard_map/ppermute | solution.py:167
  6.3 2.6 %collective-permute-start.5 = (bf16[48,3584]{1,0:T(8,128)(2,1)}, bf16[48,3584]{1,0:T(8,128)(2,1)S(1)}, u32[]{:S(2)}, u32[]{:S(2)}) collective-permute-start(bf16[48,3584]{1,0:T(8,128)(2,1)} %get-tuple-element.43), channel_id=1, source_target_pairs={{0,8},{1,9},{2,10},{3,11},{4,12},{5,13},{6,14},{7,15},{8,0},{9,1},... | collective-permute-start | bytes 1032200 | tf_op jit(solution)/shard_map/ppermute | solution.py:172
  8.9 1.5 %copy-done = bf16[1,3584,256]{2,1,0:T(8,128)(2,1)S(1)} copy-done((bf16[1,3584,256]{2,1,0:T(8,128)(2,1)S(1)}, bf16[1,3584,256]{2,1,0:T(8,128)(2,1)}, u32[]{:S(2)}) %copy-start) | copy-done | bytes 1835032
  10.4 1.5 %copy-done.2 = bf16[1,3584,256]{2,1,0:T(8,128)(2,1)S(1)} copy-done((bf16[1,3584,256]{2,1,0:T(8,128)(2,1)S(1)}, bf16[1,3584,256]{2,1,0:T(8,128)(2,1)}, u32[]{:S(2)}) %copy-start.2) | copy-done | bytes 1835032
  11.9 1.5 %copy-done.4 = bf16[1,256,3584]{2,1,0:T(8,128)(2,1)S(1)} copy-done((bf16[1,256,3584]{2,1,0:T(8,128)(2,1)S(1)}, bf16[1,256,3584]{2,1,0:T(8,128)(2,1)}, u32[]{:S(2)}) %copy-start.4) | copy-done | bytes 1835032
  13.4 1.0 %copy-done.7 = bf16[48,3584]{1,0:T(8,128)(2,1)S(1)} copy-done((bf16[48,3584]{1,0:T(8,128)(2,1)S(1)}, bf16[48,3584]{1,0:T(8,128)(2,1)}, u32[]{:S(2)}) %copy-start.7) | copy-done | bytes 344088
  14.4 1.1 %shard_map.83.refs_6_ = f32[48,3584]{1,0:T(8,128)S(1)} custom-call(bf16[48,3584]{1,0:T(8,128)(2,1)S(1)} %copy-done.7, bf16[3584,256]{1,0:T(8,128)(2,1)S(1)} %bitcast.7, bf16[3584,256]{1,0:T(8,128)(2,1)S(1)} %bitcast.13, bf16[256,3584]{1,0:T(8,128)(2,1)S(1)} %bitcast.19), custom_call_target="tpu_custom_call" | custom-call | flops 1 | bytes 1 | tf_op jit(solution)/shard_map/pallas_call | solution.py:158
  15.5 0.0 copy-start.1
  15.6 0.0 copy-start.3
  15.6 0.0 copy-start.5
  15.6 0.0 collective-permute-done.1.refs_3_
  15.6 0.0 collective-permute-done.2.refs_4_
  15.6 2.0 %shard_map.84 = (f32[48,3584]{1,0:T(8,128)S(1)}, bf16[48,3584]{1,0:T(8,128)(2,1)S(1)}) custom-call(bf16[48,3584]{1,0:T(8,128)(2,1)S(1)} %copy-done.7, bf16[48,3584]{1,0:T(8,128)(2,1)S(1)} %collective-permute-done.theirs_ref, bf16[3584,256]{1,0:T(8,128)(2,1)S(1)} %bitcast.8, bf16[3584,256]{1,0:T(8,128)(2,1)S(1)} %bitcast.14, bf16[256,3584]{1,0:T(8,128)(2,1)S(1)} %bitcast.20, ...), custom_call_target="tpu_custom_call" | custom-call | flops 1 | bytes 1 | tf_op jit(solution)/shard_map/pallas_call | solution.py:149
  17.7 1.4 %collective-permute-start.4 = (bf16[48,3584]{1,0:T(8,128)(2,1)S(1)}, bf16[48,3584]{1,0:T(8,128)(2,1)S(1)}, u32[]{:S(2)}, u32[]{:S(2)}) collective-permute-start(bf16[48,3584]{1,0:T(8,128)(2,1)S(1)} %get-tuple-element.41), channel_id=1, source_target_pairs={{0,2},{1,3},{2,0},{3,1},{4,6},{5,7},{6,4},{7,5},{8,10},{9,11},{10,... | collective-permute-start | bytes 1032200 | tf_op jit(solution)/shard_map/ppermute | solution.py:167
  19.1 5.9 %collective-permute-done.5.mine_ref = bf16[48,3584]{1,0:T(8,128)(2,1)S(1)} collective-permute-done((bf16[48,3584]{1,0:T(8,128)(2,1)}, bf16[48,3584]{1,0:T(8,128)(2,1)S(1)}, u32[]{:S(2)}, u32[]{:S(2)}) %collective-permute-start.5) | collective-permute-done | bytes 344096 | tf_op jit(solution)/shard_map/ppermute | solution.py:172
  24.9 2.6 %collective-permute-done.4.other_ref = bf16[48,3584]{1,0:T(8,128)(2,1)S(1)} collective-permute-done((bf16[48,3584]{1,0:T(8,128)(2,1)S(1)}, bf16[48,3584]{1,0:T(8,128)(2,1)S(1)}, u32[]{:S(2)}, u32[]{:S(2)}) %collective-permute-start.4) | collective-permute-done | bytes 344096 | tf_op jit(solution)/shard_map/ppermute | solution.py:167
  27.6 1.6 %collective-permute-start.6 = (bf16[48,3584]{1,0:T(8,128)(2,1)S(1)}, bf16[48,3584]{1,0:T(8,128)(2,1)S(1)}, u32[]{:S(2)}, u32[]{:S(2)}) collective-permute-start(bf16[48,3584]{1,0:T(8,128)(2,1)S(1)} %copy-done.11), channel_id=1, source_target_pairs={{0,4},{1,5},{2,6},{3,7},{4,8},{5,9},{6,10},{7,11},{8,12},{9,13},{1... | collective-permute-start | bytes 1032200 | tf_op jit(solution)/shard_map/ppermute | solution.py:177
  29.2 1.1 %collective-permute-start.10 = (bf16[48,3584]{1,0:T(8,128)(2,1)S(1)}, bf16[48,3584]{1,0:T(8,128)(2,1)S(1)}, u32[]{:S(2)}, u32[]{:S(2)}) collective-permute-start(bf16[48,3584]{1,0:T(8,128)(2,1)S(1)} %collective-permute-done.5.mine_ref), channel_id=1, source_target_pairs={{0,2},{1,3},{2,0},{3,1},{4,6},{5,7},{6,4},{7,5},{8,10},{9,11},{10,... | collective-permute-start | bytes 1032200 | tf_op jit(solution)/shard_map/ppermute | solution.py:167
  30.3 8.1 %collective-permute-done.6.mine_ref = bf16[48,3584]{1,0:T(8,128)(2,1)S(1)} collective-permute-done((bf16[48,3584]{1,0:T(8,128)(2,1)S(1)}, bf16[48,3584]{1,0:T(8,128)(2,1)S(1)}, u32[]{:S(2)}, u32[]{:S(2)}) %collective-permute-start.6) | collective-permute-done | bytes 344096 | tf_op jit(solution)/shard_map/ppermute | solution.py:177
  38.4 0.9 %collective-permute-start.7 = (bf16[48,3584]{1,0:T(8,128)(2,1)S(1)}, bf16[48,3584]{1,0:T(8,128)(2,1)S(1)}, u32[]{:S(2)}, u32[]{:S(2)}) collective-permute-start(bf16[48,3584]{1,0:T(8,128)(2,1)S(1)} %collective-permute-done.6.mine_ref), channel_id=1, source_target_pairs={{0,2},{1,3},{2,0},{3,1},{4,6},{5,7},{6,4},{7,5},{8,10},{9,11},{10,... | collective-permute-start | bytes 1032200 | tf_op jit(solution)/shard_map/ppermute | solution.py:167
  39.3 1.7 %collective-permute-start.8 = (bf16[48,3584]{1,0:T(8,128)(2,1)S(1)}, bf16[48,3584]{1,0:T(8,128)(2,1)S(1)}, u32[]{:S(2)}, u32[]{:S(2)}) collective-permute-start(bf16[48,3584]{1,0:T(8,128)(2,1)S(1)} %copy-done.10), channel_id=1, source_target_pairs={{0,12},{1,13},{2,14},{3,15},{4,0},{5,1},{6,2},{7,3},{8,4},{9,5},{1... | collective-permute-start | bytes 1032200 | tf_op jit(solution)/shard_map/ppermute | solution.py:177
  41.0 0.0 collective-permute-done.10.theirs_ref
  41.0 1.9 %shard_map.86 = (f32[48,3584]{1,0:T(8,128)S(1)}, bf16[48,3584]{1,0:T(8,128)(2,1)S(1)}) custom-call(bf16[48,3584]{1,0:T(8,128)(2,1)S(1)} %collective-permute-done.5.mine_ref, bf16[48,3584]{1,0:T(8,128)(2,1)S(1)} %collective-permute-done.10.theirs_ref, bf16[3584,256]{1,0:T(8,128)(2,1)S(1)} %bitcast.9, bf16[3584,256]{1,0:T(8,128)(2,1)S(1)} %bitcast.15, ...), custom_call_target="tpu_custom_call" | custom-call | flops 1 | bytes 1 | tf_op jit(solution)/shard_map/pallas_call | solution.py:149
  42.9 0.6 collective-permute-start.12
  43.5 5.9 %collective-permute-done.7.theirs_ref = bf16[48,3584]{1,0:T(8,128)(2,1)S(1)} collective-permute-done((bf16[48,3584]{1,0:T(8,128)(2,1)S(1)}, bf16[48,3584]{1,0:T(8,128)(2,1)S(1)}, u32[]{:S(2)}, u32[]{:S(2)}) %collective-permute-start.7) | collective-permute-done | bytes 344096 | tf_op jit(solution)/shard_map/ppermute | solution.py:167
  49.4 0.9 %collective-permute-start.11 = (bf16[48,3584]{1,0:T(8,128)(2,1)S(1)}, bf16[48,3584]{1,0:T(8,128)(2,1)S(1)}, u32[]{:S(2)}, u32[]{:S(2)}) collective-permute-start(bf16[48,3584]{1,0:T(8,128)(2,1)S(1)} %collective-permute-done.8.mine_ref), channel_id=1, source_target_pairs={{0,2},{1,3},{2,0},{3,1},{4,6},{5,7},{6,4},{7,5},{8,10},{9,11},{10,... | collective-permute-start | bytes 1032200 | tf_op jit(solution)/shard_map/ppermute | solution.py:167
  50.3 1.9 %shard_map.85 = (f32[48,3584]{1,0:T(8,128)S(1)}, bf16[48,3584]{1,0:T(8,128)(2,1)S(1)}) custom-call(bf16[48,3584]{1,0:T(8,128)(2,1)S(1)} %collective-permute-done.6.mine_ref, bf16[48,3584]{1,0:T(8,128)(2,1)S(1)} %collective-permute-done.7.theirs_ref, bf16[3584,256]{1,0:T(8,128)(2,1)S(1)} %bitcast.10, bf16[3584,256]{1,0:T(8,128)(2,1)S(1)} %bitcast.16, ...), custom_call_target="tpu_custom_call" | custom-call | flops 1 | bytes 1 | tf_op jit(solution)/shard_map/pallas_call | solution.py:149
  52.2 1.2 %collective-permute-start.9 = (bf16[48,3584]{1,0:T(8,128)(2,1)S(1)}, bf16[48,3584]{1,0:T(8,128)(2,1)S(1)}, u32[]{:S(2)}, u32[]{:S(2)}) collective-permute-start(bf16[48,3584]{1,0:T(8,128)(2,1)S(1)} %get-tuple-element.50), channel_id=1, source_target_pairs={{0,2},{1,3},{2,0},{3,1},{4,6},{5,7},{6,4},{7,5},{8,10},{9,11},{10,... | collective-permute-start | bytes 1032200 | tf_op jit(solution)/shard_map/ppermute | solution.py:167
  53.3 3.4 %collective-permute-done.12 = bf16[48,3584]{1,0:T(8,128)(2,1)S(1)} collective-permute-done((bf16[48,3584]{1,0:T(8,128)(2,1)S(1)}, bf16[48,3584]{1,0:T(8,128)(2,1)S(1)}, u32[]{:S(2)}, u32[]{:S(2)}) %collective-permute-start.12) | collective-permute-done | bytes 344096 | tf_op jit(solution)/shard_map/ppermute | solution.py:167
  56.7 0.1 add_convert_fusion.2
  56.8 0.2 collective-permute-start.14
  57.0 7.1 %collective-permute-done.11.theirs_ref = bf16[48,3584]{1,0:T(8,128)(2,1)S(1)} collective-permute-done((bf16[48,3584]{1,0:T(8,128)(2,1)S(1)}, bf16[48,3584]{1,0:T(8,128)(2,1)S(1)}, u32[]{:S(2)}, u32[]{:S(2)}) %collective-permute-start.11) | collective-permute-done | bytes 344096 | tf_op jit(solution)/shard_map/ppermute | solution.py:167
  64.1 1.9 %shard_map.87 = (f32[48,3584]{1,0:T(8,128)S(1)}, bf16[48,3584]{1,0:T(8,128)(2,1)S(1)}) custom-call(bf16[48,3584]{1,0:T(8,128)(2,1)S(1)} %collective-permute-done.8.mine_ref, bf16[48,3584]{1,0:T(8,128)(2,1)S(1)} %collective-permute-done.11.theirs_ref, bf16[3584,256]{1,0:T(8,128)(2,1)S(1)} %bitcast.11, bf16[3584,256]{1,0:T(8,128)(2,1)S(1)} %bitcast.17, ...), custom_call_target="tpu_custom_call" | custom-call | flops 1 | bytes 1 | tf_op jit(solution)/shard_map/pallas_call | solution.py:149
  66.0 0.0 copy-start.6
  66.0 2.6 %collective-permute-done.9 = bf16[48,3584]{1,0:T(8,128)(2,1)S(1)} collective-permute-done((bf16[48,3584]{1,0:T(8,128)(2,1)S(1)}, bf16[48,3584]{1,0:T(8,128)(2,1)S(1)}, u32[]{:S(2)}, u32[]{:S(2)}) %collective-permute-start.9) | collective-permute-done | bytes 344096 | tf_op jit(solution)/shard_map/ppermute | solution.py:167
  68.6 0.1 add_convert_fusion.1
  68.6 1.0 %collective-permute-start.15 = (bf16[48,3584]{1,0:T(8,128)(2,1)S(1)}, bf16[48,3584]{1,0:T(8,128)(2,1)S(1)}, u32[]{:S(2)}, u32[]{:S(2)}) collective-permute-start(bf16[48,3584]{1,0:T(8,128)(2,1)S(1)} %get-tuple-element.61), channel_id=1, source_target_pairs={{0,2},{1,3},{2,0},{3,1},{4,6},{5,7},{6,4},{7,5},{8,10},{9,11},{10,... | collective-permute-start | bytes 1032200 | tf_op jit(solution)/shard_map/ppermute | solution.py:167
  69.6 1.7 %collective-permute-start.13 = (bf16[48,3584]{1,0:T(8,128)(2,1)S(1)}, bf16[48,3584]{1,0:T(8,128)(2,1)S(1)}, u32[]{:S(2)}, u32[]{:S(2)}) collective-permute-start(bf16[48,3584]{1,0:T(8,128)(2,1)S(1)} %add_convert_fusion.1), channel_id=1, source_target_pairs={{0,12},{1,13},{2,14},{3,15},{4,0},{5,1},{6,2},{7,3},{8,4},{9,5},{1... | collective-permute-start | bytes 1032200 | tf_op jit(solution)/shard_map/ppermute | solution.py:188
  71.4 4.6 %collective-permute-done.15 = bf16[48,3584]{1,0:T(8,128)(2,1)S(1)} collective-permute-done((bf16[48,3584]{1,0:T(8,128)(2,1)S(1)}, bf16[48,3584]{1,0:T(8,128)(2,1)S(1)}, u32[]{:S(2)}, u32[]{:S(2)}) %collective-permute-start.15) | collective-permute-done | bytes 344096 | tf_op jit(solution)/shard_map/ppermute | solution.py:167
  76.0 0.1 add_convert_fusion
  76.0 0.1 collective-permute-start.16
  76.1 3.5 %collective-permute-done.13.refs_0_ = bf16[48,3584]{1,0:T(8,128)(2,1)S(1)} collective-permute-done((bf16[48,3584]{1,0:T(8,128)(2,1)S(1)}, bf16[48,3584]{1,0:T(8,128)(2,1)S(1)}, u32[]{:S(2)}, u32[]{:S(2)}) %collective-permute-start.13) | collective-permute-done | bytes 344096 | tf_op jit(solution)/shard_map/ppermute | solution.py:188
  79.6 5.7 %collective-permute-done.16.refs_2_ = bf16[48,3584]{1,0:T(8,128)(2,1)S(1)} collective-permute-done((bf16[48,3584]{1,0:T(8,128)(2,1)S(1)}, bf16[48,3584]{1,0:T(8,128)(2,1)S(1)}, u32[]{:S(2)}, u32[]{:S(2)}) %collective-permute-start.16) | collective-permute-done | bytes 344096 | tf_op jit(solution)/shard_map/ppermute | solution.py:188
  85.2 1.5 %shard_map.88 = bf16[64,3584]{1,0:T(8,128)(2,1)} custom-call(bf16[64,3584]{1,0:T(8,128)(2,1)S(1)} %copy-done.6, f32[64,8]{1,0:T(8,128)S(1)} %copy-done.8, f32[64,8]{1,0:T(8,128)S(1)} %copy-done.9, f32[48,3584]{1,0:T(8,128)S(1)} %get-tuple-element.40.own_ref, bf16[48,3584]{1,0:T(8,128)(2,1)S(1)} %collective-permute-done.4.other_ref, ...), custom_call_target="tpu_custom_call" | custom-call | tf_op jit(solution)/shard_map/pallas_call | solution.py:207
  (20 shorter events, 0.0 us)
Async XLA Ops:
  2.8 12.8 %collective-permute-start.1 = (bf16[3584,256]{1,0:T(8,128)(2,1)}, bf16[3584,256]{1,0:T(8,128)(2,1)S(1)}, u32[]{:S(2)}, u32[]{:S(2)}) collective-permute-start(bf16[3584,256]{1,0:T(8,128)(2,1)} %bitcast.6), channel_id=1, source_target_pairs={{0,1},{1,0},{2,3},{3,2},{4,5},{5,4},{6,7},{7,6},{8,9},{9,8},{10,11... | collective-permute-start | bytes 5505032 | tf_op jit(solution)/shard_map/ppermute | solution.py:174
  3.2 12.4 %collective-permute-start.2 = (bf16[3584,256]{1,0:T(8,128)(2,1)}, bf16[3584,256]{1,0:T(8,128)(2,1)S(1)}, u32[]{:S(2)}, u32[]{:S(2)}) collective-permute-start(bf16[3584,256]{1,0:T(8,128)(2,1)} %bitcast.12), channel_id=1, source_target_pairs={{0,1},{1,0},{2,3},{3,2},{4,5},{5,4},{6,7},{7,6},{8,9},{9,8},{10,11... | collective-permute-start | bytes 5505032 | tf_op jit(solution)/shard_map/ppermute | solution.py:174
  3.3 12.3 %collective-permute-start.3 = (bf16[256,3584]{1,0:T(8,128)(2,1)}, bf16[256,3584]{1,0:T(8,128)(2,1)S(1)}, u32[]{:S(2)}, u32[]{:S(2)}) collective-permute-start(bf16[256,3584]{1,0:T(8,128)(2,1)} %bitcast.18), channel_id=1, source_target_pairs={{0,1},{1,0},{2,3},{3,2},{4,5},{5,4},{6,7},{7,6},{8,9},{9,8},{10,11... | collective-permute-start | bytes 5505032 | tf_op jit(solution)/shard_map/ppermute | solution.py:174
  3.8 11.8 %collective-permute-start = (bf16[48,3584]{1,0:T(8,128)(2,1)}, bf16[48,3584]{1,0:T(8,128)(2,1)S(1)}, u32[]{:S(2)}, u32[]{:S(2)}) collective-permute-start(bf16[48,3584]{1,0:T(8,128)(2,1)} %get-tuple-element.36.rows_ref.mine_ref), channel_id=1, source_target_pairs={{0,2},{1,3},{2,0},{3,1},{4,6},{5,7},{6,4},{7,5},{8,10},{9,11},{10,... | collective-permute-start | bytes 1032200 | tf_op jit(solution)/shard_map/ppermute | solution.py:167
  6.3 18.6 %collective-permute-start.5 = (bf16[48,3584]{1,0:T(8,128)(2,1)}, bf16[48,3584]{1,0:T(8,128)(2,1)S(1)}, u32[]{:S(2)}, u32[]{:S(2)}) collective-permute-start(bf16[48,3584]{1,0:T(8,128)(2,1)} %get-tuple-element.43), channel_id=1, source_target_pairs={{0,8},{1,9},{2,10},{3,11},{4,12},{5,13},{6,14},{7,15},{8,0},{9,1},... | collective-permute-start | bytes 1032200 | tf_op jit(solution)/shard_map/ppermute | solution.py:172
  8.9 1.5 %copy-start = (bf16[1,3584,256]{2,1,0:T(8,128)(2,1)S(1)}, bf16[1,3584,256]{2,1,0:T(8,128)(2,1)}, u32[]{:S(2)}) copy-start(bf16[1,3584,256]{2,1,0:T(8,128)(2,1)} %param.11) | copy-start | bytes 5505028
  10.4 1.5 %copy-start.2 = (bf16[1,3584,256]{2,1,0:T(8,128)(2,1)S(1)}, bf16[1,3584,256]{2,1,0:T(8,128)(2,1)}, u32[]{:S(2)}) copy-start(bf16[1,3584,256]{2,1,0:T(8,128)(2,1)} %param.12) | copy-start | bytes 5505028
  11.9 1.5 %copy-start.4 = (bf16[1,256,3584]{2,1,0:T(8,128)(2,1)S(1)}, bf16[1,256,3584]{2,1,0:T(8,128)(2,1)}, u32[]{:S(2)}) copy-start(bf16[1,256,3584]{2,1,0:T(8,128)(2,1)} %param.13) | copy-start | bytes 5505028
  13.4 1.0 %copy-start.7 = (bf16[48,3584]{1,0:T(8,128)(2,1)S(1)}, bf16[48,3584]{1,0:T(8,128)(2,1)}, u32[]{:S(2)}) copy-start(bf16[48,3584]{1,0:T(8,128)(2,1)} %get-tuple-element.36.rows_ref.mine_ref) | copy-start | bytes 1032196
  15.5 12.0 %copy-start.11 = (bf16[48,3584]{1,0:T(8,128)(2,1)S(1)}, bf16[48,3584]{1,0:T(8,128)(2,1)}, u32[]{:S(2)}) copy-start(bf16[48,3584]{1,0:T(8,128)(2,1)} %get-tuple-element.44) | copy-start | bytes 1032196
  15.5 23.7 %copy-start.10 = (bf16[48,3584]{1,0:T(8,128)(2,1)S(1)}, bf16[48,3584]{1,0:T(8,128)(2,1)}, u32[]{:S(2)}) copy-start(bf16[48,3584]{1,0:T(8,128)(2,1)} %get-tuple-element.47) | copy-start | bytes 1032196
  15.5 25.5 %copy-start.1 = (bf16[1,3584,256]{2,1,0:T(8,128)(2,1)S(1)}, bf16[1,3584,256]{2,1,0:T(8,128)(2,1)}, u32[]{:S(2)}) copy-start(bf16[1,3584,256]{2,1,0:T(8,128)(2,1)} %param.11) | copy-start | bytes 5505028
  15.6 25.5 %copy-start.3 = (bf16[1,3584,256]{2,1,0:T(8,128)(2,1)S(1)}, bf16[1,3584,256]{2,1,0:T(8,128)(2,1)}, u32[]{:S(2)}) copy-start(bf16[1,3584,256]{2,1,0:T(8,128)(2,1)} %param.12) | copy-start | bytes 5505028
  15.6 25.5 %copy-start.5 = (bf16[1,256,3584]{2,1,0:T(8,128)(2,1)S(1)}, bf16[1,256,3584]{2,1,0:T(8,128)(2,1)}, u32[]{:S(2)}) copy-start(bf16[1,256,3584]{2,1,0:T(8,128)(2,1)} %param.13) | copy-start | bytes 5505028
  17.7 9.9 %collective-permute-start.4 = (bf16[48,3584]{1,0:T(8,128)(2,1)S(1)}, bf16[48,3584]{1,0:T(8,128)(2,1)S(1)}, u32[]{:S(2)}, u32[]{:S(2)}) collective-permute-start(bf16[48,3584]{1,0:T(8,128)(2,1)S(1)} %get-tuple-element.41), channel_id=1, source_target_pairs={{0,2},{1,3},{2,0},{3,1},{4,6},{5,7},{6,4},{7,5},{8,10},{9,11},{10,... | collective-permute-start | bytes 1032200 | tf_op jit(solution)/shard_map/ppermute | solution.py:167
  27.6 10.8 %collective-permute-start.6 = (bf16[48,3584]{1,0:T(8,128)(2,1)S(1)}, bf16[48,3584]{1,0:T(8,128)(2,1)S(1)}, u32[]{:S(2)}, u32[]{:S(2)}) collective-permute-start(bf16[48,3584]{1,0:T(8,128)(2,1)S(1)} %copy-done.11), channel_id=1, source_target_pairs={{0,4},{1,5},{2,6},{3,7},{4,8},{5,9},{6,10},{7,11},{8,12},{9,13},{1... | collective-permute-start | bytes 1032200 | tf_op jit(solution)/shard_map/ppermute | solution.py:177
  29.2 11.9 %collective-permute-start.10 = (bf16[48,3584]{1,0:T(8,128)(2,1)S(1)}, bf16[48,3584]{1,0:T(8,128)(2,1)S(1)}, u32[]{:S(2)}, u32[]{:S(2)}) collective-permute-start(bf16[48,3584]{1,0:T(8,128)(2,1)S(1)} %collective-permute-done.5.mine_ref), channel_id=1, source_target_pairs={{0,2},{1,3},{2,0},{3,1},{4,6},{5,7},{6,4},{7,5},{8,10},{9,11},{10,... | collective-permute-start | bytes 1032200 | tf_op jit(solution)/shard_map/ppermute | solution.py:167
  38.4 11.0 %collective-permute-start.7 = (bf16[48,3584]{1,0:T(8,128)(2,1)S(1)}, bf16[48,3584]{1,0:T(8,128)(2,1)S(1)}, u32[]{:S(2)}, u32[]{:S(2)}) collective-permute-start(bf16[48,3584]{1,0:T(8,128)(2,1)S(1)} %collective-permute-done.6.mine_ref), channel_id=1, source_target_pairs={{0,2},{1,3},{2,0},{3,1},{4,6},{5,7},{6,4},{7,5},{8,10},{9,11},{10,... | collective-permute-start | bytes 1032200 | tf_op jit(solution)/shard_map/ppermute | solution.py:167
  39.3 10.1 %collective-permute-start.8 = (bf16[48,3584]{1,0:T(8,128)(2,1)S(1)}, bf16[48,3584]{1,0:T(8,128)(2,1)S(1)}, u32[]{:S(2)}, u32[]{:S(2)}) collective-permute-start(bf16[48,3584]{1,0:T(8,128)(2,1)S(1)} %copy-done.10), channel_id=1, source_target_pairs={{0,12},{1,13},{2,14},{3,15},{4,0},{5,1},{6,2},{7,3},{8,4},{9,5},{1... | collective-permute-start | bytes 1032200 | tf_op jit(solution)/shard_map/ppermute | solution.py:177
  42.9 13.8 %collective-permute-start.12 = (bf16[48,3584]{1,0:T(8,128)(2,1)S(1)}, bf16[48,3584]{1,0:T(8,128)(2,1)S(1)}, u32[]{:S(2)}, u32[]{:S(2)}) collective-permute-start(bf16[48,3584]{1,0:T(8,128)(2,1)S(1)} %get-tuple-element.53), channel_id=1, source_target_pairs={{0,2},{1,3},{2,0},{3,1},{4,6},{5,7},{6,4},{7,5},{8,10},{9,11},{10,... | collective-permute-start | bytes 1032200 | tf_op jit(solution)/shard_map/ppermute | solution.py:167
  49.4 14.7 %collective-permute-start.11 = (bf16[48,3584]{1,0:T(8,128)(2,1)S(1)}, bf16[48,3584]{1,0:T(8,128)(2,1)S(1)}, u32[]{:S(2)}, u32[]{:S(2)}) collective-permute-start(bf16[48,3584]{1,0:T(8,128)(2,1)S(1)} %collective-permute-done.8.mine_ref), channel_id=1, source_target_pairs={{0,2},{1,3},{2,0},{3,1},{4,6},{5,7},{6,4},{7,5},{8,10},{9,11},{10,... | collective-permute-start | bytes 1032200 | tf_op jit(solution)/shard_map/ppermute | solution.py:167
  52.2 16.4 %collective-permute-start.9 = (bf16[48,3584]{1,0:T(8,128)(2,1)S(1)}, bf16[48,3584]{1,0:T(8,128)(2,1)S(1)}, u32[]{:S(2)}, u32[]{:S(2)}) collective-permute-start(bf16[48,3584]{1,0:T(8,128)(2,1)S(1)} %get-tuple-element.50), channel_id=1, source_target_pairs={{0,2},{1,3},{2,0},{3,1},{4,6},{5,7},{6,4},{7,5},{8,10},{9,11},{10,... | collective-permute-start | bytes 1032200 | tf_op jit(solution)/shard_map/ppermute | solution.py:167
  56.8 14.6 %collective-permute-start.14 = (bf16[48,3584]{1,0:T(8,128)(2,1)S(1)}, bf16[48,3584]{1,0:T(8,128)(2,1)S(1)}, u32[]{:S(2)}, u32[]{:S(2)}) collective-permute-start(bf16[48,3584]{1,0:T(8,128)(2,1)S(1)} %add_convert_fusion.2), channel_id=1, source_target_pairs={{0,8},{1,9},{2,10},{3,11},{4,12},{5,13},{6,14},{7,15},{8,0},{9,1},... | collective-permute-start | bytes 1032200 | tf_op jit(solution)/shard_map/ppermute | solution.py:188
  66.0 19.2 %copy-start.6 = (bf16[64,3584]{1,0:T(8,128)(2,1)S(1)}, bf16[64,3584]{1,0:T(8,128)(2,1)}, u32[]{:S(2)}) copy-start(bf16[64,3584]{1,0:T(8,128)(2,1)} %hidden_ref.3) | copy-start | bytes 1376260
  66.0 19.2 %copy-start.8 = (f32[64,8]{1,0:T(8,128)S(1)}, f32[64,8]{1,0:T(8,128)}, u32[]{:S(2)}) copy-start(f32[64,8]{1,0:T(8,128)} %get-tuple-element.34.slot_ref) | copy-start | bytes 6148
  66.0 19.2 %copy-start.9 = (f32[64,8]{1,0:T(8,128)S(1)}, f32[64,8]{1,0:T(8,128)}, u32[]{:S(2)}) copy-start(f32[64,8]{1,0:T(8,128)} %get-tuple-element.35.weight_ref) | copy-start | bytes 6148
  68.6 7.3 %collective-permute-start.15 = (bf16[48,3584]{1,0:T(8,128)(2,1)S(1)}, bf16[48,3584]{1,0:T(8,128)(2,1)S(1)}, u32[]{:S(2)}, u32[]{:S(2)}) collective-permute-start(bf16[48,3584]{1,0:T(8,128)(2,1)S(1)} %get-tuple-element.61), channel_id=1, source_target_pairs={{0,2},{1,3},{2,0},{3,1},{4,6},{5,7},{6,4},{7,5},{8,10},{9,11},{10,... | collective-permute-start | bytes 1032200 | tf_op jit(solution)/shard_map/ppermute | solution.py:167
  69.6 9.9 %collective-permute-start.13 = (bf16[48,3584]{1,0:T(8,128)(2,1)S(1)}, bf16[48,3584]{1,0:T(8,128)(2,1)S(1)}, u32[]{:S(2)}, u32[]{:S(2)}) collective-permute-start(bf16[48,3584]{1,0:T(8,128)(2,1)S(1)} %add_convert_fusion.1), channel_id=1, source_target_pairs={{0,12},{1,13},{2,14},{3,15},{4,0},{5,1},{6,2},{7,3},{8,4},{9,5},{1... | collective-permute-start | bytes 1032200 | tf_op jit(solution)/shard_map/ppermute | solution.py:188
  76.0 9.2 %collective-permute-start.16 = (bf16[48,3584]{1,0:T(8,128)(2,1)S(1)}, bf16[48,3584]{1,0:T(8,128)(2,1)S(1)}, u32[]{:S(2)}, u32[]{:S(2)}) collective-permute-start(bf16[48,3584]{1,0:T(8,128)(2,1)S(1)} %add_convert_fusion), channel_id=1, source_target_pairs={{0,4},{1,5},{2,6},{3,7},{4,8},{5,9},{6,10},{7,11},{8,12},{9,13},{1... | collective-permute-start | bytes 1032200 | tf_op jit(solution)/shard_map/ppermute | solution.py:188
